TPU v7x, 32 devices: a whole 2x2x4 slice. The times are simulated.
32 devices in a mesh: row: 8 (over z, x), grp: 4 (over y, core).
Axes of the slice: x: 2, y: 2, z: 4, core: 2. Of those that a mesh axis runs over, the one named last changes fastest.
Arguments:
- features: bfloat16 [65536, 768], P(('row', 'grp')), may hold values from -6 to 6
- dense_edge_weights: bfloat16 [256, 4, 256, 256], P(('row', 'grp')), may hold values from -0.15625 to 0.15625
- dense_cols: int32 [256, 4], P(('row', 'grp')), may hold values from 0 to 7
- dense_ids: int32 [8], replicated, may hold values from 0 to 255, as said below
- sparse_w: bfloat16 [65536, 256], P(('row', 'grp')), may hold values from -0.15625 to 0.15625
- sparse_rows: int32 [32, 32, 8], P(('row', 'grp')), may hold values from 0 to 2047, as said below
- sparse_counts: int32 [32, 32], P(('row', 'grp')), may hold values from 1 to 8, as said below
- weight: bfloat16 [768, 768], replicated, may hold values from -0.21875 to 0.21875
- bias: float32 [768], replicated, may hold values from -3 to 3
Outputs:
- output: bfloat16 [65536, 768], P(('row', 'grp'))
Inputs may be any that keep to these rules, and one draw needn't show every extreme that they name: `dense_ids`: distinct row block ids; the first and the last row block are both among them. `sparse_rows`: local row indices of the sender. `sparse_counts`: at most 8 rows from one sender to one receiver; one receiver gets 8 rows from every sender.
All inputs are finite; a program needn't handle non-finite values.
Results may differ from a plain program's by a relative error of at most 0.0044.
Values may be sent and summed in bfloat16 or wider, within the bound.
No kernel may reach another device: no remote copies, remote signals or barrier semaphores. Data moves between devices by JAX's collectives and lax.ppermute only.
A program may use at most 128 MiB of HBM per device.

v0:
```python
import jax
import jax.numpy as jnp
from jax import lax
from jax.sharding import PartitionSpec as P


def from_root(x, axis, root):
    mine = lax.axis_index(axis) == root
    return lax.psum(jnp.where(mine, x, jnp.zeros_like(x)), axis)


def on_device(
    features,
    dense_edge_weights,
    dense_cols,
    dense_ids,
    sparse_w,
    sparse_rows,
    sparse_counts,
    weight,
    bias,
):
    block_count = dense_edge_weights.shape[0]
    tiles_per = dense_edge_weights.shape[1]
    tile_size = dense_edge_weights.shape[2]
    feature_width = features.shape[1]
    stripe_count = dense_ids.shape[0]
    local_blocks = features.reshape(block_count, tile_size, feature_width)

    def fetch_stripe(index, dense_bands):
        global_id = dense_ids[index]
        owner = global_id // block_count
        candidate = lax.dynamic_index_in_dim(
            local_blocks, global_id % block_count, 0, keepdims=False
        )
        arrived = from_root(candidate, ("row", "grp"), owner)
        return lax.dynamic_update_index_in_dim(dense_bands, arrived, index, 0)

    empty_stripes = jnp.zeros((stripe_count, tile_size, feature_width), jnp.bfloat16)
    dense_bands = lax.fori_loop(0, stripe_count, fetch_stripe, empty_stripes)
    dense_sum = jnp.zeros((block_count, tile_size, feature_width), jnp.float32)
    for tile_index in range(tiles_per):
        picked_tiles = dense_bands[dense_cols[:, tile_index]]
        dense_sum = dense_sum + jnp.einsum(
            "eim,emh->eih",
            dense_edge_weights[:, tile_index],
            picked_tiles,
            preferred_element_type=jnp.float32,
        )
    rows_out = sparse_rows[0]
    counts_out = sparse_counts[0]
    peer_count = rows_out.shape[0]
    slot_count = rows_out.shape[1]
    outgoing = features[rows_out]
    slot_ids = jnp.arange(slot_count, dtype=jnp.int32)
    live_slots = slot_ids[None, :] < counts_out[:, None]
    outgoing = jnp.where(live_slots[:, :, None], outgoing, jnp.zeros((), outgoing.dtype))
    arrived_rows = lax.all_to_all(outgoing, ("row", "grp"), split_axis=0, concat_axis=0, tiled=True)
    incoming_rows = arrived_rows.reshape(peer_count * slot_count, feature_width)
    sparse_sum = jnp.dot(sparse_w, incoming_rows, preferred_element_type=jnp.float32)
    aggregate = (dense_sum.reshape(block_count * tile_size, feature_width) + sparse_sum).astype(
        jnp.bfloat16
    )
    result = jnp.dot(aggregate, weight, preferred_element_type=jnp.float32) + bias
    return jnp.maximum(result, 0.0).astype(jnp.bfloat16)


def solution(mesh):
    placed = (
        P(("row", "grp"), None),
        P(("row", "grp"), None, None, None),
        P(("row", "grp"), None),
        P(),
        P(("row", "grp"), None),
        P(("row", "grp"), None, None),
        P(("row", "grp"), None),
        P(),
        P(),
    )
    return jax.shard_map(
        on_device, mesh=mesh, in_specs=placed, out_specs=P(("row", "grp"), None), check_vma=False
    )
```

profile of v0, /device:TPU:0, one launch (start us, length us, event | category | flops | bytes accessed | tf_op | source)
XLA Modules:
  0.0 1156.7 jit_solution(15612302753313953998)
XLA Ops:
  6.5 0.0 copy-start
  6.5 0.8 compare_select_fusion
  7.3 0.1 copy.18
  7.4 0.1 reshape.103
  7.5 0.7 iota_compare_fusion
  8.2 3.7 gather_fusion.4
  11.9 0.9 bitcast_select_fusion
  12.8 7.3 all-to-all-start
  20.2 0.0 copy-done.5
  20.2 1076.3 %while.15 = (s32[]{:T(128)}, bf16[8,256,768]{2,1,0:T(8,128)(2,1)}, s32[8]{0:T(128)S(1)}, bf16[8,256,768]{2,1,0:T(8,128)(2,1)}, s32[]{:T(128)}, /*index=5*/s32[]{...) while((s32[]{:T(128)}, bf16[8,256,768]{2,1,0:T(8,128)(2,1)}, ...), condition=%wide.region_2.3_spmd, body=%wide.region_0.2_spmd.sunk | while | flops 393248 | bytes 3932668 | solution.py:40
  20.2 0.0 all-reduce.2.cloned.1.call-start
  20.2 0.6 dynamic_slice.25
  23.4 1.8 dynamic-slice_select_fusion.2
  25.2 0.0 all-reduce.2.cloned.1.call-update
  25.2 129.9 %all-reduce.2.cloned.1.call-done = bf16[1,256,768]{2,1,0:T(8,128)(2,1)} async-done(((bf16[1,256,768]{2,1,0:T(8,128)(2,1)}), bf16[1,256,768]{2,1,0:T(8,128)(2,1)}) %all-reduce.2.cloned.1.call-update) | async-done | bytes 393232 | tf_op jit(solution)/shard_map/while/body/eval_jaxpr/psum | solution.py:9
  155.1 1.8 constant_dynamic-update-slice_fusion.2
  156.9 0.0 all-reduce.2.cloned.1.call-start
  156.9 0.6 dynamic_slice.25
  160.0 1.8 dynamic-slice_select_fusion.2
  161.8 0.0 all-reduce.2.cloned.1.call-update
  161.8 127.6 %all-reduce.2.cloned.1.call-done = bf16[1,256,768]{2,1,0:T(8,128)(2,1)} async-done(((bf16[1,256,768]{2,1,0:T(8,128)(2,1)}), bf16[1,256,768]{2,1,0:T(8,128)(2,1)}) %all-reduce.2.cloned.1.call-update) | async-done | bytes 393232 | tf_op jit(solution)/shard_map/while/body/eval_jaxpr/psum | solution.py:9
  289.5 1.8 constant_dynamic-update-slice_fusion.2
  291.2 0.6 dynamic_slice.25
  294.4 1.8 dynamic-slice_select_fusion.2
  296.2 0.0 all-reduce.2.cloned.1.call-update
  296.2 127.6 %all-reduce.2.cloned.1.call-done = bf16[1,256,768]{2,1,0:T(8,128)(2,1)} async-done(((bf16[1,256,768]{2,1,0:T(8,128)(2,1)}), bf16[1,256,768]{2,1,0:T(8,128)(2,1)}) %all-reduce.2.cloned.1.call-update) | async-done | bytes 393232 | tf_op jit(solution)/shard_map/while/body/eval_jaxpr/psum | solution.py:9
  423.8 1.8 constant_dynamic-update-slice_fusion.2
  425.6 0.6 dynamic_slice.25
  428.8 1.8 dynamic-slice_select_fusion.2
  430.5 0.0 all-reduce.2.cloned.1.call-update
  430.6 127.3 %all-reduce.2.cloned.1.call-done = bf16[1,256,768]{2,1,0:T(8,128)(2,1)} async-done(((bf16[1,256,768]{2,1,0:T(8,128)(2,1)}), bf16[1,256,768]{2,1,0:T(8,128)(2,1)}) %all-reduce.2.cloned.1.call-update) | async-done | bytes 393232 | tf_op jit(solution)/shard_map/while/body/eval_jaxpr/psum | solution.py:9
  557.9 1.8 constant_dynamic-update-slice_fusion.2
  559.6 0.0 all-reduce.2.cloned.1.call-start
  559.6 0.6 dynamic_slice.25
  562.8 1.8 dynamic-slice_select_fusion.2
  564.6 0.0 all-reduce.2.cloned.1.call-update
  564.6 127.3 %all-reduce.2.cloned.1.call-done = bf16[1,256,768]{2,1,0:T(8,128)(2,1)} async-done(((bf16[1,256,768]{2,1,0:T(8,128)(2,1)}), bf16[1,256,768]{2,1,0:T(8,128)(2,1)}) %all-reduce.2.cloned.1.call-update) | async-done | bytes 393232 | tf_op jit(solution)/shard_map/while/body/eval_jaxpr/psum | solution.py:9
  691.9 1.8 constant_dynamic-update-slice_fusion.2
  693.7 0.6 dynamic_slice.25
  696.9 1.8 dynamic-slice_select_fusion.2
  698.6 0.0 all-reduce.2.cloned.1.call-update
  698.7 127.3 %all-reduce.2.cloned.1.call-done = bf16[1,256,768]{2,1,0:T(8,128)(2,1)} async-done(((bf16[1,256,768]{2,1,0:T(8,128)(2,1)}), bf16[1,256,768]{2,1,0:T(8,128)(2,1)}) %all-reduce.2.cloned.1.call-update) | async-done | bytes 393232 | tf_op jit(solution)/shard_map/while/body/eval_jaxpr/psum | solution.py:9
  826.0 1.8 constant_dynamic-update-slice_fusion.2
  827.7 0.6 dynamic_slice.25
  830.9 1.8 dynamic-slice_select_fusion.2
  832.7 0.0 all-reduce.2.cloned.1.call-update
  832.7 127.6 %all-reduce.2.cloned.1.call-done = bf16[1,256,768]{2,1,0:T(8,128)(2,1)} async-done(((bf16[1,256,768]{2,1,0:T(8,128)(2,1)}), bf16[1,256,768]{2,1,0:T(8,128)(2,1)}) %all-reduce.2.cloned.1.call-update) | async-done | bytes 393232 | tf_op jit(solution)/shard_map/while/body/eval_jaxpr/psum | solution.py:9
  960.3 1.8 constant_dynamic-update-slice_fusion.2
  962.1 0.6 dynamic_slice.25
  965.3 1.8 dynamic-slice_select_fusion.2
  967.1 0.0 all-reduce.2.cloned.1.call-update
  967.1 127.6 %all-reduce.2.cloned.1.call-done = bf16[1,256,768]{2,1,0:T(8,128)(2,1)} async-done(((bf16[1,256,768]{2,1,0:T(8,128)(2,1)}), bf16[1,256,768]{2,1,0:T(8,128)(2,1)}) %all-reduce.2.cloned.1.call-update) | async-done | bytes 393232 | tf_op jit(solution)/shard_map/while/body/eval_jaxpr/psum | solution.py:9
  1094.7 1.8 constant_dynamic-update-slice_fusion.2
  1096.5 4.3 gather_fusion.1
  1100.7 4.3 gather_fusion
  1105.1 6.0 fusion.4
  1111.1 4.9 fusion.6
  1115.9 4.3 gather_fusion.2
  1120.3 5.8 fusion.2
  1126.0 4.3 gather_fusion.3
  1130.4 11.8 %add_add_fusion = f32[8,768,256]{1,2,0:T(8,128)} fusion(f32[8,768,256]{1,2,0:T(8,128)} %fusion.2, f32[8,768,256]{1,2,0:T(8,128)} %fusion.6, f32[8,768,256]{1,2,0:T(8,128)} %fusion.4, bf16[8,256,768]{2,1,0:T(8,128)(2,1)} %gather_fusion.3, bf16[8,4,256,256]{3,2,1,0:T(8,128)(2,1)} %param.12), kind=kOutput, calls=%fused_computation.10 | convolution fusion | flops 810024960 | bytes 29360128 | tf_op jit(solution)/shard_map/eim,emh->eih/dot_general | solution.py:44
  1142.1 0.0 all-to-all-done
  1142.2 3.8 fusion
  1145.9 4.0 maximum_convert_fusion
  (20 shorter events, 0.1 us)
Async XLA Ops:
  6.5 1139.4 %copy-start = (bf16[768,768]{1,0:T(8,128)(2,1)S(1)}, bf16[768,768]{1,0:T(8,128)(2,1)}, u32[]{:S(2)}) copy-start(bf16[768,768]{1,0:T(8,128)(2,1)} %param.18) | copy-start | bytes 3538948
  6.5 13.6 %copy-start.3 = (s32[8,4]{0,1:T(4,128)S(1)}, s32[8,4]{0,1:T(4,128)}, u32[]{:S(2)}) copy-start(s32[8,4]{0,1:T(4,128)} %param.13) | copy-start | bytes 388
  6.5 13.6 %copy-start.5 = (s32[8]{0:T(128)S(1)}, s32[8]{0:T(128)}, u32[]{:S(2)}) copy-start(s32[8]{0:T(128)} %param.14) | copy-start | bytes 100
  12.8 1129.3 %all-to-all-start = ((bf16[32,8,768]{2,1,0:T(8,128)(2,1)}), bf16[32,8,768]{2,1,0:T(8,128)(2,1)S(1)}, u32[]{:S(2)}, u32[]{:S(2)}) async-start(bf16[32,8,768]{2,1,0:T(8,128)(2,1)} %bitcast_select_fusion), calls=%async_computation | async-start | bytes 786432 | tf_op jit(solution)/shard_map/all_to_all | solution.py:58
  20.2 134.9 %all-reduce.2.cloned.1.call-start = ((), (), s32[]{:S(2)}) async-start(), calls=%async_computation.1 | async-start | bytes 786432 | tf_op jit(solution)/shard_map/while/body/eval_jaxpr/psum | solution.py:9
  156.9 132.6 %all-reduce.2.cloned.1.call-start = ((), (), s32[]{:S(2)}) async-start(), calls=%async_computation.1 | async-start | bytes 786432 | tf_op jit(solution)/shard_map/while/body/eval_jaxpr/psum | solution.py:9
  291.2 132.6 %all-reduce.2.cloned.1.call-start = ((), (), s32[]{:S(2)}) async-start(), calls=%async_computation.1 | async-start | bytes 786432 | tf_op jit(solution)/shard_map/while/body/eval_jaxpr/psum | solution.py:9
  425.6 132.3 %all-reduce.2.cloned.1.call-start = ((), (), s32[]{:S(2)}) async-start(), calls=%async_computation.1 | async-start | bytes 786432 | tf_op jit(solution)/shard_map/while/body/eval_jaxpr/psum | solution.py:9
  559.6 132.3 %all-reduce.2.cloned.1.call-start = ((), (), s32[]{:S(2)}) async-start(), calls=%async_computation.1 | async-start | bytes 786432 | tf_op jit(solution)/shard_map/while/body/eval_jaxpr/psum | solution.py:9
  693.7 132.3 %all-reduce.2.cloned.1.call-start = ((), (), s32[]{:S(2)}) async-start(), calls=%async_computation.1 | async-start | bytes 786432 | tf_op jit(solution)/shard_map/while/body/eval_jaxpr/psum | solution.py:9
  827.7 132.6 %all-reduce.2.cloned.1.call-start = ((), (), s32[]{:S(2)}) async-start(), calls=%async_computation.1 | async-start | bytes 786432 | tf_op jit(solution)/shard_map/while/body/eval_jaxpr/psum | solution.py:9
  962.1 132.6 %all-reduce.2.cloned.1.call-start = ((), (), s32[]{:S(2)}) async-start(), calls=%async_computation.1 | async-start | bytes 786432 | tf_op jit(solution)/shard_map/while/body/eval_jaxpr/psum | solution.py:9
  1105.1 6.0 copy-start.1
  1130.4 11.8 %copy-start.2 = (bf16[2048,256]{1,0:T(8,128)(2,1)S(1)}, bf16[2048,256]{1,0:T(8,128)(2,1)}, u32[]{:S(2)}) copy-start(bf16[2048,256]{1,0:T(8,128)(2,1)} %param.15) | copy-start | bytes 3145732
  1142.1 3.8 copy-start.4
Sparse Core Ops, SparseCore 0:
  26.3 128.7 all-reduce.1
  163.0 126.4 all-reduce.1
  297.3 126.4 all-reduce.1
  431.4 126.4 all-reduce.1
  565.5 126.4 all-reduce.1
  699.5 126.4 all-reduce.1
  833.9 126.4 all-reduce.1
  968.2 126.4 all-reduce.1
where the time goes:
time: 1160 us
  waiting for transfers between devices  1020 us (88%)
  local copies, waits for them, and re-layouts  40.1 us (3%)
  matrix products  36.1 us (3%)
  loops' own time  20.7 us (2%)
  other arithmetic  16.6 us (1%)
  between operations  13.5 us (1%)
    psum x8, waiting for transfers between devices, from_root(): return lax.psum(jnp.where(mine, x, jnp.zeros_like(x)), axis)  1020 us
    dot_general x4, matrix products, on_device(): jnp.einsum('eim,emh->eih', dense_edge_weights[:, tile_index], picked_tile...  28.4 us
  transfers between devices with their start and end apart: 9, of which 8 were waited for; matrix products, arithmetic and copies ran while one was open for 7% of the time, Pallas kernels for 0%

commit v1 on v0

v1 whole, which is shorter than its diff:
```python
import functools

import jax
import jax.numpy as jnp
from jax import lax
from jax.experimental import pallas as pl
from jax.experimental.pallas import tpu as pltpu
from jax.sharding import PartitionSpec as P

AXES = ("row", "grp")
PLANE = 8


def layer_kernel(meta, *refs):
    pieces = refs[:PLANE]
    rows_in, edge, sparse, weight, bias, out, bands = refs[PLANE:]
    block = pl.program_id(0)
    tiles_per = edge.shape[1]
    stripes, piece_rows, _ = pieces[0].shape
    cols_at = pl.num_programs(0) * tiles_per

    @pl.when(block == 0)
    def _():
        for i in range(PLANE):
            at = pl.multiple_of(meta[cols_at + i] * piece_rows, piece_rows)
            for j in range(stripes):
                bands[j, pl.ds(at, piece_rows), :] = pieces[i][j]

    total = jnp.dot(sparse[...], rows_in[...], preferred_element_type=jnp.float32)
    for t in range(tiles_per):
        band = bands[meta[block * tiles_per + t]]
        total += jnp.dot(edge[0, t], band, preferred_element_type=jnp.float32)
    result = jnp.dot(total.astype(jnp.bfloat16), weight[...], preferred_element_type=jnp.float32)
    out[...] = jnp.maximum(result + bias[...], 0.0).astype(out.dtype)


def layer(meta, pieces, rows_in, edge, sparse, weight, bias):
    blocks, tiles_per, tile, _ = edge.shape
    width = weight.shape[0]
    stripes = pieces[0].shape[0]
    whole = pl.BlockSpec(memory_space=pltpu.VMEM)
    return pl.pallas_call(
        layer_kernel,
        out_shape=jax.ShapeDtypeStruct((blocks * tile, width), jnp.bfloat16),
        grid_spec=pltpu.PrefetchScalarGridSpec(
            num_scalar_prefetch=1,
            grid=(blocks,),
            in_specs=[whole] * (PLANE + 1)
            + [
                pl.BlockSpec((1, tiles_per, tile, tile), lambda b, m: (b, 0, 0, 0)),
                pl.BlockSpec((tile, sparse.shape[1]), lambda b, m: (b, 0)),
                whole,
                whole,
            ],
            out_specs=pl.BlockSpec((tile, width), lambda b, m: (b, 0)),
            scratch_shapes=[pltpu.VMEM((stripes, tile, width), jnp.bfloat16)],
        ),
        compiler_params=pltpu.CompilerParams(vmem_limit_bytes=40 * 2**20),
        cost_estimate=pl.CostEstimate(
            flops=2 * blocks * tile * width * (tiles_per * tile + sparse.shape[1] + width),
            bytes_accessed=2 * (edge.size + sparse.size + 2 * blocks * tile * width),
            transcendentals=0,
        ),
    )(meta, *pieces, rows_in, edge, sparse, weight, bias)


def spread(slots, blocks, mine, at, outgoing, flat_slot, devices):
    _, tile, width = blocks.shape
    part = tile // devices
    sends = []
    for s in range(slots):
        block = lax.dynamic_index_in_dim(blocks, at[s], 0, keepdims=False)
        block = block.reshape(PLANE, devices // PLANE, part, width)
        sends.append(block.transpose(1, 0, 2, 3).reshape(devices, part, width))
    sends.append(outgoing)
    got = lax.all_to_all(jnp.concatenate(sends, axis=1), AXES, 0, 0, tiled=True)
    held = got[:, : slots * part].reshape(devices * slots, part, width)
    stripes = jnp.take(held, flat_slot(slots), axis=0, mode="clip")
    return stripes, got[:, slots * part :].reshape(-1, width)


def on_device(features, edge, cols, ids, sparse_w, sparse_rows, sparse_counts, weight, bias):
    block_count, tiles_per, tile, _ = edge.shape
    width = features.shape[1]
    stripe_count = ids.shape[0]
    devices = sparse_rows.shape[1]
    groups = devices // PLANE
    me = lax.axis_index(AXES)
    group, place = me // PLANE, me % PLANE
    blocks = features.reshape(block_count, tile, width)

    owner = ids // block_count
    earlier = jnp.arange(stripe_count)[:, None] > jnp.arange(stripe_count)[None, :]
    slot = jnp.sum(jnp.where(earlier & (owner[:, None] == owner[None, :]), 1, 0), axis=1)
    mine = owner == me
    slot_ids = jnp.arange(stripe_count)
    at = jnp.sum(
        jnp.where(mine[None, :] & (slot[None, :] == slot_ids[:, None]), ids % block_count, 0), axis=1
    )

    outgoing = features[sparse_rows[0]]
    live = jnp.arange(sparse_rows.shape[2], dtype=jnp.int32)[None, :] < sparse_counts[0][:, None]
    outgoing = jnp.where(live[:, :, None], outgoing, jnp.zeros((), outgoing.dtype))

    def scattered(slots):
        return lambda: spread(
            slots, blocks, mine, at, outgoing, lambda s: owner * s + slot, devices
        )

    held, rows_in = lax.cond(
        jnp.max(slot) < 2, scattered(2), scattered(min(stripe_count, block_count))
    )

    def swap(x, mask):
        return lax.ppermute(x, AXES, [(d, d ^ mask) for d in range(devices)])

    parts = [held] + [swap(held, PLANE * g) for g in range(1, groups)]
    ordered = [lax.select_n(group, *[parts[q ^ g] for g in range(groups)]) for q in range(groups)]
    piece = jnp.concatenate(ordered, axis=1)
    pieces = []
    for xy in range(0, PLANE, 2):
        got = swap(piece, xy) if xy else piece
        pieces += [got, swap(got, 1)]
    meta = jnp.concatenate(
        [cols.reshape(-1), place ^ jnp.arange(PLANE, dtype=jnp.int32)]
    ).astype(jnp.int32)
    return layer(meta, pieces, rows_in, edge, sparse_w, weight, bias.reshape(1, -1))


def solution(mesh):
    placed = (
        P(AXES, None),
        P(AXES, None, None, None),
        P(AXES, None),
        P(),
        P(AXES, None),
        P(AXES, None, None),
        P(AXES, None),
        P(),
        P(),
    )
    return jax.shard_map(
        on_device, mesh=mesh, in_specs=placed, out_specs=P(AXES, None), check_vma=False
    )
```

time: 1160 us -> 104 us (0.09)
  waiting for transfers between devices: 1020 us -> 53.7 us
  matrix products: 36.1 us -> 0 us
  local copies, waits for them, and re-layouts: 40.1 us -> 11.5 us
  loops' own time: 20.7 us -> 4.09 us
  Pallas kernels: 0 us -> 12.8 us
  between operations: 13.5 us -> 0.76 us
    psum x8 -> x0, waiting for transfers between devices: 1020 us -> none  [from_root(): return lax.psum(jnp.where(mine, x, jnp.zeros_like(x)), axis)]
    dot_general x6 -> x0, matrix products: 36.1 us -> none  [the longest x4 28.4 us: on_device(): jnp.einsum('eim,emh->eih', dense_edge_weights[:, tile_index], picked_tile...]
    all_to_all x1, waiting for transfers between devices: 0.01 us -> 29.1 us  [spread(): got = lax.all_to_all(jnp.concatenate(sends, axis=1), AXES, 0, 0, tiled=True)]
    ppermute x0 -> x10, waiting for transfers between devices: none -> 24.6 us  [swap(): return lax.ppermute(x, AXES, [(d, d ^ mask) for d in range(devices)])]
    another operation x1, loops' own time: 20.7 us -> 4.09 us  [on_device(): lax.cond(jnp.max(slot) < 2, scattered(2), scattered(min(stripe_count, blo...]
    gather x5 -> x2, local copies, waits for them, and re-layouts: 20.9 us -> 5.38 us  [the longest x1 3.69 us: on_device(): outgoing = features[sparse_rows[0]]]
    select_n x11 -> x4, other arithmetic: 15.8 us -> 1.51 us  [the longest x1 0.69 us: on_device(): outgoing = features[sparse_rows[0]]]
    dynamic_update_slice x8 -> x0, local copies, waits for them, and re-layouts: 14.1 us -> none  [fetch_stripe(): return lax.dynamic_update_index_in_dim(dense_bands, arrived, index, 0)]
  transfers between devices with their start and end apart: 9 -> 11, of which waited for: 8 -> 7; matrix products, arithmetic and copies ran while one was open for 7% -> 0% of each run, Pallas kernels for 0% -> 0%
where the time goes in v1:
time: 104 us; the launch traced here: 103 us
  waiting for transfers between devices  53.7 us (52%)
  starting transfers between devices  15.2 us (15%)
  Pallas kernels  12.8 us (12%)
  local copies, waits for them, and re-layouts  11.5 us (11%)
  other arithmetic  5.05 us (5%)
  loops' own time  4.09 us (4%)
    all_to_all x1, waiting for transfers between devices, spread(): got = lax.all_to_all(jnp.concatenate(sends, axis=1), AXES, 0, 0, tiled=True)  29.1 us
    ppermute x10, waiting for transfers between devices, swap(): return lax.ppermute(x, AXES, [(d, d ^ mask) for d in range(devices)])  24.6 us
    pallas_call x1, Pallas kernels, layer(): pl.pallas_call(layer_kernel, out_shape=jax.ShapeDtypeStruct((blocks * til...  12.8 us
    ppermute x10, starting transfers between devices, swap(): return lax.ppermute(x, AXES, [(d, d ^ mask) for d in range(devices)])  7.95 us
    all_to_all x1, starting transfers between devices, spread(): got = lax.all_to_all(jnp.concatenate(sends, axis=1), AXES, 0, 0, tiled=True)  7.3 us
    another operation x1, loops' own time, on_device(): lax.cond(jnp.max(slot) < 2, scattered(2), scattered(min(stripe_count, blo...  4.09 us
    gather x1, local copies, waits for them, and re-layouts, on_device(): outgoing = features[sparse_rows[0]]  3.69 us
    unnamed x11, local copies, waits for them, and re-layouts  2.29 us
  transfers between devices with their start and end apart: 11, of which 7 were waited for; matrix products, arithmetic and copies ran while one was open for 0% of the time, Pallas kernels for 0%

profile of v1, /device:TPU:0, one launch (start us, length us, event | category | flops | bytes accessed | tf_op | source)
XLA Modules:
  0.0 103.1 jit_solution(7444057049958983898)
XLA Ops:
  0.0 0.7 and_select_fusion
  0.7 0.7 broadcast_compare_fusion
  1.3 0.2 select_reduce_fusion.1
  1.5 0.7 compare_select_fusion
  2.2 0.1 copy.36
  2.3 0.1 reshape.168
  2.4 0.7 iota_compare_fusion
  3.1 0.6 reduce_max.9
  4.4 0.1 select_reduce_fusion
  4.5 3.7 %gather_fusion.2 = bf16[256,768]{1,0:T(8,128)(2,1)S(1)} fusion(bf16[2048,768]{1,0:T(8,128)(2,1)} %param.11, s32[1024]{0:T(1024)S(1)} %pad_clamp_fusion.2), kind=kCustom, calls=%fused_computation.2 | custom fusion | bytes 787456 | tf_op jit(solution)/shard_map/gather | solution.py:101
  8.2 0.1 bitcast_select_fusion
  8.3 0.0 copy-start.4
  8.3 0.0 copy-start.3
  8.4 0.0 copy-start.1
  8.4 0.0 copy-start.2
  8.4 46.8 %conditional.1 = (bf16[8,8,768]{2,1,0:T(8,128)(2,1)S(1)}, bf16[256,768]{1,0:T(8,128)(2,1)}) conditional(s32[]{:T(128)} %convert_element_type.3, (s32[8]{0:T(128)S(1)}, bf16[8,256,768]{2,1,0:T(8,128)(2,1)}, bf16[32,8,768]{2,1,0:T(8,128)(2,1)S(1)}, s32[8]{0:T(128)S(1)}, s32[8]{0:T(128)S(1)}) %tuple.36, (s32[8]{0:T(128)S(1)}, ...), branch_computations={%region_3.4_spmd, %region_4.5_spmd} | conditional | flops 3539990 | bytes 37556800 | solution.py:110
  8.4 0.7 fusion.3
  13.1 1.2 %constant_dynamic-slice_fusion.9 = (bf16[1,256,768]{2,1,0:T(8,128)(2,1)S(1)}, bf16[1,256,768]{2,1,0:T(8,128)(2,1)S(1)}) fusion(bf16[8,256,768]{2,1,0:T(8,128)(2,1)} %get-tuple-element.30, s32[]{:T(128)S(6)} %select_n.119, s32[]{:T(128)S(6)} %select_n.120), kind=kLoop, calls=%fused_computation.28 | loop fusion | bytes 1572872 | tf_op jit(solution)/shard_map/cond/branch_1_fun/jit(dynamic_index_in_dim)/dynamic_slice | solution.py:72
  14.3 1.1 %pad_maximum_fusion = bf16[32,24,768]{2,1,0:T(8,128)(2,1)} fusion(bf16[32,8,768]{2,1,0:T(8,128)(2,1)S(1)} %get-tuple-element.32, bf16[32,8,768]{2,1,0:T(8,128)(2,1)S(1)} %bitcast.75, bf16[32,8,768]{2,1,0:T(8,128)(2,1)S(1)} %bitcast.74), kind=kLoop, calls=%fused_computation.23 | loop fusion | flops 3538944 | bytes 2359296 | tf_op jit(solution)/shard_map/cond/branch_1_fun/concatenate | solution.py:76
  15.4 7.3 %all-to-all-start.1 = ((bf16[32,24,768]{2,1,0:T(8,128)(2,1)}), bf16[32,24,768]{2,1,0:T(8,128)(2,1)S(1)}, u32[]{:S(2)}, u32[]{:S(2)}) async-start(bf16[32,24,768]{2,1,0:T(8,128)(2,1)} %pad_maximum_fusion), calls=%async_computation.1 | async-start | bytes 2359296 | tf_op jit(solution)/shard_map/cond/branch_1_fun/all_to_all | solution.py:76
  22.7 29.1 %all-to-all-done.1 = bf16[32,24,768]{2,1,0:T(8,128)(2,1)S(1)} async-done(((bf16[32,24,768]{2,1,0:T(8,128)(2,1)}), bf16[32,24,768]{2,1,0:T(8,128)(2,1)S(1)}, u32[]{:S(2)}, u32[]{:S(2)}) %all-to-all-start.1) | async-done | bytes 1179680 | tf_op jit(solution)/shard_map/cond/branch_1_fun/all_to_all | solution.py:76
  51.8 0.9 slice.50
  52.7 1.7 %gather_fusion.1 = bf16[8,8,768]{2,1,0:T(8,128)(2,1)S(1)} fusion(bf16[64,8,768]{2,1,0:T(8,128)(2,1)} %bitcast.87, s32[1024]{0:T(1024)S(1)} %pad_clamp_fusion.1), kind=kCustom, calls=%fused_computation.1 | custom fusion | bytes 196640 | tf_op jit(solution)/shard_map/cond/branch_1_fun/jit(_take)/gather | solution.py:78
  54.4 0.8 slice_bitcast_fusion.1
  55.2 0.5 collective-permute-start
  55.7 1.4 %collective-permute-start.1 = (bf16[8,8,768]{2,1,0:T(8,128)(2,1)S(1)}, bf16[8,8,768]{2,1,0:T(8,128)(2,1)S(1)}, u32[]{:S(2)}, u32[]{:S(2)}) collective-permute-start(bf16[8,8,768]{2,1,0:T(8,128)(2,1)S(1)} %get-tuple-element.37), channel_id=1, source_target_pairs={{0,16},{1,17},{2,18},{3,19},{4,20},{5,21},{6,22},{7,23},{8,24},{9,... | collective-permute-start | bytes 294920 | tf_op jit(solution)/shard_map/ppermute | solution.py:115
  57.0 2.6 %collective-permute-start.2 = (bf16[8,8,768]{2,1,0:T(8,128)(2,1)S(1)}, bf16[8,8,768]{2,1,0:T(8,128)(2,1)S(1)}, u32[]{:S(2)}, u32[]{:S(2)}) collective-permute-start(bf16[8,8,768]{2,1,0:T(8,128)(2,1)S(1)} %get-tuple-element.37), channel_id=1, source_target_pairs={{0,24},{1,25},{2,26},{3,27},{4,28},{5,29},{6,30},{7,31},{8,16},{9,... | collective-permute-start | bytes 294920 | tf_op jit(solution)/shard_map/ppermute | solution.py:115
  59.6 1.6 %collective-permute-done = bf16[8,8,768]{2,1,0:T(8,128)(2,1)S(1)} collective-permute-done((bf16[8,8,768]{2,1,0:T(8,128)(2,1)S(1)}, bf16[8,8,768]{2,1,0:T(8,128)(2,1)S(1)}, u32[]{:S(2)}, u32[]{:S(2)}) %collective-permute-start) | collective-permute-done | bytes 98336 | tf_op jit(solution)/shard_map/ppermute | solution.py:115
  61.2 5.2 %collective-permute-done.1 = bf16[8,8,768]{2,1,0:T(8,128)(2,1)S(1)} collective-permute-done((bf16[8,8,768]{2,1,0:T(8,128)(2,1)S(1)}, bf16[8,8,768]{2,1,0:T(8,128)(2,1)S(1)}, u32[]{:S(2)}, u32[]{:S(2)}) %collective-permute-start.1) | collective-permute-done | bytes 98336 | tf_op jit(solution)/shard_map/ppermute | solution.py:115
  66.5 0.0 collective-permute-done.2
  66.6 1.0 collective-permute-start.4
  67.6 1.0 collective-permute-start.6
  68.6 1.5 %collective-permute-start.8 = (bf16[8,32,768]{2,1,0:T(8,128)(2,1)S(1)}, bf16[8,32,768]{2,1,0:T(8,128)(2,1)}, u32[]{:S(2)}, u32[]{:S(2)}) collective-permute-start(bf16[8,32,768]{2,1,0:T(8,128)(2,1)S(1)} %pad_maximum_fusion.1.refs_0_), channel_id=1, source_target_pairs={{0,6},{1,7},{2,4},{3,5},{4,2},{5,3},{6,0},{7,1},{8,14},{9,15},{10,... | collective-permute-start | bytes 1179656 | tf_op jit(solution)/shard_map/ppermute | solution.py:115
  70.1 0.0 collective-permute-start.3
  70.1 7.5 %collective-permute-done.4.refs_2_ = bf16[8,32,768]{2,1,0:T(8,128)(2,1)S(1)} collective-permute-done((bf16[8,32,768]{2,1,0:T(8,128)(2,1)S(1)}, bf16[8,32,768]{2,1,0:T(8,128)(2,1)S(1)}, u32[]{:S(2)}, u32[]{:S(2)}) %collective-permute-start.4) | collective-permute-done | bytes 393248 | tf_op jit(solution)/shard_map/ppermute | solution.py:115
  77.6 0.0 collective-permute-start.5
  77.6 2.0 %collective-permute-done.6.refs_4_ = bf16[8,32,768]{2,1,0:T(8,128)(2,1)S(1)} collective-permute-done((bf16[8,32,768]{2,1,0:T(8,128)(2,1)S(1)}, bf16[8,32,768]{2,1,0:T(8,128)(2,1)S(1)}, u32[]{:S(2)}, u32[]{:S(2)}) %collective-permute-start.6) | collective-permute-done | bytes 393248 | tf_op jit(solution)/shard_map/ppermute | solution.py:115
  79.6 0.0 collective-permute-start.7
  79.6 6.5 %collective-permute-done.8.refs_6_ = bf16[8,32,768]{2,1,0:T(8,128)(2,1)} collective-permute-done((bf16[8,32,768]{2,1,0:T(8,128)(2,1)S(1)}, bf16[8,32,768]{2,1,0:T(8,128)(2,1)}, u32[]{:S(2)}, u32[]{:S(2)}) %collective-permute-start.8) | collective-permute-done | bytes 393248 | tf_op jit(solution)/shard_map/ppermute | solution.py:115
  86.1 0.0 collective-permute-start.9
  86.1 0.0 copy-done.4
  86.1 0.1 copy.35
  86.2 0.1 reshape.147
  86.2 0.0 copy-done.3
  86.3 0.1 pad_add_fusion.meta
  86.4 0.0 collective-permute-done.3.refs_1_
  86.4 0.0 collective-permute-done.5.refs_3_
  86.4 0.0 collective-permute-done.7.refs_5_
  86.4 1.8 %collective-permute-done.9.refs_7_ = bf16[8,32,768]{2,1,0:T(8,128)(2,1)} collective-permute-done((bf16[8,32,768]{2,1,0:T(8,128)(2,1)}, bf16[8,32,768]{2,1,0:T(8,128)(2,1)}, u32[]{:S(2)}, u32[]{:S(2)}) %collective-permute-start.9) | collective-permute-done | bytes 393248 | tf_op jit(solution)/shard_map/ppermute | solution.py:115
  88.1 0.0 copy-done.1
  88.1 0.0 copy-done.2
  88.2 0.0 copy-start
  88.2 2.2 %copy-done = bf16[8,4,256,256]{3,2,1,0:T(8,128)(2,1)S(1)} copy-done((bf16[8,4,256,256]{3,2,1,0:T(8,128)(2,1)S(1)}, bf16[8,4,256,256]{3,2,1,0:T(8,128)(2,1)}, u32[]{:S(2)}) %copy-start) | copy-done | bytes 4194328
  90.3 12.8 %shard_map.91 = bf16[2048,768]{1,0:T(8,128)(2,1)} custom-call(s32[40]{0:T(128)S(1)} %pad_add_fusion.meta, bf16[8,32,768]{2,1,0:T(8,128)(2,1)S(1)} %pad_maximum_fusion.1.refs_0_, bf16[8,32,768]{2,1,0:T(8,128)(2,1)} %collective-permute-done.3.refs_1_, bf16[8,32,768]{2,1,0:T(8,128)(2,1)S(1)} %collective-permute-done.4.refs_2_, ...), custom_call_target="tpu_custom_call" | custom-call | flops 6442450944 | bytes 11534336 | tf_op jit(solution)/shard_map/pallas_call | solution.py:42
  (9 shorter events, 0.2 us)
Async XLA Ops:
  8.3 77.8 %copy-start.4 = (s32[8,4]{0,1:T(4,128)S(1)}, s32[8,4]{0,1:T(4,128)}, u32[]{:S(2)}) copy-start(s32[8,4]{0,1:T(4,128)} %param.13) | copy-start | bytes 388
  8.3 77.9 %copy-start.3 = (f32[768]{0:T(1024)S(1)}, f32[768]{0:T(1024)}, u32[]{:S(2)}) copy-start(f32[768]{0:T(1024)} %param.19) | copy-start | bytes 9220
  8.4 79.8 %copy-start.1 = (bf16[768,768]{1,0:T(8,128)(2,1)S(1)}, bf16[768,768]{1,0:T(8,128)(2,1)}, u32[]{:S(2)}) copy-start(bf16[768,768]{1,0:T(8,128)(2,1)} %refs_11_.1) | copy-start | bytes 3538948
  8.4 79.8 %copy-start.2 = (bf16[2048,256]{1,0:T(8,128)(2,1)S(1)}, bf16[2048,256]{1,0:T(8,128)(2,1)}, u32[]{:S(2)}) copy-start(bf16[2048,256]{1,0:T(8,128)(2,1)} %refs_10_.1) | copy-start | bytes 3145732
  15.4 36.4 %all-to-all-start.1 = ((bf16[32,24,768]{2,1,0:T(8,128)(2,1)}), bf16[32,24,768]{2,1,0:T(8,128)(2,1)S(1)}, u32[]{:S(2)}, u32[]{:S(2)}) async-start(bf16[32,24,768]{2,1,0:T(8,128)(2,1)} %pad_maximum_fusion), calls=%async_computation.1 | async-start | bytes 2359296 | tf_op jit(solution)/shard_map/cond/branch_1_fun/all_to_all | solution.py:76
  55.2 6.0 %collective-permute-start = (bf16[8,8,768]{2,1,0:T(8,128)(2,1)S(1)}, bf16[8,8,768]{2,1,0:T(8,128)(2,1)S(1)}, u32[]{:S(2)}, u32[]{:S(2)}) collective-permute-start(bf16[8,8,768]{2,1,0:T(8,128)(2,1)S(1)} %get-tuple-element.37), channel_id=1, source_target_pairs={{0,8},{1,9},{2,10},{3,11},{4,12},{5,13},{6,14},{7,15},{8,0},{9,1},... | collective-permute-start | bytes 294920 | tf_op jit(solution)/shard_map/ppermute | solution.py:115
  55.7 10.8 %collective-permute-start.1 = (bf16[8,8,768]{2,1,0:T(8,128)(2,1)S(1)}, bf16[8,8,768]{2,1,0:T(8,128)(2,1)S(1)}, u32[]{:S(2)}, u32[]{:S(2)}) collective-permute-start(bf16[8,8,768]{2,1,0:T(8,128)(2,1)S(1)} %get-tuple-element.37), channel_id=1, source_target_pairs={{0,16},{1,17},{2,18},{3,19},{4,20},{5,21},{6,22},{7,23},{8,24},{9,... | collective-permute-start | bytes 294920 | tf_op jit(solution)/shard_map/ppermute | solution.py:115
  57.0 9.4 %collective-permute-start.2 = (bf16[8,8,768]{2,1,0:T(8,128)(2,1)S(1)}, bf16[8,8,768]{2,1,0:T(8,128)(2,1)S(1)}, u32[]{:S(2)}, u32[]{:S(2)}) collective-permute-start(bf16[8,8,768]{2,1,0:T(8,128)(2,1)S(1)} %get-tuple-element.37), channel_id=1, source_target_pairs={{0,24},{1,25},{2,26},{3,27},{4,28},{5,29},{6,30},{7,31},{8,16},{9,... | collective-permute-start | bytes 294920 | tf_op jit(solution)/shard_map/ppermute | solution.py:115
  66.6 11.1 %collective-permute-start.4 = (bf16[8,32,768]{2,1,0:T(8,128)(2,1)S(1)}, bf16[8,32,768]{2,1,0:T(8,128)(2,1)S(1)}, u32[]{:S(2)}, u32[]{:S(2)}) collective-permute-start(bf16[8,32,768]{2,1,0:T(8,128)(2,1)S(1)} %pad_maximum_fusion.1.refs_0_), channel_id=1, source_target_pairs={{0,2},{1,3},{2,0},{3,1},{4,6},{5,7},{6,4},{7,5},{8,10},{9,11},{10,... | collective-permute-start | bytes 1179656 | tf_op jit(solution)/shard_map/ppermute | solution.py:115
  67.6 12.1 %collective-permute-start.6 = (bf16[8,32,768]{2,1,0:T(8,128)(2,1)S(1)}, bf16[8,32,768]{2,1,0:T(8,128)(2,1)S(1)}, u32[]{:S(2)}, u32[]{:S(2)}) collective-permute-start(bf16[8,32,768]{2,1,0:T(8,128)(2,1)S(1)} %pad_maximum_fusion.1.refs_0_), channel_id=1, source_target_pairs={{0,4},{1,5},{2,6},{3,7},{4,0},{5,1},{6,2},{7,3},{8,12},{9,13},{10,... | collective-permute-start | bytes 1179656 | tf_op jit(solution)/shard_map/ppermute | solution.py:115
  68.6 17.5 %collective-permute-start.8 = (bf16[8,32,768]{2,1,0:T(8,128)(2,1)S(1)}, bf16[8,32,768]{2,1,0:T(8,128)(2,1)}, u32[]{:S(2)}, u32[]{:S(2)}) collective-permute-start(bf16[8,32,768]{2,1,0:T(8,128)(2,1)S(1)} %pad_maximum_fusion.1.refs_0_), channel_id=1, source_target_pairs={{0,6},{1,7},{2,4},{3,5},{4,2},{5,3},{6,0},{7,1},{8,14},{9,15},{10,... | collective-permute-start | bytes 1179656 | tf_op jit(solution)/shard_map/ppermute | solution.py:115
  70.1 16.2 %collective-permute-start.3 = (bf16[8,32,768]{2,1,0:T(8,128)(2,1)S(1)}, bf16[8,32,768]{2,1,0:T(8,128)(2,1)}, u32[]{:S(2)}, u32[]{:S(2)}) collective-permute-start(bf16[8,32,768]{2,1,0:T(8,128)(2,1)S(1)} %pad_maximum_fusion.1.refs_0_), channel_id=1, source_target_pairs={{0,1},{1,0},{2,3},{3,2},{4,5},{5,4},{6,7},{7,6},{8,9},{9,8},{10,11... | collective-permute-start | bytes 1179656 | tf_op jit(solution)/shard_map/ppermute | solution.py:115
  77.6 8.7 %collective-permute-start.5 = (bf16[8,32,768]{2,1,0:T(8,128)(2,1)S(1)}, bf16[8,32,768]{2,1,0:T(8,128)(2,1)}, u32[]{:S(2)}, u32[]{:S(2)}) collective-permute-start(bf16[8,32,768]{2,1,0:T(8,128)(2,1)S(1)} %collective-permute-done.4.refs_2_), channel_id=1, source_target_pairs={{0,1},{1,0},{2,3},{3,2},{4,5},{5,4},{6,7},{7,6},{8,9},{9,8},{10,11... | collective-permute-start | bytes 1179656 | tf_op jit(solution)/shard_map/ppermute | solution.py:115
  79.6 6.7 %collective-permute-start.7 = (bf16[8,32,768]{2,1,0:T(8,128)(2,1)S(1)}, bf16[8,32,768]{2,1,0:T(8,128)(2,1)}, u32[]{:S(2)}, u32[]{:S(2)}) collective-permute-start(bf16[8,32,768]{2,1,0:T(8,128)(2,1)S(1)} %collective-permute-done.6.refs_4_), channel_id=1, source_target_pairs={{0,1},{1,0},{2,3},{3,2},{4,5},{5,4},{6,7},{7,6},{8,9},{9,8},{10,11... | collective-permute-start | bytes 1179656 | tf_op jit(solution)/shard_map/ppermute | solution.py:115
  86.1 2.1 %collective-permute-start.9 = (bf16[8,32,768]{2,1,0:T(8,128)(2,1)}, bf16[8,32,768]{2,1,0:T(8,128)(2,1)}, u32[]{:S(2)}, u32[]{:S(2)}) collective-permute-start(bf16[8,32,768]{2,1,0:T(8,128)(2,1)} %collective-permute-done.8.refs_6_), channel_id=1, source_target_pairs={{0,1},{1,0},{2,3},{3,2},{4,5},{5,4},{6,7},{7,6},{8,9},{9,8},{10,11... | collective-permute-start | bytes 1179656 | tf_op jit(solution)/shard_map/ppermute | solution.py:115
  88.2 2.2 %copy-start = (bf16[8,4,256,256]{3,2,1,0:T(8,128)(2,1)S(1)}, bf16[8,4,256,256]{3,2,1,0:T(8,128)(2,1)}, u32[]{:S(2)}) copy-start(bf16[8,4,256,256]{3,2,1,0:T(8,128)(2,1)} %refs_9_.1) | copy-start | bytes 12582916

commit v2 on v1

v2 whole, which is shorter than its diff:
```python
import functools

import jax
import jax.numpy as jnp
from jax import lax
from jax.experimental import pallas as pl
from jax.experimental.pallas import tpu as pltpu
from jax.sharding import PartitionSpec as P

AXES = ("row", "grp")
PLANE = 8
SLOTS = 2
VMEM = pl.BlockSpec(memory_space=pltpu.VMEM)
SMEM = pl.BlockSpec(memory_space=pltpu.SMEM)
HBM = pl.BlockSpec(memory_space=pl.ANY)


def params(mib):
    return pltpu.CompilerParams(vmem_limit_bytes=mib * 2**20)


def held_in_vmem(x):
    return pltpu.with_memory_space_constraint(x, pltpu.VMEM)


def send_kernel(ids, blocks, out, sems):
    me = lax.axis_index(AXES)
    count, _, groups, _, _ = blocks.shape
    slots = out.shape[1]
    held = jnp.int32(0)
    at = [jnp.int32(0)] * slots
    for j in range(ids.shape[0]):
        own = ids[j] // count == me
        for s in range(slots):
            at[s] = jnp.where(own & (held == s), ids[j] % count, at[s])
        held = held + own.astype(jnp.int32)
    copies = []
    for s in range(slots):
        for g in range(groups):
            copies.append(
                pltpu.make_async_copy(
                    blocks.at[at[s], :, g],
                    out.at[pl.ds(g * PLANE, PLANE), s],
                    sems.at[len(copies)],
                )
            )
            copies[-1].start()
    for copy in copies:
        copy.wait()


def send_layout(slots, ids, blocks, devices):
    count, tile, width = blocks.shape
    part = tile // devices
    groups = devices // PLANE
    return pl.pallas_call(
        send_kernel,
        out_shape=jax.ShapeDtypeStruct((devices, slots, part, width), blocks.dtype),
        in_specs=[SMEM, HBM],
        out_specs=VMEM,
        scratch_shapes=[pltpu.SemaphoreType.DMA((slots * groups,))],
        compiler_params=params(16),
    )(ids, blocks.reshape(count, PLANE, groups, part, width))


def rows_kernel(rows, counts, features, weight, out):
    slots, peers = rows.shape
    n = slots * peers
    slot = lax.broadcasted_iota(jnp.int32, (slots, peers), 0)
    wanted = jnp.where(slot < counts[...], rows[...], -1).astype(jnp.float32)
    line = lax.broadcasted_iota(jnp.int32, (n, peers), 0)
    peer = lax.broadcasted_iota(jnp.int32, (n, peers), 1)
    spread = jnp.where(line // slots == peer, 1.0, 0.0)
    by_slot = lax.dot_general(
        spread, wanted, (((1,), (1,)), ((), ())), precision=lax.Precision.HIGHEST,
        preferred_element_type=jnp.float32,
    )
    line = lax.broadcasted_iota(jnp.int32, (n, slots), 0)
    slot = lax.broadcasted_iota(jnp.int32, (n, slots), 1)
    row = jnp.sum(jnp.where(line % slots == slot, by_slot, 0.0), axis=1, keepdims=True)
    row = jnp.round(row).astype(jnp.int32)
    hit = row == lax.broadcasted_iota(jnp.int32, (n, features.shape[0]), 1)
    picked = jnp.where(hit, 1.0, 0.0).astype(jnp.bfloat16)
    picked = jnp.dot(picked, features[...], preferred_element_type=jnp.float32)
    picked = jnp.dot(
        picked.astype(jnp.bfloat16), weight[...], preferred_element_type=jnp.float32
    )
    out[...] = picked.astype(out.dtype)


def listed_rows(rows, counts, features, weight):
    peers, slots = rows.shape
    return pl.pallas_call(
        rows_kernel,
        out_shape=jax.ShapeDtypeStruct((peers * slots, weight.shape[1]), features.dtype),
        in_specs=[VMEM] * 4,
        out_specs=VMEM,
        compiler_params=params(24),
    )(rows.T, counts.reshape(1, -1), features, held_in_vmem(weight))


def pick_kernel(count, ids, got, weight, out):
    n = ids.shape[0]
    owners = [ids[j] // count for j in range(n)]
    parts = []
    for j in range(n):
        slot = jnp.int32(0)
        for i in range(j):
            slot = slot + (owners[i] == owners[j]).astype(jnp.int32)
        part = got[owners[j], jnp.minimum(slot, got.shape[1] - 1)]
        parts.append(part.astype(jnp.float32))
    rows = jnp.concatenate(parts).astype(jnp.bfloat16)
    result = jnp.dot(rows, weight[...], preferred_element_type=jnp.float32)
    out[...] = result.reshape(out.shape).astype(out.dtype)


def pick(ids, got, weight, count):
    return pl.pallas_call(
        functools.partial(pick_kernel, count),
        out_shape=jax.ShapeDtypeStruct((ids.shape[0], *got.shape[2:]), got.dtype),
        in_specs=[SMEM, VMEM, VMEM],
        out_specs=VMEM,
        compiler_params=params(16),
    )(ids, got, held_in_vmem(weight))


def layer_kernel(group, meta, *refs):
    near, far = refs[:6], refs[6:10]
    rows_in, edge, sparse, bias, out, bands = refs[10:]
    first = pl.program_id(0) * group
    blocks = pl.num_programs(0) * group
    _, tiles_per, tile, _ = edge.shape
    stripes, piece_rows, width = near[0].shape
    half = width // 2

    @pl.when(first == 0)
    def _():
        for i in range(PLANE):
            at = pl.multiple_of(meta[blocks * tiles_per + i] * piece_rows, piece_rows)
            for j in range(stripes):
                if i < 6:
                    bands[j, pl.ds(at, piece_rows), :] = near[i][j]
                else:
                    bands[j, pl.ds(at, piece_rows), :half] = far[i - 6][j]
                    bands[j, pl.ds(at, piece_rows), half:] = far[i - 4][j]

    for k in range(group):
        rows = slice(k * tile, (k + 1) * tile)
        total = jnp.dot(sparse[rows], rows_in[...], preferred_element_type=jnp.float32)
        for t in range(tiles_per):
            band = bands[meta[(first + k) * tiles_per + t]]
            total += jnp.dot(edge[k, t], band, preferred_element_type=jnp.float32)
        out[rows] = jnp.maximum(total + bias[...], 0.0).astype(out.dtype)


def layer(meta, pieces, rows_in, edge, sparse, bias, group=2):
    blocks, tiles_per, tile, _ = edge.shape
    stripes, _, width = pieces[0].shape
    return pl.pallas_call(
        functools.partial(layer_kernel, group),
        out_shape=jax.ShapeDtypeStruct((blocks * tile, width), jnp.bfloat16),
        grid_spec=pltpu.PrefetchScalarGridSpec(
            num_scalar_prefetch=1,
            grid=(blocks // group,),
            in_specs=[VMEM] * (len(pieces) + 1)
            + [
                pl.BlockSpec((group, tiles_per, tile, tile), lambda b, m: (b, 0, 0, 0)),
                pl.BlockSpec((group * tile, sparse.shape[1]), lambda b, m: (b, 0)),
                VMEM,
            ],
            out_specs=pl.BlockSpec((group * tile, width), lambda b, m: (b, 0)),
            scratch_shapes=[pltpu.VMEM((stripes, tile, width), jnp.bfloat16)],
        ),
        compiler_params=params(24),
        cost_estimate=pl.CostEstimate(
            flops=2 * blocks * tile * width * (tiles_per * tile + sparse.shape[1]),
            bytes_accessed=2 * (edge.size + sparse.size + blocks * tile * width),
            transcendentals=0,
        ),
    )(
        meta,
        *[held_in_vmem(x) for x in (*pieces, rows_in)],
        pltpu.with_memory_space_constraint(edge, pltpu.HBM),
        pltpu.with_memory_space_constraint(sparse, pltpu.HBM),
        held_in_vmem(bias),
    )


def on_device(features, edge, cols, ids, sparse_w, sparse_rows, sparse_counts, weight, bias):
    block_count, tiles_per, tile, _ = edge.shape
    width = features.shape[1]
    stripe_count = ids.shape[0]
    devices = sparse_rows.shape[1]
    groups = devices // PLANE
    me = lax.axis_index(AXES)
    group, place = me // PLANE, me % PLANE
    blocks = features.reshape(block_count, tile, width)

    def exchange(x):
        return lax.all_to_all(x, AXES, 0, 0, tiled=True)

    def swap(x, mask):
        return lax.ppermute(x, AXES, [(d, d ^ mask) for d in range(devices)])

    def scattered(slots):
        return pick(ids, exchange(send_layout(slots, ids, blocks, devices)), block_count)

    sent = send_layout(SLOTS, ids, blocks, devices)
    features, sent = lax.optimization_barrier((features, sent))
    got = exchange(sent)
    outgoing = listed_rows(sparse_rows[0], sparse_counts[0], features, weight)
    got, outgoing = lax.optimization_barrier((got, outgoing))

    owner = ids // block_count
    load = jnp.max(jnp.sum((owner[:, None] == owner[None, :]).astype(jnp.int32), axis=1))
    most = min(stripe_count, block_count)
    held = lax.cond(
        load > SLOTS,
        lambda x: pick(ids, exchange(send_layout(most, ids, blocks, devices)), weight, block_count),
        lambda x: x,
        pick(ids, got, weight, block_count),
    )

    parts = [held] + [swap(held, PLANE * g) for g in range(1, groups)]
    ordered = [lax.select_n(group, *[parts[q ^ g] for g in range(groups)]) for q in range(groups)]
    own = jnp.concatenate(ordered, axis=1)

    own, outgoing = lax.optimization_barrier((own, outgoing))
    x, y = swap(own, 4), swap(own, 2)
    half = width // 2
    rows_in = exchange(outgoing.reshape(devices, -1, width)).reshape(-1, width)
    left, right = swap(x[:, :, :half], 2), swap(y[:, :, half:], 4)
    pieces = [own, swap(own, 1), y, swap(y, 1), x, swap(x, 1)]
    pieces += [left, swap(left, 1), right, swap(right, 1)]

    meta = jnp.concatenate(
        [cols.reshape(-1), place ^ jnp.arange(PLANE, dtype=jnp.int32)]
    ).astype(jnp.int32)
    return layer(meta, pieces, rows_in, edge, sparse_w, bias.reshape(1, -1))


def solution(mesh):
    placed = (
        P(AXES, None),
        P(AXES, None, None, None),
        P(AXES, None),
        P(),
        P(AXES, None),
        P(AXES, None, None),
        P(AXES, None),
        P(),
        P(),
    )
    return jax.shard_map(
        on_device, mesh=mesh, in_specs=placed, out_specs=P(AXES, None), check_vma=False
    )
```

time: 104 us -> 74.9 us (0.72)
  waiting for transfers between devices: 53.7 us -> 37.8 us
  local copies, waits for them, and re-layouts: 11.5 us -> 0.23 us
  loops' own time: 4.09 us -> 0.01 us
  other arithmetic: 5.05 us -> 1.06 us
  Pallas kernels: 12.8 us -> 16.6 us
  starting transfers between devices: 15.2 us -> 17.9 us
    all_to_all x1 -> x2, waiting for transfers between devices: 29.1 us -> 14.5 us  [exchange(): return lax.all_to_all(x, AXES, 0, 0, tiled=True)]
    gather x2 -> x0, local copies, waits for them, and re-layouts: 5.38 us -> none  [the longest x1 3.69 us: on_device(): outgoing = features[sparse_rows[0]]]
    another operation x1, loops' own time: 4.09 us -> 0.01 us  [on_device(): lax.cond(load > SLOTS, lambda x: pick(ids, exchange(send_layout(most, ids...]
    pallas_call x1 -> x4, Pallas kernels: 12.8 us -> 16.6 us  [the longest x1 8.17 us: layer(): pl.pallas_call(functools.partial(layer_kernel, group), out_shape=jax.Shap...]
    all_to_all x1 -> x2, starting transfers between devices: 7.3 us -> 11 us  [exchange(): return lax.all_to_all(x, AXES, 0, 0, tiled=True)]
    unnamed x11 -> x13, local copies, waits for them, and re-layouts: 2.29 us -> 0.11 us
    slice x2, local copies, waits for them, and re-layouts: 1.59 us -> 0.04 us  [on_device(): left, right = (swap(x[:, :, :half], 2), swap(y[:, :, half:], 4))]
    select_n x3 -> x1, other arithmetic: 1.46 us -> 0.01 us  [on_device(): owner = ids // block_count]
  transfers between devices with their start and end apart: 11 -> 14, of which waited for: 7 -> 8; matrix products, arithmetic and copies ran while one was open for 0% -> 2% of each run, Pallas kernels for 0% -> 6%
where the time goes in v2:
time: 74.9 us; the launch traced here: 74.4 us
  waiting for transfers between devices  37.8 us (50%)
  starting transfers between devices  17.9 us (24%)
  Pallas kernels  16.6 us (22%)
  other arithmetic  1.06 us (1%)
  between operations  0.87 us (1%)
    ppermute x12, waiting for transfers between devices, swap(): return lax.ppermute(x, AXES, [(d, d ^ mask) for d in range(devices)])  23.3 us
    all_to_all x2, waiting for transfers between devices, exchange(): return lax.all_to_all(x, AXES, 0, 0, tiled=True)  14.5 us
    all_to_all x2, starting transfers between devices, exchange(): return lax.all_to_all(x, AXES, 0, 0, tiled=True)  11 us
    pallas_call x1, Pallas kernels, layer(): pl.pallas_call(functools.partial(layer_kernel, group), out_shape=jax.Shap...  8.17 us
    ppermute x12, starting transfers between devices, swap(): return lax.ppermute(x, AXES, [(d, d ^ mask) for d in range(devices)])  6.82 us
    pallas_call x1, Pallas kernels, listed_rows(): pl.pallas_call(rows_kernel, out_shape=jax.ShapeDtypeStruct((peers * slots...  4.51 us
    pallas_call x1, Pallas kernels, send_layout(): pl.pallas_call(send_kernel, out_shape=jax.ShapeDtypeStruct((devices, slot...  3.02 us
  transfers between devices with their start and end apart: 14, of which 8 were waited for; matrix products, arithmetic and copies ran while one was open for 2% of the time, Pallas kernels for 6%

profile of v2, /device:TPU:0, one launch (start us, length us, event | category | flops | bytes accessed | tf_op | source)
XLA Modules:
  0.0 74.4 jit_solution(12354075097369169281)
XLA Ops:
  0.0 0.0 copy-start.3
  0.0 0.0 copy-start
  0.0 0.0 copy-start.1
  0.0 0.0 copy-start.2
  0.0 3.0 %shard_map.91 = bf16[32,2,8,768]{3,2,1,0:T(8,128)(2,1)} custom-call(s32[8]{0:T(128)} %ids.3, bf16[8,8,4,8,768]{4,3,2,1,0:T(8,128)(2,1)} %bitcast.9), custom_call_target="tpu_custom_call" | custom-call | tf_op jit(solution)/shard_map/pallas_call | solution.py:56
  3.0 7.3 %all-to-all-start.1 = ((bf16[32,2,8,768]{3,2,1,0:T(8,128)(2,1)}), bf16[32,2,8,768]{3,2,1,0:T(8,128)(2,1)S(1)}, u32[]{:S(2)}, u32[]{:S(2)}) async-start(bf16[32,2,8,768]{3,2,1,0:T(8,128)(2,1)} %shard_map.91), calls=%async_computation.1 | async-start | bytes 1572864 | tf_op jit(solution)/shard_map/all_to_all | solution.py:200
  10.4 0.0 copy-done.3
  10.4 0.2 convert_reduce_fusion
  10.6 0.7 reduce_max.9
  12.0 0.0 copy-done
  12.0 0.0 copy-done.1
  12.0 0.0 copy-done.2
  12.0 4.5 %shard_map.92 = bf16[256,768]{1,0:T(8,128)(2,1)} custom-call(s32[8,32]{1,0:T(8,128)S(1)} %bitcast.8, s32[1,32]{1,0:T(1,128)S(1)} %copy-done.2, bf16[2048,768]{1,0:T(8,128)(2,1)} %features, bf16[768,768]{1,0:T(8,128)(2,1)S(1)} %copy-done), custom_call_target="tpu_custom_call" | custom-call | tf_op jit(solution)/shard_map/pallas_call | solution.py:93
  16.5 14.5 %all-to-all-done.1.got = bf16[32,2,8,768]{3,2,1,0:T(8,128)(2,1)S(1)} async-done(((bf16[32,2,8,768]{3,2,1,0:T(8,128)(2,1)}), bf16[32,2,8,768]{3,2,1,0:T(8,128)(2,1)S(1)}, u32[]{:S(2)}, u32[]{:S(2)}) %all-to-all-start.1) | async-done | bytes 786464 | tf_op jit(solution)/shard_map/all_to_all | solution.py:200
  31.0 0.9 %shard_map.93 = bf16[8,8,768]{2,1,0:T(8,128)(2,1)S(1)} custom-call(s32[8]{0:T(128)S(1)} %copy-done.3, bf16[32,2,8,768]{3,2,1,0:T(8,128)(2,1)S(1)} %all-to-all-done.1.got, bf16[768,768]{1,0:T(8,128)(2,1)S(1)} %copy-done), custom_call_target="tpu_custom_call" | custom-call | tf_op jit(solution)/shard_map/pallas_call | solution.py:118
  31.9 0.0 copy-start.5
  31.9 0.0 copy-start.4
  31.9 1.4 %collective-permute-start = (bf16[8,8,768]{2,1,0:T(8,128)(2,1)S(1)}, bf16[8,8,768]{2,1,0:T(8,128)(2,1)S(1)}, u32[]{:S(2)}, u32[]{:S(2)}) collective-permute-start(bf16[8,8,768]{2,1,0:T(8,128)(2,1)S(1)} %get-tuple-element.34), channel_id=1, source_target_pairs={{0,8},{1,9},{2,10},{3,11},{4,12},{5,13},{6,14},{7,15},{8,0},{9,1},... | collective-permute-start | bytes 294920 | tf_op jit(solution)/shard_map/ppermute | solution.py:203
  33.3 0.5 collective-permute-start.1
  33.8 2.6 %collective-permute-start.2 = (bf16[8,8,768]{2,1,0:T(8,128)(2,1)S(1)}, bf16[8,8,768]{2,1,0:T(8,128)(2,1)S(1)}, u32[]{:S(2)}, u32[]{:S(2)}) collective-permute-start(bf16[8,8,768]{2,1,0:T(8,128)(2,1)S(1)} %get-tuple-element.34), channel_id=1, source_target_pairs={{0,24},{1,25},{2,26},{3,27},{4,28},{5,29},{6,30},{7,31},{8,16},{9,... | collective-permute-start | bytes 294920 | tf_op jit(solution)/shard_map/ppermute | solution.py:203
  36.4 0.2 collective-permute-done
  36.6 7.3 %collective-permute-done.1 = bf16[8,8,768]{2,1,0:T(8,128)(2,1)S(1)} collective-permute-done((bf16[8,8,768]{2,1,0:T(8,128)(2,1)S(1)}, bf16[8,8,768]{2,1,0:T(8,128)(2,1)S(1)}, u32[]{:S(2)}, u32[]{:S(2)}) %collective-permute-start.1) | collective-permute-done | bytes 98336 | tf_op jit(solution)/shard_map/ppermute | solution.py:203
  43.9 0.0 collective-permute-done.2
  43.9 0.1 select_select_fusion.3
  44.0 0.8 %collective-permute-start.4 = (bf16[8,32,768]{2,1,0:T(8,128)(2,1)S(1)}, bf16[8,32,768]{2,1,0:T(8,128)(2,1)S(1)}, u32[]{:S(2)}, u32[]{:S(2)}) collective-permute-start(bf16[8,32,768]{2,1,0:T(8,128)(2,1)S(1)} %pad_maximum_fusion.refs_0_), channel_id=1, source_target_pairs={{0,2},{1,3},{2,0},{3,1},{4,6},{5,7},{6,4},{7,5},{8,10},{9,11},{10,... | collective-permute-start | bytes 1179656 | tf_op jit(solution)/shard_map/ppermute | solution.py:203
  44.8 0.8 %collective-permute-start.6 = (bf16[8,32,768]{2,1,0:T(8,128)(2,1)S(1)}, bf16[8,32,768]{2,1,0:T(8,128)(2,1)S(1)}, u32[]{:S(2)}, u32[]{:S(2)}) collective-permute-start(bf16[8,32,768]{2,1,0:T(8,128)(2,1)S(1)} %pad_maximum_fusion.refs_0_), channel_id=1, source_target_pairs={{0,4},{1,5},{2,6},{3,7},{4,0},{5,1},{6,2},{7,3},{8,12},{9,13},{10,... | collective-permute-start | bytes 1179656 | tf_op jit(solution)/shard_map/ppermute | solution.py:203
  45.6 3.7 %all-to-all-start.2 = ((bf16[32,8,768]{2,1,0:T(8,128)(2,1)}), bf16[32,8,768]{2,1,0:T(8,128)(2,1)S(1)}, u32[]{:S(2)}, u32[]{:S(2)}) async-start(bf16[32,8,768]{2,1,0:T(8,128)(2,1)} %bitcast.4), calls=%async_computation.2 | async-start | bytes 786432 | tf_op jit(solution)/shard_map/all_to_all | solution.py:200
  49.3 4.4 %collective-permute-done.4.refs_2_ = bf16[8,32,768]{2,1,0:T(8,128)(2,1)S(1)} collective-permute-done((bf16[8,32,768]{2,1,0:T(8,128)(2,1)S(1)}, bf16[8,32,768]{2,1,0:T(8,128)(2,1)S(1)}, u32[]{:S(2)}, u32[]{:S(2)}) %collective-permute-start.4) | collective-permute-done | bytes 393248 | tf_op jit(solution)/shard_map/ppermute | solution.py:203
  53.7 0.1 collective-permute-start.10
  53.8 5.2 %collective-permute-done.6.refs_4_ = bf16[8,32,768]{2,1,0:T(8,128)(2,1)S(1)} collective-permute-done((bf16[8,32,768]{2,1,0:T(8,128)(2,1)S(1)}, bf16[8,32,768]{2,1,0:T(8,128)(2,1)S(1)}, u32[]{:S(2)}, u32[]{:S(2)}) %collective-permute-start.6) | collective-permute-done | bytes 393248 | tf_op jit(solution)/shard_map/ppermute | solution.py:203
  59.1 0.1 collective-permute-start.8
  59.1 0.1 collective-permute-start.3
  59.2 0.5 collective-permute-start.5
  59.7 0.1 collective-permute-start.7
  59.8 0.0 copy-done.5
  59.8 0.1 copy.12
  59.9 0.1 reshape.14
  60.0 0.0 copy-done.4
  60.0 2.8 %collective-permute-done.10.refs_8_ = bf16[8,32,384]{2,1,0:T(8,128)(2,1)S(1)} collective-permute-done((bf16[8,32,384]{2,1,0:T(8,128)(2,1)S(1)}, bf16[8,32,384]{2,1,0:T(8,128)(2,1)S(1)}, u32[]{:S(2)}, u32[]{:S(2)}) %collective-permute-start.10) | collective-permute-done | bytes 196640 | tf_op jit(solution)/shard_map/ppermute | solution.py:203
  62.8 0.0 collective-permute-start.11
  62.8 2.0 %collective-permute-done.8.refs_6_ = bf16[8,32,384]{2,1,0:T(8,128)(2,1)S(1)} collective-permute-done((bf16[8,32,384]{2,1,0:T(8,128)(2,1)S(1)}, bf16[8,32,384]{2,1,0:T(8,128)(2,1)S(1)}, u32[]{:S(2)}, u32[]{:S(2)}) %collective-permute-start.8) | collective-permute-done | bytes 196640 | tf_op jit(solution)/shard_map/ppermute | solution.py:203
  64.8 0.0 collective-permute-start.9
  64.8 0.1 pad_add_fusion.meta
  64.9 0.0 collective-permute-done.3.refs_1_
  64.9 0.0 all-to-all-done.2
  64.9 0.0 collective-permute-done.5.refs_3_
  64.9 0.0 collective-permute-done.7.refs_5_
  64.9 0.0 collective-permute-done.11.refs_9_
  64.9 1.3 %collective-permute-done.9.refs_7_ = bf16[8,32,384]{2,1,0:T(8,128)(2,1)S(1)} collective-permute-done((bf16[8,32,384]{2,1,0:T(8,128)(2,1)S(1)}, bf16[8,32,384]{2,1,0:T(8,128)(2,1)S(1)}, u32[]{:S(2)}, u32[]{:S(2)}) %collective-permute-start.9) | collective-permute-done | bytes 196640 | tf_op jit(solution)/shard_map/ppermute | solution.py:203
  66.2 8.2 %shard_map.94 = bf16[2048,768]{1,0:T(8,128)(2,1)} custom-call(s32[40]{0:T(128)S(1)} %pad_add_fusion.meta, bf16[8,32,768]{2,1,0:T(8,128)(2,1)S(1)} %pad_maximum_fusion.refs_0_, bf16[8,32,768]{2,1,0:T(8,128)(2,1)S(1)} %collective-permute-done.3.refs_1_, bf16[8,32,768]{2,1,0:T(8,128)(2,1)S(1)} %collective-permute-done.4.refs_2_, ...), custom_call_target="tpu_custom_call" | custom-call | flops 4026531840 | bytes 8388608 | tf_op jit(solution)/shard_map/pallas_call | solution.py:159
  (7 shorter events, 0.1 us)
Async XLA Ops:
  0.0 10.4 %copy-start.3 = (s32[8]{0:T(128)S(1)}, s32[8]{0:T(128)}, u32[]{:S(2)}) copy-start(s32[8]{0:T(128)} %ids.3) | copy-start | bytes 100
  0.0 12.0 %copy-start = (bf16[768,768]{1,0:T(8,128)(2,1)S(1)}, bf16[768,768]{1,0:T(8,128)(2,1)}, u32[]{:S(2)}) copy-start(bf16[768,768]{1,0:T(8,128)(2,1)} %weight.3) | copy-start | bytes 3538948
  0.0 12.0 %copy-start.1 = (s32[1,32,8]{1,2,0:T(8,128)S(1)}, s32[1,32,8]{1,2,0:T(8,128)}, u32[]{:S(2)}) copy-start(s32[1,32,8]{1,2,0:T(8,128)} %param.16) | copy-start | bytes 3076
  0.0 12.0 %copy-start.2 = (s32[1,32]{1,0:T(1,128)S(1)}, s32[1,32]{1,0:T(1,128)}, u32[]{:S(2)}) copy-start(s32[1,32]{1,0:T(1,128)} %counts.1) | copy-start | bytes 388
  3.0 27.9 %all-to-all-start.1 = ((bf16[32,2,8,768]{3,2,1,0:T(8,128)(2,1)}), bf16[32,2,8,768]{3,2,1,0:T(8,128)(2,1)S(1)}, u32[]{:S(2)}, u32[]{:S(2)}) async-start(bf16[32,2,8,768]{3,2,1,0:T(8,128)(2,1)} %shard_map.91), calls=%async_computation.1 | async-start | bytes 1572864 | tf_op jit(solution)/shard_map/all_to_all | solution.py:200
  31.9 27.9 %copy-start.5 = (s32[8,4]{0,1:T(4,128)S(1)}, s32[8,4]{0,1:T(4,128)}, u32[]{:S(2)}) copy-start(s32[8,4]{0,1:T(4,128)} %param.13) | copy-start | bytes 388
  31.9 28.1 %copy-start.4 = (f32[768]{0:T(1024)S(1)}, f32[768]{0:T(1024)}, u32[]{:S(2)}) copy-start(f32[768]{0:T(1024)} %param.19) | copy-start | bytes 9220
  31.9 4.7 %collective-permute-start = (bf16[8,8,768]{2,1,0:T(8,128)(2,1)S(1)}, bf16[8,8,768]{2,1,0:T(8,128)(2,1)S(1)}, u32[]{:S(2)}, u32[]{:S(2)}) collective-permute-start(bf16[8,8,768]{2,1,0:T(8,128)(2,1)S(1)} %get-tuple-element.34), channel_id=1, source_target_pairs={{0,8},{1,9},{2,10},{3,11},{4,12},{5,13},{6,14},{7,15},{8,0},{9,1},... | collective-permute-start | bytes 294920 | tf_op jit(solution)/shard_map/ppermute | solution.py:203
  33.3 10.7 %collective-permute-start.1 = (bf16[8,8,768]{2,1,0:T(8,128)(2,1)S(1)}, bf16[8,8,768]{2,1,0:T(8,128)(2,1)S(1)}, u32[]{:S(2)}, u32[]{:S(2)}) collective-permute-start(bf16[8,8,768]{2,1,0:T(8,128)(2,1)S(1)} %get-tuple-element.34), channel_id=1, source_target_pairs={{0,16},{1,17},{2,18},{3,19},{4,20},{5,21},{6,22},{7,23},{8,24},{9,... | collective-permute-start | bytes 294920 | tf_op jit(solution)/shard_map/ppermute | solution.py:203
  33.8 10.1 %collective-permute-start.2 = (bf16[8,8,768]{2,1,0:T(8,128)(2,1)S(1)}, bf16[8,8,768]{2,1,0:T(8,128)(2,1)S(1)}, u32[]{:S(2)}, u32[]{:S(2)}) collective-permute-start(bf16[8,8,768]{2,1,0:T(8,128)(2,1)S(1)} %get-tuple-element.34), channel_id=1, source_target_pairs={{0,24},{1,25},{2,26},{3,27},{4,28},{5,29},{6,30},{7,31},{8,16},{9,... | collective-permute-start | bytes 294920 | tf_op jit(solution)/shard_map/ppermute | solution.py:203
  44.0 9.7 %collective-permute-start.4 = (bf16[8,32,768]{2,1,0:T(8,128)(2,1)S(1)}, bf16[8,32,768]{2,1,0:T(8,128)(2,1)S(1)}, u32[]{:S(2)}, u32[]{:S(2)}) collective-permute-start(bf16[8,32,768]{2,1,0:T(8,128)(2,1)S(1)} %pad_maximum_fusion.refs_0_), channel_id=1, source_target_pairs={{0,2},{1,3},{2,0},{3,1},{4,6},{5,7},{6,4},{7,5},{8,10},{9,11},{10,... | collective-permute-start | bytes 1179656 | tf_op jit(solution)/shard_map/ppermute | solution.py:203
  44.8 14.2 %collective-permute-start.6 = (bf16[8,32,768]{2,1,0:T(8,128)(2,1)S(1)}, bf16[8,32,768]{2,1,0:T(8,128)(2,1)S(1)}, u32[]{:S(2)}, u32[]{:S(2)}) collective-permute-start(bf16[8,32,768]{2,1,0:T(8,128)(2,1)S(1)} %pad_maximum_fusion.refs_0_), channel_id=1, source_target_pairs={{0,4},{1,5},{2,6},{3,7},{4,0},{5,1},{6,2},{7,3},{8,12},{9,13},{10,... | collective-permute-start | bytes 1179656 | tf_op jit(solution)/shard_map/ppermute | solution.py:203
  45.6 19.3 %all-to-all-start.2 = ((bf16[32,8,768]{2,1,0:T(8,128)(2,1)}), bf16[32,8,768]{2,1,0:T(8,128)(2,1)S(1)}, u32[]{:S(2)}, u32[]{:S(2)}) async-start(bf16[32,8,768]{2,1,0:T(8,128)(2,1)} %bitcast.4), calls=%async_computation.2 | async-start | bytes 786432 | tf_op jit(solution)/shard_map/all_to_all | solution.py:200
  53.7 9.1 %collective-permute-start.10 = (bf16[8,32,384]{2,1,0:T(8,128)(2,1)S(1)}, bf16[8,32,384]{2,1,0:T(8,128)(2,1)S(1)}, u32[]{:S(2)}, u32[]{:S(2)}) collective-permute-start(bf16[8,32,384]{2,1,0:T(8,128)(2,1)S(1)} %slice.9), channel_id=1, source_target_pairs={{0,4},{1,5},{2,6},{3,7},{4,0},{5,1},{6,2},{7,3},{8,12},{9,13},{10,... | collective-permute-start | bytes 589832 | tf_op jit(solution)/shard_map/ppermute | solution.py:203
  59.1 5.7 %collective-permute-start.8 = (bf16[8,32,384]{2,1,0:T(8,128)(2,1)S(1)}, bf16[8,32,384]{2,1,0:T(8,128)(2,1)S(1)}, u32[]{:S(2)}, u32[]{:S(2)}) collective-permute-start(bf16[8,32,384]{2,1,0:T(8,128)(2,1)S(1)} %slice.8), channel_id=1, source_target_pairs={{0,2},{1,3},{2,0},{3,1},{4,6},{5,7},{6,4},{7,5},{8,10},{9,11},{10,... | collective-permute-start | bytes 589832 | tf_op jit(solution)/shard_map/ppermute | solution.py:203
  59.1 5.7 %collective-permute-start.3 = (bf16[8,32,768]{2,1,0:T(8,128)(2,1)S(1)}, bf16[8,32,768]{2,1,0:T(8,128)(2,1)S(1)}, u32[]{:S(2)}, u32[]{:S(2)}) collective-permute-start(bf16[8,32,768]{2,1,0:T(8,128)(2,1)S(1)} %pad_maximum_fusion.refs_0_), channel_id=1, source_target_pairs={{0,1},{1,0},{2,3},{3,2},{4,5},{5,4},{6,7},{7,6},{8,9},{9,8},{10,11... | collective-permute-start | bytes 1179656 | tf_op jit(solution)/shard_map/ppermute | solution.py:203
  59.2 5.7 %collective-permute-start.5 = (bf16[8,32,768]{2,1,0:T(8,128)(2,1)S(1)}, bf16[8,32,768]{2,1,0:T(8,128)(2,1)S(1)}, u32[]{:S(2)}, u32[]{:S(2)}) collective-permute-start(bf16[8,32,768]{2,1,0:T(8,128)(2,1)S(1)} %collective-permute-done.4.refs_2_), channel_id=1, source_target_pairs={{0,1},{1,0},{2,3},{3,2},{4,5},{5,4},{6,7},{7,6},{8,9},{9,8},{10,11... | collective-permute-start | bytes 1179656 | tf_op jit(solution)/shard_map/ppermute | solution.py:203
  59.7 5.2 %collective-permute-start.7 = (bf16[8,32,768]{2,1,0:T(8,128)(2,1)S(1)}, bf16[8,32,768]{2,1,0:T(8,128)(2,1)S(1)}, u32[]{:S(2)}, u32[]{:S(2)}) collective-permute-start(bf16[8,32,768]{2,1,0:T(8,128)(2,1)S(1)} %collective-permute-done.6.refs_4_), channel_id=1, source_target_pairs={{0,1},{1,0},{2,3},{3,2},{4,5},{5,4},{6,7},{7,6},{8,9},{9,8},{10,11... | collective-permute-start | bytes 1179656 | tf_op jit(solution)/shard_map/ppermute | solution.py:203
  62.8 2.1 %collective-permute-start.11 = (bf16[8,32,384]{2,1,0:T(8,128)(2,1)S(1)}, bf16[8,32,384]{2,1,0:T(8,128)(2,1)S(1)}, u32[]{:S(2)}, u32[]{:S(2)}) collective-permute-start(bf16[8,32,384]{2,1,0:T(8,128)(2,1)S(1)} %collective-permute-done.10.refs_8_), channel_id=1, source_target_pairs={{0,1},{1,0},{2,3},{3,2},{4,5},{5,4},{6,7},{7,6},{8,9},{9,8},{10,11... | collective-permute-start | bytes 589832 | tf_op jit(solution)/shard_map/ppermute | solution.py:203
  64.8 1.4 %collective-permute-start.9 = (bf16[8,32,384]{2,1,0:T(8,128)(2,1)S(1)}, bf16[8,32,384]{2,1,0:T(8,128)(2,1)S(1)}, u32[]{:S(2)}, u32[]{:S(2)}) collective-permute-start(bf16[8,32,384]{2,1,0:T(8,128)(2,1)S(1)} %collective-permute-done.8.refs_6_), channel_id=1, source_target_pairs={{0,1},{1,0},{2,3},{3,2},{4,5},{5,4},{6,7},{7,6},{8,9},{9,8},{10,11... | collective-permute-start | bytes 589832 | tf_op jit(solution)/shard_map/ppermute | solution.py:203

commit v3 on v2

--- a/solution.py
+++ b/solution.py
@@ -9,7 +9,8 @@
 
 AXES = ("row", "grp")
 PLANE = 8
-SLOTS = 2
+SLOTS = 3
+PLANE_SLOTS = 5
 VMEM = pl.BlockSpec(memory_space=pltpu.VMEM)
 SMEM = pl.BlockSpec(memory_space=pltpu.SMEM)
 HBM = pl.BlockSpec(memory_space=pl.ANY)
@@ -21,6 +22,140 @@
 
 def held_in_vmem(x):
     return pltpu.with_memory_space_constraint(x, pltpu.VMEM)
+
+
+def scan(ids, mine, fields):
+    held = jnp.int32(0)
+    found = [[jnp.int32(0)] * SLOTS for _ in fields]
+    for j in range(ids.shape[0]):
+        own = mine(ids[j])
+        for f, field in enumerate(fields):
+            for s in range(SLOTS):
+                found[f][s] = jnp.where(own & (held == s), field(ids[j]), found[f][s])
+        held = held + own.astype(jnp.int32)
+    return found
+
+
+def slot_of(ids, j, unit):
+    slot = jnp.int32(0)
+    for i in range(j):
+        slot = slot + (ids[i] // unit == ids[j] // unit).astype(jnp.int32)
+    return slot
+
+
+def halves_kernel(ids, blocks, keep, give, sems):
+    me = lax.axis_index(AXES)
+    count = blocks.shape[0]
+    core = me % 2
+    (at,) = scan(ids, lambda i: i // (2 * count) == me // 2, [lambda i: i % count])
+    copies = []
+    for s in range(SLOTS):
+        for out, half in ((give, 1 - core), (keep, core)):
+            copies.append(
+                pltpu.make_async_copy(blocks.at[at[s], :, half], out.at[:, s], sems.at[len(copies)])
+            )
+            copies[-1].start()
+    for copy in copies:
+        copy.wait()
+
+
+def halves(ids, blocks, devices):
+    count, tile, width = blocks.shape
+    part = tile // devices
+    groups = devices // PLANE
+    shape = pltpu.VMEM((PLANE // 2, SLOTS, groups, part, width), blocks.dtype)
+    return pl.pallas_call(
+        halves_kernel,
+        out_shape=[shape, shape],
+        in_specs=[SMEM, HBM],
+        out_specs=[VMEM, VMEM],
+        scratch_shapes=[pltpu.SemaphoreType.DMA((2 * SLOTS,))],
+        compiler_params=params(16),
+    )(ids, blocks.reshape(count, PLANE // 2, 2, groups, part, width))
+
+
+def merge_kernel(count, ids, keep, got, *outs):
+    me = lax.axis_index(AXES)
+    core, place = me % 2, me % PLANE // 2
+    (cores,) = scan(
+        ids, lambda i: i // (2 * count) == me // 2, [lambda i: i // count % 2]
+    )
+    for s in range(SLOTS):
+
+        @pl.when(cores[s] == core)
+        def _():
+            for m, out in enumerate(outs):
+                out[s] = keep[place ^ m, s]
+
+        @pl.when(cores[s] != core)
+        def _():
+            for m, out in enumerate(outs):
+                out[s] = got[place ^ m, s]
+
+
+def merge(ids, keep, got, count):
+    shape = pltpu.VMEM(keep.shape[1:], keep.dtype)
+    return pl.pallas_call(
+        functools.partial(merge_kernel, count),
+        out_shape=[shape] * keep.shape[0],
+        in_specs=[SMEM, VMEM, VMEM],
+        out_specs=[VMEM] * keep.shape[0],
+        compiler_params=params(16),
+    )(ids, held_in_vmem(keep), held_in_vmem(got))
+
+
+def sort_kernel(count, ids, *refs):
+    near, outs = refs[: PLANE // 2], refs[PLANE // 2 :]
+    me = lax.axis_index(AXES)
+    group, place = me // PLANE, me % PLANE // 2
+    for j in range(ids.shape[0]):
+        owner = ids[j] // count
+        slot = jnp.minimum(slot_of(ids, j, 2 * count), SLOTS - 1)
+        to = jnp.minimum(slot_of(ids, j, PLANE * count), PLANE_SLOTS - 1)
+        for m, ref in enumerate(near):
+
+            @pl.when((owner // PLANE == group) & (owner % PLANE // 2 ^ place == m))
+            def _():
+                for g, out in enumerate(outs):
+                    out[to] = ref[slot, group ^ g]
+
+
+def sort(ids, near, count):
+    _, groups, part, width = near[0].shape
+    shape = pltpu.VMEM((PLANE_SLOTS, part, width), near[0].dtype)
+    return pl.pallas_call(
+        functools.partial(sort_kernel, count),
+        out_shape=[shape] * groups,
+        in_specs=[SMEM] + [VMEM] * len(near),
+        out_specs=[VMEM] * groups,
+        compiler_params=params(16),
+    )(ids, *[held_in_vmem(x) for x in near])
+
+
+def choose_kernel(count, ids, *refs):
+    arrived, weight, out = refs[:-2], refs[-2], refs[-1]
+    group = lax.axis_index(AXES) // PLANE
+    parts = []
+    for j in range(ids.shape[0]):
+        at = group ^ ids[j] // (count * PLANE)
+        slot = jnp.minimum(slot_of(ids, j, PLANE * count), PLANE_SLOTS - 1)
+        part = arrived[0][slot].astype(jnp.float32)
+        for g in range(1, len(arrived)):
+            part = jnp.where(at == g, arrived[g][slot].astype(jnp.float32), part)
+        parts.append(part)
+    rows = jnp.concatenate(parts).astype(jnp.bfloat16)
+    result = jnp.dot(rows, weight[...], preferred_element_type=jnp.float32)
+    out[...] = result.reshape(out.shape).astype(out.dtype)
+
+
+def choose(ids, arrived, weight, count):
+    return pl.pallas_call(
+        functools.partial(choose_kernel, count),
+        out_shape=jax.ShapeDtypeStruct((ids.shape[0], *arrived[0].shape[1:]), arrived[0].dtype),
+        in_specs=[SMEM] + [VMEM] * (len(arrived) + 1),
+        out_specs=VMEM,
+        compiler_params=params(16),
+    )(ids, *[held_in_vmem(x) for x in arrived], held_in_vmem(weight))
 
 
 def send_kernel(ids, blocks, out, sems):
@@ -63,14 +198,17 @@
     )(ids, blocks.reshape(count, PLANE, groups, part, width))
 
 
-def rows_kernel(rows, counts, features, weight, out):
+def rows_kernel(rows, counts, features, weight, *outs):
     slots, peers = rows.shape
     n = slots * peers
+    groups = peers // PLANE
+    me = lax.axis_index(AXES)
     slot = lax.broadcasted_iota(jnp.int32, (slots, peers), 0)
     wanted = jnp.where(slot < counts[...], rows[...], -1).astype(jnp.float32)
-    line = lax.broadcasted_iota(jnp.int32, (n, peers), 0)
+    at = lax.broadcasted_iota(jnp.int32, (n, peers), 0) // slots
+    away = at % groups * PLANE + at // groups % (PLANE // 2) * 2 + at // (groups * PLANE // 2)
     peer = lax.broadcasted_iota(jnp.int32, (n, peers), 1)
-    spread = jnp.where(line // slots == peer, 1.0, 0.0)
+    spread = jnp.where(away ^ peer == me, 1.0, 0.0)
     by_slot = lax.dot_general(
         spread, wanted, (((1,), (1,)), ((), ())), precision=lax.Precision.HIGHEST,
         preferred_element_type=jnp.float32,
@@ -85,30 +223,29 @@
     picked = jnp.dot(
         picked.astype(jnp.bfloat16), weight[...], preferred_element_type=jnp.float32
     )
-    out[...] = picked.astype(out.dtype)
+    picked = picked.reshape(len(outs), *outs[0].shape)
+    for core, out in enumerate(outs):
+        out[...] = picked[core].astype(out.dtype)
 
 
 def listed_rows(rows, counts, features, weight):
     peers, slots = rows.shape
+    shape = pltpu.VMEM((PLANE // 2, peers // PLANE, slots, weight.shape[1]), features.dtype)
     return pl.pallas_call(
         rows_kernel,
-        out_shape=jax.ShapeDtypeStruct((peers * slots, weight.shape[1]), features.dtype),
+        out_shape=[shape, shape],
         in_specs=[VMEM] * 4,
-        out_specs=VMEM,
+        out_specs=[VMEM] * 2,
         compiler_params=params(24),
     )(rows.T, counts.reshape(1, -1), features, held_in_vmem(weight))
 
 
 def pick_kernel(count, ids, got, weight, out):
     n = ids.shape[0]
-    owners = [ids[j] // count for j in range(n)]
     parts = []
     for j in range(n):
-        slot = jnp.int32(0)
-        for i in range(j):
-            slot = slot + (owners[i] == owners[j]).astype(jnp.int32)
-        part = got[owners[j], jnp.minimum(slot, got.shape[1] - 1)]
-        parts.append(part.astype(jnp.float32))
+        slot = jnp.minimum(slot_of(ids, j, count), got.shape[1] - 1)
+        parts.append(got[ids[j] // count, slot].astype(jnp.float32))
     rows = jnp.concatenate(parts).astype(jnp.bfloat16)
     result = jnp.dot(rows, weight[...], preferred_element_type=jnp.float32)
     out[...] = result.reshape(out.shape).astype(out.dtype)
@@ -126,7 +263,8 @@
 
 def layer_kernel(group, meta, *refs):
     near, far = refs[:6], refs[6:10]
-    rows_in, edge, sparse, bias, out, bands = refs[10:]
+    listed, refs = refs[10:-7], refs[-7:]
+    edge, sparse, bias, out, bands, rows_f32, rows_in = refs
     first = pl.program_id(0) * group
     blocks = pl.num_programs(0) * group
     _, tiles_per, tile, _ = edge.shape
@@ -143,6 +281,14 @@
                 else:
                     bands[j, pl.ds(at, piece_rows), :half] = far[i - 6][j]
                     bands[j, pl.ds(at, piece_rows), half:] = far[i - 4][j]
+        me = lax.axis_index(AXES)
+        slots = listed[0].shape[2]
+        for g, ref in enumerate(listed):
+            for m in range(PLANE // 2):
+                for k in range(2):
+                    at = pl.multiple_of((me ^ (g * PLANE + m * 2 + k)) * slots, slots)
+                    rows_f32[pl.ds(at, slots), :] = ref[m, k].astype(jnp.float32)
+        rows_in[...] = rows_f32[...].astype(rows_in.dtype)
 
     for k in range(group):
         rows = slice(k * tile, (k + 1) * tile)
@@ -153,33 +299,38 @@
         out[rows] = jnp.maximum(total + bias[...], 0.0).astype(out.dtype)
 
 
-def layer(meta, pieces, rows_in, edge, sparse, bias, group=2):
+def layer(meta, pieces, listed, edge, sparse, bias, group=2):
     blocks, tiles_per, tile, _ = edge.shape
     stripes, _, width = pieces[0].shape
+    lines = sparse.shape[1]
     return pl.pallas_call(
         functools.partial(layer_kernel, group),
         out_shape=jax.ShapeDtypeStruct((blocks * tile, width), jnp.bfloat16),
         grid_spec=pltpu.PrefetchScalarGridSpec(
             num_scalar_prefetch=1,
             grid=(blocks // group,),
-            in_specs=[VMEM] * (len(pieces) + 1)
+            in_specs=[VMEM] * (len(pieces) + len(listed))
             + [
                 pl.BlockSpec((group, tiles_per, tile, tile), lambda b, m: (b, 0, 0, 0)),
-                pl.BlockSpec((group * tile, sparse.shape[1]), lambda b, m: (b, 0)),
+                pl.BlockSpec((group * tile, lines), lambda b, m: (b, 0)),
                 VMEM,
             ],
             out_specs=pl.BlockSpec((group * tile, width), lambda b, m: (b, 0)),
-            scratch_shapes=[pltpu.VMEM((stripes, tile, width), jnp.bfloat16)],
+            scratch_shapes=[
+                pltpu.VMEM((stripes, tile, width), jnp.bfloat16),
+                pltpu.VMEM((lines, width), jnp.float32),
+                pltpu.VMEM((lines, width), jnp.bfloat16),
+            ],
         ),
         compiler_params=params(24),
         cost_estimate=pl.CostEstimate(
-            flops=2 * blocks * tile * width * (tiles_per * tile + sparse.shape[1]),
+            flops=2 * blocks * tile * width * (tiles_per * tile + lines),
             bytes_accessed=2 * (edge.size + sparse.size + blocks * tile * width),
             transcendentals=0,
         ),
     )(
         meta,
-        *[held_in_vmem(x) for x in (*pieces, rows_in)],
+        *[held_in_vmem(x) for x in (*pieces, *listed)],
         pltpu.with_memory_space_constraint(edge, pltpu.HBM),
         pltpu.with_memory_space_constraint(sparse, pltpu.HBM),
         held_in_vmem(bias),
@@ -205,30 +356,46 @@
     def scattered(slots):
         return pick(ids, exchange(send_layout(slots, ids, blocks, devices)), block_count)
 
-    sent = send_layout(SLOTS, ids, blocks, devices)
-    features, sent = lax.optimization_barrier((features, sent))
-    got = exchange(sent)
-    outgoing = listed_rows(sparse_rows[0], sparse_counts[0], features, weight)
-    got, outgoing = lax.optimization_barrier((got, outgoing))
-
-    owner = ids // block_count
-    load = jnp.max(jnp.sum((owner[:, None] == owner[None, :]).astype(jnp.int32), axis=1))
+    keep, give = halves(ids, blocks, devices)
+    sent = merge(ids, keep, swap(give, 1), block_count)
+    near = [sent[0]] + [swap(x, 2 * m) for m, x in enumerate(sent) if m > 0]
+
+    features, _ = lax.optimization_barrier((features, sent[0]))
+    for_own, for_pair = listed_rows(sparse_rows[0], sparse_counts[0], features, weight)
+    near[1], for_pair = lax.optimization_barrier((near[1], for_pair))
+    from_pair = swap(for_pair, 1)
+
+    over = sort(ids, near, block_count)
+    arrived = [over[0]] + [swap(x, PLANE * g) for g, x in enumerate(over) if g > 0]
+
+    from_pair, _ = lax.optimization_barrier((from_pair, over[0]))
+    listed = [jnp.stack([for_own[m], from_pair[m]]) for m in range(PLANE // 2)]
+    listed = [swap(x, 2 * m) if m else x for m, x in enumerate(listed)]
+
+    arrived[1], *listed = lax.optimization_barrier((arrived[1], *listed))
+
+    def load(unit):
+        at = ids // unit
+        return jnp.max(jnp.sum((at[:, None] == at[None, :]).astype(jnp.int32), axis=1))
+
+    full = (load(2 * block_count) > SLOTS) | (load(PLANE * block_count) > PLANE_SLOTS)
     most = min(stripe_count, block_count)
     held = lax.cond(
-        load > SLOTS,
+        full,
         lambda x: pick(ids, exchange(send_layout(most, ids, blocks, devices)), weight, block_count),
         lambda x: x,
-        pick(ids, got, weight, block_count),
+        choose(ids, arrived, weight, block_count),
     )
 
     parts = [held] + [swap(held, PLANE * g) for g in range(1, groups)]
     ordered = [lax.select_n(group, *[parts[q ^ g] for g in range(groups)]) for q in range(groups)]
     own = jnp.concatenate(ordered, axis=1)
 
-    own, outgoing = lax.optimization_barrier((own, outgoing))
+    own, *listed = lax.optimization_barrier((own, *listed))
     x, y = swap(own, 4), swap(own, 2)
+    listed = [jnp.stack([r[:, g] for r in listed]) for g in range(groups)]
+    listed = [swap(r, PLANE * g) if g else r for g, r in enumerate(listed)]
     half = width // 2
-    rows_in = exchange(outgoing.reshape(devices, -1, width)).reshape(-1, width)
     left, right = swap(x[:, :, :half], 2), swap(y[:, :, half:], 4)
     pieces = [own, swap(own, 1), y, swap(y, 1), x, swap(x, 1)]
     pieces += [left, swap(left, 1), right, swap(right, 1)]
@@ -236,7 +403,7 @@
     meta = jnp.concatenate(
         [cols.reshape(-1), place ^ jnp.arange(PLANE, dtype=jnp.int32)]
     ).astype(jnp.int32)
-    return layer(meta, pieces, rows_in, edge, sparse_w, bias.reshape(1, -1))
+    return layer(meta, pieces, listed, edge, sparse_w, bias.reshape(1, -1))
 
 
 def solution(mesh):

time: 74.9 us -> 68.6 us (0.916)
  waiting for transfers between devices: 37.8 us -> 21.1 us
  starting transfers between devices: 17.9 us -> 27.5 us
  Pallas kernels: 16.6 us -> 15.8 us
    ppermute x12 -> x26, starting transfers between devices: 6.82 us -> 27.5 us  [swap(): return lax.ppermute(x, AXES, [(d, d ^ mask) for d in range(devices)])]
    all_to_all x2 -> x0, waiting for transfers between devices: 14.5 us -> none  [exchange(): return lax.all_to_all(x, AXES, 0, 0, tiled=True)]
    all_to_all x2 -> x0, starting transfers between devices: 11 us -> none  [exchange(): return lax.all_to_all(x, AXES, 0, 0, tiled=True)]
    ppermute x12 -> x26, waiting for transfers between devices: 23.3 us -> 21.1 us  [swap(): return lax.ppermute(x, AXES, [(d, d ^ mask) for d in range(devices)])]
    pallas_call x3 -> x5, Pallas kernels: 8.41 us -> 7.53 us  [the longest x1 2.71 us: halves(): pl.pallas_call(halves_kernel, out_shape=[shape, shape], in_specs=[SMEM, H...]
  transfers between devices with their start and end apart: 14 -> 26, of which waited for: 8 -> 15; matrix products, arithmetic and copies ran while one was open for 2% -> 3% of each run, Pallas kernels for 6% -> 5%
where the time goes in v3:
time: 68.6 us; the launch traced here: 68 us
  starting transfers between devices  27.5 us (40%)
  waiting for transfers between devices  21.1 us (31%)
  Pallas kernels  15.8 us (23%)
  other arithmetic  1.75 us (3%)
  between operations  1.47 us (2%)
    ppermute x26, starting transfers between devices, swap(): return lax.ppermute(x, AXES, [(d, d ^ mask) for d in range(devices)])  27.5 us
    ppermute x26, waiting for transfers between devices, swap(): return lax.ppermute(x, AXES, [(d, d ^ mask) for d in range(devices)])  21.1 us
    pallas_call x1, Pallas kernels, layer(): pl.pallas_call(functools.partial(layer_kernel, group), out_shape=jax.Shap...  8.28 us
    pallas_call x1, Pallas kernels, halves(): pl.pallas_call(halves_kernel, out_shape=[shape, shape], in_specs=[SMEM, H...  2.71 us
    pallas_call x1, Pallas kernels, listed_rows(): pl.pallas_call(rows_kernel, out_shape=[shape, shape], in_specs=[VMEM] * 4...  1.96 us
  transfers between devices with their start and end apart: 26, of which 15 were waited for; matrix products, arithmetic and copies ran while one was open for 3% of the time, Pallas kernels for 5%

profile of v3, /device:TPU:0, one launch (start us, length us, event | category | flops | bytes accessed | tf_op | source)
XLA Modules:
  0.0 68.0 jit_solution(11116123142911985727)
XLA Ops:
  0.0 2.7 %shard_map.91 = (bf16[4,3,4,8,768]{4,3,2,1,0:T(8,128)(2,1)S(1)}, bf16[4,3,4,8,768]{4,3,2,1,0:T(8,128)(2,1)S(1)}) custom-call(s32[8]{0:T(128)} %ids.7, bf16[8,4,2,4,8,768]{5,4,3,2,1,0:T(8,128)(2,1)} %bitcast.38), custom_call_target="tpu_custom_call" | custom-call | tf_op jit(solution)/shard_map/pallas_call | solution.py:67
  2.7 0.5 collective-permute-start
  3.3 1.6 %collective-permute-done.got = bf16[4,3,4,8,768]{4,3,2,1,0:T(8,128)(2,1)S(1)} collective-permute-done((bf16[4,3,4,8,768]{4,3,2,1,0:T(8,128)(2,1)S(1)}, bf16[4,3,4,8,768]{4,3,2,1,0:T(8,128)(2,1)S(1)}, u32[]{:S(2)}, u32[]{:S(2)}) %collective-permute-start) | collective-permute-done | bytes 589856 | tf_op jit(solution)/shard_map/ppermute | solution.py:354
  4.9 0.7 %shard_map.92 = (bf16[3,4,8,768]{3,2,1,0:T(8,128)(2,1)S(1)}, bf16[3,4,8,768]{3,2,1,0:T(8,128)(2,1)S(1)}, bf16[3,4,8,768]{3,2,1,0:T(8,128)(2,1)S(1)}, bf16[3,4,8,768]{3,2,1,0:T(8,128)(2,1)S(1)}) custom-call(s32[8]{0:T(128)S(1)} %copy-done.4, bf16[4,3,4,8,768]{4,3,2,1,0:T(8,128)(2,1)S(1)} %get-tuple-element.44.keep, ...), custom_call_target="tpu_custom_call" | custom-call | tf_op jit(solution)/shard_map/pallas_call | solution.py:98
  5.6 3.0 %collective-permute-start.1 = (bf16[3,4,8,768]{3,2,1,0:T(8,128)(2,1)S(1)}, bf16[3,4,8,768]{3,2,1,0:T(8,128)(2,1)S(1)}, u32[]{:S(2)}, u32[]{:S(2)}) collective-permute-start(bf16[3,4,8,768]{3,2,1,0:T(8,128)(2,1)S(1)} %get-tuple-element.47), channel_id=1, source_target_pairs={{0,2},{1,3},{2,0},{3,1},{4,6},{5,7},{6,4},{7,5},{8,10},{9,11},{10,... | collective-permute-start | bytes 442376 | tf_op jit(solution)/shard_map/ppermute | solution.py:354
  8.6 1.5 %collective-permute-start.2 = (bf16[3,4,8,768]{3,2,1,0:T(8,128)(2,1)S(1)}, bf16[3,4,8,768]{3,2,1,0:T(8,128)(2,1)S(1)}, u32[]{:S(2)}, u32[]{:S(2)}) collective-permute-start(bf16[3,4,8,768]{3,2,1,0:T(8,128)(2,1)S(1)} %get-tuple-element.51), channel_id=1, source_target_pairs={{0,4},{1,5},{2,6},{3,7},{4,0},{5,1},{6,2},{7,3},{8,12},{9,13},{10,... | collective-permute-start | bytes 442376 | tf_op jit(solution)/shard_map/ppermute | solution.py:354
  10.1 0.0 collective-permute-start.3
  10.1 2.0 %shard_map.93 = (bf16[4,4,8,768]{3,2,1,0:T(8,128)(2,1)S(1)}, bf16[4,4,8,768]{3,2,1,0:T(8,128)(2,1)S(1)}) custom-call(s32[8,32]{1,0:T(8,128)S(1)} %bitcast.37, s32[1,32]{1,0:T(1,128)S(1)} %copy-done.2, bf16[2048,768]{1,0:T(8,128)(2,1)S(1)} %copy-done.3, bf16[768,768]{1,0:T(8,128)(2,1)S(1)} %copy-done), custom_call_target="tpu_custom_call" | custom-call | tf_op jit(solution)/shard_map/pallas_call | solution.py:234
  12.1 0.6 collective-permute-done.1.refs_1_
  12.7 0.1 collective-permute-start.5
  12.8 0.2 convert_reduce_fusion
  13.0 0.6 reduce_max.18
  13.7 0.6 reduce_max.19
  15.5 0.0 collective-permute-done.2.refs_2_
  15.5 1.6 %collective-permute-done.3.refs_3_ = bf16[3,4,8,768]{3,2,1,0:T(8,128)(2,1)S(1)} collective-permute-done((bf16[3,4,8,768]{3,2,1,0:T(8,128)(2,1)S(1)}, bf16[3,4,8,768]{3,2,1,0:T(8,128)(2,1)S(1)}, u32[]{:S(2)}, u32[]{:S(2)}) %collective-permute-start.3) | collective-permute-done | bytes 147488 | tf_op jit(solution)/shard_map/ppermute | solution.py:354
  17.1 1.2 %shard_map.94 = (bf16[5,8,768]{2,1,0:T(8,128)(2,1)S(1)}, bf16[5,8,768]{2,1,0:T(8,128)(2,1)S(1)}, bf16[5,8,768]{2,1,0:T(8,128)(2,1)S(1)}, bf16[5,8,768]{2,1,0:T(8,128)(2,1)S(1)}) custom-call(s32[8]{0:T(128)S(1)} %copy-done.4, bf16[3,4,8,768]{3,2,1,0:T(8,128)(2,1)S(1)} %get-tuple-element.46.refs_0_, bf16[3,4,8,768]{3,2,1,0:T(8,128)(2,1)S(1)} %collective-permute-done.1.refs_1_, ...), custom_call_target="tpu_custom_call" | custom-call | tf_op jit(solution)/shard_map/pallas_call | solution.py:126
  18.4 1.8 %collective-permute-start.4 = (bf16[5,8,768]{2,1,0:T(8,128)(2,1)S(1)}, bf16[5,8,768]{2,1,0:T(8,128)(2,1)S(1)}, u32[]{:S(2)}, u32[]{:S(2)}) collective-permute-start(bf16[5,8,768]{2,1,0:T(8,128)(2,1)S(1)} %get-tuple-element.54), channel_id=1, source_target_pairs={{0,8},{1,9},{2,10},{3,11},{4,12},{5,13},{6,14},{7,15},{8,0},{9,1},... | collective-permute-start | bytes 184328 | tf_op jit(solution)/shard_map/ppermute | solution.py:354
  20.1 2.5 %collective-permute-start.10 = (bf16[5,8,768]{2,1,0:T(8,128)(2,1)S(1)}, bf16[5,8,768]{2,1,0:T(8,128)(2,1)S(1)}, u32[]{:S(2)}, u32[]{:S(2)}) collective-permute-start(bf16[5,8,768]{2,1,0:T(8,128)(2,1)S(1)} %get-tuple-element.60), channel_id=1, source_target_pairs={{0,24},{1,25},{2,26},{3,27},{4,28},{5,29},{6,30},{7,31},{8,16},{9,... | collective-permute-start | bytes 184328 | tf_op jit(solution)/shard_map/ppermute | solution.py:354
  22.6 0.1 collective-permute-start.9
  22.7 0.0 collective-permute-done.5
  22.8 2.5 %collective-permute-start.8 = (bf16[2,4,8,768]{3,2,0,1:T(8,128)(2,1)S(1)}, bf16[2,4,8,768]{3,2,0,1:T(8,128)(2,1)S(1)}, u32[]{:S(2)}, u32[]{:S(2)}) collective-permute-start(bf16[2,4,8,768]{3,2,0,1:T(8,128)(2,1)S(1)} %pad_maximum_fusion.4), channel_id=1, source_target_pairs={{0,6},{1,7},{2,4},{3,5},{4,2},{5,3},{6,0},{7,1},{8,14},{9,15},{10,... | collective-permute-start | bytes 294920 | tf_op jit(solution)/shard_map/ppermute | solution.py:354
  25.3 0.6 collective-permute-start.7
  25.9 0.0 collective-permute-done.4.refs_1_
  25.9 0.6 collective-permute-start.6
  26.5 2.0 %collective-permute-done.8 = bf16[2,4,8,768]{3,2,0,1:T(8,128)(2,1)S(1)} collective-permute-done((bf16[2,4,8,768]{3,2,0,1:T(8,128)(2,1)S(1)}, bf16[2,4,8,768]{3,2,0,1:T(8,128)(2,1)S(1)}, u32[]{:S(2)}, u32[]{:S(2)}) %collective-permute-start.8) | collective-permute-done | bytes 98336 | tf_op jit(solution)/shard_map/ppermute | solution.py:354
  28.5 1.5 %collective-permute-done.7 = bf16[2,4,8,768]{3,2,0,1:T(8,128)(2,1)S(1)} collective-permute-done((bf16[2,4,8,768]{3,2,0,1:T(8,128)(2,1)S(1)}, bf16[2,4,8,768]{3,2,0,1:T(8,128)(2,1)S(1)}, u32[]{:S(2)}, u32[]{:S(2)}) %collective-permute-start.7) | collective-permute-done | bytes 98336 | tf_op jit(solution)/shard_map/ppermute | solution.py:354
  30.0 0.6 collective-permute-done.6
  30.6 0.0 collective-permute-done.10.refs_3_
  30.6 0.0 collective-permute-done.9.refs_2_
  30.6 0.9 %shard_map.95 = bf16[8,8,768]{2,1,0:T(8,128)(2,1)S(1)} custom-call(s32[8]{0:T(128)S(1)} %copy-done.4, bf16[5,8,768]{2,1,0:T(8,128)(2,1)S(1)} %get-tuple-element.53.refs_0_, bf16[5,8,768]{2,1,0:T(8,128)(2,1)S(1)} %collective-permute-done.4.refs_1_, bf16[5,8,768]{2,1,0:T(8,128)(2,1)S(1)} %collective-permute-done.9.refs_2_, ...), custom_call_target="tpu_custom_call" | custom-call | tf_op jit(solution)/shard_map/pallas_call | solution.py:152
  31.6 0.0 copy-start.6
  31.6 0.0 copy-start.5
  31.6 1.9 %collective-permute-start.11 = (bf16[8,8,768]{2,1,0:T(8,128)(2,1)S(1)}, bf16[8,8,768]{2,1,0:T(8,128)(2,1)S(1)}, u32[]{:S(2)}, u32[]{:S(2)}) collective-permute-start(bf16[8,8,768]{2,1,0:T(8,128)(2,1)S(1)} %get-tuple-element.106), channel_id=1, source_target_pairs={{0,8},{1,9},{2,10},{3,11},{4,12},{5,13},{6,14},{7,15},{8,0},{9,1},... | collective-permute-start | bytes 294920 | tf_op jit(solution)/shard_map/ppermute | solution.py:354
  33.5 1.7 %collective-permute-start.12 = (bf16[8,8,768]{2,1,0:T(8,128)(2,1)S(1)}, bf16[8,8,768]{2,1,0:T(8,128)(2,1)S(1)}, u32[]{:S(2)}, u32[]{:S(2)}) collective-permute-start(bf16[8,8,768]{2,1,0:T(8,128)(2,1)S(1)} %get-tuple-element.106), channel_id=1, source_target_pairs={{0,16},{1,17},{2,18},{3,19},{4,20},{5,21},{6,22},{7,23},{8,24},{9,... | collective-permute-start | bytes 294920 | tf_op jit(solution)/shard_map/ppermute | solution.py:354
  35.1 0.9 %collective-permute-start.13 = (bf16[8,8,768]{2,1,0:T(8,128)(2,1)S(1)}, bf16[8,8,768]{2,1,0:T(8,128)(2,1)S(1)}, u32[]{:S(2)}, u32[]{:S(2)}) collective-permute-start(bf16[8,8,768]{2,1,0:T(8,128)(2,1)S(1)} %get-tuple-element.106), channel_id=1, source_target_pairs={{0,24},{1,25},{2,26},{3,27},{4,28},{5,29},{6,30},{7,31},{8,16},{9,... | collective-permute-start | bytes 294920 | tf_op jit(solution)/shard_map/ppermute | solution.py:354
  36.0 1.3 %collective-permute-done.11 = bf16[8,8,768]{2,1,0:T(8,128)(2,1)S(1)} collective-permute-done((bf16[8,8,768]{2,1,0:T(8,128)(2,1)S(1)}, bf16[8,8,768]{2,1,0:T(8,128)(2,1)S(1)}, u32[]{:S(2)}, u32[]{:S(2)}) %collective-permute-start.11) | collective-permute-done | bytes 98336 | tf_op jit(solution)/shard_map/ppermute | solution.py:354
  37.3 2.7 %collective-permute-done.12 = bf16[8,8,768]{2,1,0:T(8,128)(2,1)S(1)} collective-permute-done((bf16[8,8,768]{2,1,0:T(8,128)(2,1)S(1)}, bf16[8,8,768]{2,1,0:T(8,128)(2,1)S(1)}, u32[]{:S(2)}, u32[]{:S(2)}) %collective-permute-start.12) | collective-permute-done | bytes 98336 | tf_op jit(solution)/shard_map/ppermute | solution.py:354
  40.0 1.6 %collective-permute-done.13 = bf16[8,8,768]{2,1,0:T(8,128)(2,1)S(1)} collective-permute-done((bf16[8,8,768]{2,1,0:T(8,128)(2,1)S(1)}, bf16[8,8,768]{2,1,0:T(8,128)(2,1)S(1)}, u32[]{:S(2)}, u32[]{:S(2)}) %collective-permute-start.13) | collective-permute-done | bytes 98336 | tf_op jit(solution)/shard_map/ppermute | solution.py:354
  41.8 1.6 %collective-permute-start.17 = (bf16[8,32,768]{2,1,0:T(8,128)(2,1)S(1)}, bf16[8,32,768]{2,1,0:T(8,128)(2,1)S(1)}, u32[]{:S(2)}, u32[]{:S(2)}) collective-permute-start(bf16[8,32,768]{2,1,0:T(8,128)(2,1)S(1)} %pad_maximum_fusion.refs_0_), channel_id=1, source_target_pairs={{0,4},{1,5},{2,6},{3,7},{4,0},{5,1},{6,2},{7,3},{8,12},{9,13},{10,... | collective-permute-start | bytes 1179656 | tf_op jit(solution)/shard_map/ppermute | solution.py:354
  43.3 0.5 collective-permute-start.15
  43.9 2.0 %collective-permute-start.25 = (bf16[4,2,8,768]{3,2,1,0:T(8,128)(2,1)S(1)}, bf16[4,2,8,768]{3,2,1,0:T(8,128)(2,1)S(1)}, u32[]{:S(2)}, u32[]{:S(2)}) collective-permute-start(bf16[4,2,8,768]{3,2,1,0:T(8,128)(2,1)S(1)} %pad_maximum_fusion.8), channel_id=1, source_target_pairs={{0,24},{1,25},{2,26},{3,27},{4,28},{5,29},{6,30},{7,31},{8,16},{9,... | collective-permute-start | bytes 294920 | tf_op jit(solution)/shard_map/ppermute | solution.py:354
  45.9 2.9 %collective-permute-start.24 = (bf16[4,2,8,768]{3,2,1,0:T(8,128)(2,1)S(1)}, bf16[4,2,8,768]{3,2,1,0:T(8,128)(2,1)S(1)}, u32[]{:S(2)}, u32[]{:S(2)}) collective-permute-start(bf16[4,2,8,768]{3,2,1,0:T(8,128)(2,1)S(1)} %pad_maximum_fusion.7), channel_id=1, source_target_pairs={{0,16},{1,17},{2,18},{3,19},{4,20},{5,21},{6,22},{7,23},{8,24},{9,... | collective-permute-start | bytes 294920 | tf_op jit(solution)/shard_map/ppermute | solution.py:354
  48.8 0.6 collective-permute-start.23
  49.4 2.3 %collective-permute-done.17.refs_4_ = bf16[8,32,768]{2,1,0:T(8,128)(2,1)S(1)} collective-permute-done((bf16[8,32,768]{2,1,0:T(8,128)(2,1)S(1)}, bf16[8,32,768]{2,1,0:T(8,128)(2,1)S(1)}, u32[]{:S(2)}, u32[]{:S(2)}) %collective-permute-start.17) | collective-permute-done | bytes 393248 | tf_op jit(solution)/shard_map/ppermute | solution.py:354
  51.7 0.5 collective-permute-start.19
  52.2 0.3 collective-permute-done.15.refs_2_
  52.5 1.3 %collective-permute-start.21 = (bf16[8,32,384]{2,1,0:T(8,128)(2,1)S(1)}, bf16[8,32,384]{2,1,0:T(8,128)(2,1)S(1)}, u32[]{:S(2)}, u32[]{:S(2)}) collective-permute-start(bf16[8,32,384]{2,1,0:T(8,128)(2,1)S(1)} %slice.109), channel_id=1, source_target_pairs={{0,4},{1,5},{2,6},{3,7},{4,0},{5,1},{6,2},{7,3},{8,12},{9,13},{10,... | collective-permute-start | bytes 589832 | tf_op jit(solution)/shard_map/ppermute | solution.py:354
  53.8 0.0 collective-permute-done.25.refs_13_
  53.8 0.0 collective-permute-start.14
  53.8 0.0 collective-permute-done.24.refs_12_
  53.8 0.5 collective-permute-start.16
  54.3 0.0 collective-permute-done.23.refs_11_
  54.3 0.1 collective-permute-start.18
  54.4 0.1 copy.22
  54.5 0.1 reshape.10
  54.6 2.9 %collective-permute-done.19.refs_6_ = bf16[8,32,384]{2,1,0:T(8,128)(2,1)S(1)} collective-permute-done((bf16[8,32,384]{2,1,0:T(8,128)(2,1)S(1)}, bf16[8,32,384]{2,1,0:T(8,128)(2,1)S(1)}, u32[]{:S(2)}, u32[]{:S(2)}) %collective-permute-start.19) | collective-permute-done | bytes 196640 | tf_op jit(solution)/shard_map/ppermute | solution.py:354
  57.5 0.0 collective-permute-start.20
  57.5 0.8 %collective-permute-done.21.refs_8_ = bf16[8,32,384]{2,1,0:T(8,128)(2,1)S(1)} collective-permute-done((bf16[8,32,384]{2,1,0:T(8,128)(2,1)S(1)}, bf16[8,32,384]{2,1,0:T(8,128)(2,1)S(1)}, u32[]{:S(2)}, u32[]{:S(2)}) %collective-permute-start.21) | collective-permute-done | bytes 196640 | tf_op jit(solution)/shard_map/ppermute | solution.py:354
  58.2 0.0 collective-permute-start.22
  58.2 0.1 pad_add_fusion.meta
  58.3 0.0 collective-permute-done.14.refs_1_
  58.4 0.5 collective-permute-done.20.refs_7_
  58.9 0.8 %collective-permute-done.22.refs_9_ = bf16[8,32,384]{2,1,0:T(8,128)(2,1)S(1)} collective-permute-done((bf16[8,32,384]{2,1,0:T(8,128)(2,1)S(1)}, bf16[8,32,384]{2,1,0:T(8,128)(2,1)S(1)}, u32[]{:S(2)}, u32[]{:S(2)}) %collective-permute-start.22) | collective-permute-done | bytes 196640 | tf_op jit(solution)/shard_map/ppermute | solution.py:354
  59.7 8.3 %shard_map.96 = bf16[2048,768]{1,0:T(8,128)(2,1)} custom-call(s32[40]{0:T(128)S(1)} %pad_add_fusion.meta, bf16[8,32,768]{2,1,0:T(8,128)(2,1)S(1)} %pad_maximum_fusion.refs_0_, bf16[8,32,768]{2,1,0:T(8,128)(2,1)S(1)} %collective-permute-done.14.refs_1_, bf16[8,32,768]{2,1,0:T(8,128)(2,1)S(1)} %collective-permute-done.15.refs_2_, ...), custom_call_target="tpu_custom_call" | custom-call | flops 4026531840 | bytes 8388608 | tf_op jit(solution)/shard_map/pallas_call | solution.py:306
  (36 shorter events, 0.4 us)
Async XLA Ops:
  0.0 10.1 %copy-start.3 = (bf16[2048,768]{1,0:T(8,128)(2,1)S(1)}, bf16[2048,768]{1,0:T(8,128)(2,1)}, u32[]{:S(2)}) copy-start(bf16[2048,768]{1,0:T(8,128)(2,1)} %features) | copy-start | bytes 9437188
  0.0 4.9 %copy-start.4 = (s32[8]{0:T(128)S(1)}, s32[8]{0:T(128)}, u32[]{:S(2)}) copy-start(s32[8]{0:T(128)} %ids.7) | copy-start | bytes 100
  0.0 10.1 %copy-start.1 = (s32[1,32,8]{1,2,0:T(8,128)S(1)}, s32[1,32,8]{1,2,0:T(8,128)}, u32[]{:S(2)}) copy-start(s32[1,32,8]{1,2,0:T(8,128)} %param.16) | copy-start | bytes 3076
  0.0 10.1 %copy-start.2 = (s32[1,32]{1,0:T(1,128)S(1)}, s32[1,32]{1,0:T(1,128)}, u32[]{:S(2)}) copy-start(s32[1,32]{1,0:T(1,128)} %counts.1) | copy-start | bytes 388
  0.0 10.1 %copy-start = (bf16[768,768]{1,0:T(8,128)(2,1)S(1)}, bf16[768,768]{1,0:T(8,128)(2,1)}, u32[]{:S(2)}) copy-start(bf16[768,768]{1,0:T(8,128)(2,1)} %refs_4_.1) | copy-start | bytes 3538948
  2.7 2.1 %collective-permute-start = (bf16[4,3,4,8,768]{4,3,2,1,0:T(8,128)(2,1)S(1)}, bf16[4,3,4,8,768]{4,3,2,1,0:T(8,128)(2,1)S(1)}, u32[]{:S(2)}, u32[]{:S(2)}) collective-permute-start(bf16[4,3,4,8,768]{4,3,2,1,0:T(8,128)(2,1)S(1)} %get-tuple-element.45), channel_id=1, source_target_pairs={{0,1},{1,0},{2,3},{3,2},{4,5},{5,4},{6,7},{7,6},{8,9},{9,8},{10,11... | collective-permute-start | bytes 1769480 | tf_op jit(solution)/shard_map/ppermute | solution.py:354
  5.6 7.1 %collective-permute-start.1 = (bf16[3,4,8,768]{3,2,1,0:T(8,128)(2,1)S(1)}, bf16[3,4,8,768]{3,2,1,0:T(8,128)(2,1)S(1)}, u32[]{:S(2)}, u32[]{:S(2)}) collective-permute-start(bf16[3,4,8,768]{3,2,1,0:T(8,128)(2,1)S(1)} %get-tuple-element.47), channel_id=1, source_target_pairs={{0,2},{1,3},{2,0},{3,1},{4,6},{5,7},{6,4},{7,5},{8,10},{9,11},{10,... | collective-permute-start | bytes 442376 | tf_op jit(solution)/shard_map/ppermute | solution.py:354
  8.6 7.0 %collective-permute-start.2 = (bf16[3,4,8,768]{3,2,1,0:T(8,128)(2,1)S(1)}, bf16[3,4,8,768]{3,2,1,0:T(8,128)(2,1)S(1)}, u32[]{:S(2)}, u32[]{:S(2)}) collective-permute-start(bf16[3,4,8,768]{3,2,1,0:T(8,128)(2,1)S(1)} %get-tuple-element.51), channel_id=1, source_target_pairs={{0,4},{1,5},{2,6},{3,7},{4,0},{5,1},{6,2},{7,3},{8,12},{9,13},{10,... | collective-permute-start | bytes 442376 | tf_op jit(solution)/shard_map/ppermute | solution.py:354
  10.1 7.1 %collective-permute-start.3 = (bf16[3,4,8,768]{3,2,1,0:T(8,128)(2,1)S(1)}, bf16[3,4,8,768]{3,2,1,0:T(8,128)(2,1)S(1)}, u32[]{:S(2)}, u32[]{:S(2)}) collective-permute-start(bf16[3,4,8,768]{3,2,1,0:T(8,128)(2,1)S(1)} %get-tuple-element.52), channel_id=1, source_target_pairs={{0,6},{1,7},{2,4},{3,5},{4,2},{5,3},{6,0},{7,1},{8,14},{9,15},{10,... | collective-permute-start | bytes 442376 | tf_op jit(solution)/shard_map/ppermute | solution.py:354
  12.7 10.0 %collective-permute-start.5 = (bf16[4,4,8,768]{3,2,0,1:T(8,128)(2,1)S(1)}, bf16[4,4,8,768]{3,2,0,1:T(8,128)(2,1)S(1)}, u32[]{:S(2)}, u32[]{:S(2)}) collective-permute-start(bf16[4,4,8,768]{3,2,0,1:T(8,128)(2,1)S(1)} %copy.24), channel_id=1, source_target_pairs={{0,1},{1,0},{2,3},{3,2},{4,5},{5,4},{6,7},{7,6},{8,9},{9,8},{10,11... | collective-permute-start | bytes 589832 | tf_op jit(solution)/shard_map/ppermute | solution.py:354
  18.4 7.6 %collective-permute-start.4 = (bf16[5,8,768]{2,1,0:T(8,128)(2,1)S(1)}, bf16[5,8,768]{2,1,0:T(8,128)(2,1)S(1)}, u32[]{:S(2)}, u32[]{:S(2)}) collective-permute-start(bf16[5,8,768]{2,1,0:T(8,128)(2,1)S(1)} %get-tuple-element.54), channel_id=1, source_target_pairs={{0,8},{1,9},{2,10},{3,11},{4,12},{5,13},{6,14},{7,15},{8,0},{9,1},... | collective-permute-start | bytes 184328 | tf_op jit(solution)/shard_map/ppermute | solution.py:354
  20.1 10.5 %collective-permute-start.10 = (bf16[5,8,768]{2,1,0:T(8,128)(2,1)S(1)}, bf16[5,8,768]{2,1,0:T(8,128)(2,1)S(1)}, u32[]{:S(2)}, u32[]{:S(2)}) collective-permute-start(bf16[5,8,768]{2,1,0:T(8,128)(2,1)S(1)} %get-tuple-element.60), channel_id=1, source_target_pairs={{0,24},{1,25},{2,26},{3,27},{4,28},{5,29},{6,30},{7,31},{8,16},{9,... | collective-permute-start | bytes 184328 | tf_op jit(solution)/shard_map/ppermute | solution.py:354
  22.6 8.0 %collective-permute-start.9 = (bf16[5,8,768]{2,1,0:T(8,128)(2,1)S(1)}, bf16[5,8,768]{2,1,0:T(8,128)(2,1)S(1)}, u32[]{:S(2)}, u32[]{:S(2)}) collective-permute-start(bf16[5,8,768]{2,1,0:T(8,128)(2,1)S(1)} %get-tuple-element.59), channel_id=1, source_target_pairs={{0,16},{1,17},{2,18},{3,19},{4,20},{5,21},{6,22},{7,23},{8,24},{9,... | collective-permute-start | bytes 184328 | tf_op jit(solution)/shard_map/ppermute | solution.py:354
  22.8 5.7 %collective-permute-start.8 = (bf16[2,4,8,768]{3,2,0,1:T(8,128)(2,1)S(1)}, bf16[2,4,8,768]{3,2,0,1:T(8,128)(2,1)S(1)}, u32[]{:S(2)}, u32[]{:S(2)}) collective-permute-start(bf16[2,4,8,768]{3,2,0,1:T(8,128)(2,1)S(1)} %pad_maximum_fusion.4), channel_id=1, source_target_pairs={{0,6},{1,7},{2,4},{3,5},{4,2},{5,3},{6,0},{7,1},{8,14},{9,15},{10,... | collective-permute-start | bytes 294920 | tf_op jit(solution)/shard_map/ppermute | solution.py:354
  25.3 4.7 %collective-permute-start.7 = (bf16[2,4,8,768]{3,2,0,1:T(8,128)(2,1)S(1)}, bf16[2,4,8,768]{3,2,0,1:T(8,128)(2,1)S(1)}, u32[]{:S(2)}, u32[]{:S(2)}) collective-permute-start(bf16[2,4,8,768]{3,2,0,1:T(8,128)(2,1)S(1)} %pad_maximum_fusion.3), channel_id=1, source_target_pairs={{0,4},{1,5},{2,6},{3,7},{4,0},{5,1},{6,2},{7,3},{8,12},{9,13},{10,... | collective-permute-start | bytes 294920 | tf_op jit(solution)/shard_map/ppermute | solution.py:354
  25.9 4.7 %collective-permute-start.6 = (bf16[2,4,8,768]{3,2,0,1:T(8,128)(2,1)S(1)}, bf16[2,4,8,768]{3,2,0,1:T(8,128)(2,1)S(1)}, u32[]{:S(2)}, u32[]{:S(2)}) collective-permute-start(bf16[2,4,8,768]{3,2,0,1:T(8,128)(2,1)S(1)} %pad_maximum_fusion.2), channel_id=1, source_target_pairs={{0,2},{1,3},{2,0},{3,1},{4,6},{5,7},{6,4},{7,5},{8,10},{9,11},{10,... | collective-permute-start | bytes 294920 | tf_op jit(solution)/shard_map/ppermute | solution.py:354
  31.6 22.8 %copy-start.6 = (s32[8,4]{0,1:T(4,128)S(1)}, s32[8,4]{0,1:T(4,128)}, u32[]{:S(2)}) copy-start(s32[8,4]{0,1:T(4,128)} %param.13) | copy-start | bytes 388
  31.6 23.0 %copy-start.5 = (f32[768]{0:T(1024)S(1)}, f32[768]{0:T(1024)}, u32[]{:S(2)}) copy-start(f32[768]{0:T(1024)} %param.19) | copy-start | bytes 9220
  31.6 5.7 %collective-permute-start.11 = (bf16[8,8,768]{2,1,0:T(8,128)(2,1)S(1)}, bf16[8,8,768]{2,1,0:T(8,128)(2,1)S(1)}, u32[]{:S(2)}, u32[]{:S(2)}) collective-permute-start(bf16[8,8,768]{2,1,0:T(8,128)(2,1)S(1)} %get-tuple-element.106), channel_id=1, source_target_pairs={{0,8},{1,9},{2,10},{3,11},{4,12},{5,13},{6,14},{7,15},{8,0},{9,1},... | collective-permute-start | bytes 294920 | tf_op jit(solution)/shard_map/ppermute | solution.py:354
  33.5 6.6 %collective-permute-start.12 = (bf16[8,8,768]{2,1,0:T(8,128)(2,1)S(1)}, bf16[8,8,768]{2,1,0:T(8,128)(2,1)S(1)}, u32[]{:S(2)}, u32[]{:S(2)}) collective-permute-start(bf16[8,8,768]{2,1,0:T(8,128)(2,1)S(1)} %get-tuple-element.106), channel_id=1, source_target_pairs={{0,16},{1,17},{2,18},{3,19},{4,20},{5,21},{6,22},{7,23},{8,24},{9,... | collective-permute-start | bytes 294920 | tf_op jit(solution)/shard_map/ppermute | solution.py:354
  35.1 6.5 %collective-permute-start.13 = (bf16[8,8,768]{2,1,0:T(8,128)(2,1)S(1)}, bf16[8,8,768]{2,1,0:T(8,128)(2,1)S(1)}, u32[]{:S(2)}, u32[]{:S(2)}) collective-permute-start(bf16[8,8,768]{2,1,0:T(8,128)(2,1)S(1)} %get-tuple-element.106), channel_id=1, source_target_pairs={{0,24},{1,25},{2,26},{3,27},{4,28},{5,29},{6,30},{7,31},{8,16},{9,... | collective-permute-start | bytes 294920 | tf_op jit(solution)/shard_map/ppermute | solution.py:354
  41.8 9.9 %collective-permute-start.17 = (bf16[8,32,768]{2,1,0:T(8,128)(2,1)S(1)}, bf16[8,32,768]{2,1,0:T(8,128)(2,1)S(1)}, u32[]{:S(2)}, u32[]{:S(2)}) collective-permute-start(bf16[8,32,768]{2,1,0:T(8,128)(2,1)S(1)} %pad_maximum_fusion.refs_0_), channel_id=1, source_target_pairs={{0,4},{1,5},{2,6},{3,7},{4,0},{5,1},{6,2},{7,3},{8,12},{9,13},{10,... | collective-permute-start | bytes 1179656 | tf_op jit(solution)/shard_map/ppermute | solution.py:354
  43.3 9.2 %collective-permute-start.15 = (bf16[8,32,768]{2,1,0:T(8,128)(2,1)S(1)}, bf16[8,32,768]{2,1,0:T(8,128)(2,1)S(1)}, u32[]{:S(2)}, u32[]{:S(2)}) collective-permute-start(bf16[8,32,768]{2,1,0:T(8,128)(2,1)S(1)} %pad_maximum_fusion.refs_0_), channel_id=1, source_target_pairs={{0,2},{1,3},{2,0},{3,1},{4,6},{5,7},{6,4},{7,5},{8,10},{9,11},{10,... | collective-permute-start | bytes 1179656 | tf_op jit(solution)/shard_map/ppermute | solution.py:354
  43.9 9.9 %collective-permute-start.25 = (bf16[4,2,8,768]{3,2,1,0:T(8,128)(2,1)S(1)}, bf16[4,2,8,768]{3,2,1,0:T(8,128)(2,1)S(1)}, u32[]{:S(2)}, u32[]{:S(2)}) collective-permute-start(bf16[4,2,8,768]{3,2,1,0:T(8,128)(2,1)S(1)} %pad_maximum_fusion.8), channel_id=1, source_target_pairs={{0,24},{1,25},{2,26},{3,27},{4,28},{5,29},{6,30},{7,31},{8,16},{9,... | collective-permute-start | bytes 294920 | tf_op jit(solution)/shard_map/ppermute | solution.py:354
  45.9 8.0 %collective-permute-start.24 = (bf16[4,2,8,768]{3,2,1,0:T(8,128)(2,1)S(1)}, bf16[4,2,8,768]{3,2,1,0:T(8,128)(2,1)S(1)}, u32[]{:S(2)}, u32[]{:S(2)}) collective-permute-start(bf16[4,2,8,768]{3,2,1,0:T(8,128)(2,1)S(1)} %pad_maximum_fusion.7), channel_id=1, source_target_pairs={{0,16},{1,17},{2,18},{3,19},{4,20},{5,21},{6,22},{7,23},{8,24},{9,... | collective-permute-start | bytes 294920 | tf_op jit(solution)/shard_map/ppermute | solution.py:354
  48.8 5.5 %collective-permute-start.23 = (bf16[4,2,8,768]{3,2,1,0:T(8,128)(2,1)S(1)}, bf16[4,2,8,768]{3,2,1,0:T(8,128)(2,1)S(1)}, u32[]{:S(2)}, u32[]{:S(2)}) collective-permute-start(bf16[4,2,8,768]{3,2,1,0:T(8,128)(2,1)S(1)} %pad_maximum_fusion.6), channel_id=1, source_target_pairs={{0,8},{1,9},{2,10},{3,11},{4,12},{5,13},{6,14},{7,15},{8,0},{9,1},... | collective-permute-start | bytes 294920 | tf_op jit(solution)/shard_map/ppermute | solution.py:354
  51.7 5.7 %collective-permute-start.19 = (bf16[8,32,384]{2,1,0:T(8,128)(2,1)S(1)}, bf16[8,32,384]{2,1,0:T(8,128)(2,1)S(1)}, u32[]{:S(2)}, u32[]{:S(2)}) collective-permute-start(bf16[8,32,384]{2,1,0:T(8,128)(2,1)S(1)} %slice.108), channel_id=1, source_target_pairs={{0,2},{1,3},{2,0},{3,1},{4,6},{5,7},{6,4},{7,5},{8,10},{9,11},{10,... | collective-permute-start | bytes 589832 | tf_op jit(solution)/shard_map/ppermute | solution.py:354
  52.5 5.7 %collective-permute-start.21 = (bf16[8,32,384]{2,1,0:T(8,128)(2,1)S(1)}, bf16[8,32,384]{2,1,0:T(8,128)(2,1)S(1)}, u32[]{:S(2)}, u32[]{:S(2)}) collective-permute-start(bf16[8,32,384]{2,1,0:T(8,128)(2,1)S(1)} %slice.109), channel_id=1, source_target_pairs={{0,4},{1,5},{2,6},{3,7},{4,0},{5,1},{6,2},{7,3},{8,12},{9,13},{10,... | collective-permute-start | bytes 589832 | tf_op jit(solution)/shard_map/ppermute | solution.py:354
  53.8 4.5 %collective-permute-start.14 = (bf16[8,32,768]{2,1,0:T(8,128)(2,1)S(1)}, bf16[8,32,768]{2,1,0:T(8,128)(2,1)S(1)}, u32[]{:S(2)}, u32[]{:S(2)}) collective-permute-start(bf16[8,32,768]{2,1,0:T(8,128)(2,1)S(1)} %pad_maximum_fusion.refs_0_), channel_id=1, source_target_pairs={{0,1},{1,0},{2,3},{3,2},{4,5},{5,4},{6,7},{7,6},{8,9},{9,8},{10,11... | collective-permute-start | bytes 1179656 | tf_op jit(solution)/shard_map/ppermute | solution.py:354
  53.8 4.5 %collective-permute-start.16 = (bf16[8,32,768]{2,1,0:T(8,128)(2,1)S(1)}, bf16[8,32,768]{2,1,0:T(8,128)(2,1)S(1)}, u32[]{:S(2)}, u32[]{:S(2)}) collective-permute-start(bf16[8,32,768]{2,1,0:T(8,128)(2,1)S(1)} %collective-permute-done.15.refs_2_), channel_id=1, source_target_pairs={{0,1},{1,0},{2,3},{3,2},{4,5},{5,4},{6,7},{7,6},{8,9},{9,8},{10,11... | collective-permute-start | bytes 1179656 | tf_op jit(solution)/shard_map/ppermute | solution.py:354
  54.3 4.0 %collective-permute-start.18 = (bf16[8,32,768]{2,1,0:T(8,128)(2,1)S(1)}, bf16[8,32,768]{2,1,0:T(8,128)(2,1)S(1)}, u32[]{:S(2)}, u32[]{:S(2)}) collective-permute-start(bf16[8,32,768]{2,1,0:T(8,128)(2,1)S(1)} %collective-permute-done.17.refs_4_), channel_id=1, source_target_pairs={{0,1},{1,0},{2,3},{3,2},{4,5},{5,4},{6,7},{7,6},{8,9},{9,8},{10,11... | collective-permute-start | bytes 1179656 | tf_op jit(solution)/shard_map/ppermute | solution.py:354
  57.5 1.4 %collective-permute-start.20 = (bf16[8,32,384]{2,1,0:T(8,128)(2,1)S(1)}, bf16[8,32,384]{2,1,0:T(8,128)(2,1)S(1)}, u32[]{:S(2)}, u32[]{:S(2)}) collective-permute-start(bf16[8,32,384]{2,1,0:T(8,128)(2,1)S(1)} %collective-permute-done.19.refs_6_), channel_id=1, source_target_pairs={{0,1},{1,0},{2,3},{3,2},{4,5},{5,4},{6,7},{7,6},{8,9},{9,8},{10,11... | collective-permute-start | bytes 589832 | tf_op jit(solution)/shard_map/ppermute | solution.py:354
  58.2 1.4 %collective-permute-start.22 = (bf16[8,32,384]{2,1,0:T(8,128)(2,1)S(1)}, bf16[8,32,384]{2,1,0:T(8,128)(2,1)S(1)}, u32[]{:S(2)}, u32[]{:S(2)}) collective-permute-start(bf16[8,32,384]{2,1,0:T(8,128)(2,1)S(1)} %collective-permute-done.21.refs_8_), channel_id=1, source_target_pairs={{0,1},{1,0},{2,3},{3,2},{4,5},{5,4},{6,7},{7,6},{8,9},{9,8},{10,11... | collective-permute-start | bytes 589832 | tf_op jit(solution)/shard_map/ppermute | solution.py:354

commit v4 on v3

--- a/solution.py
+++ b/solution.py
@@ -132,8 +132,8 @@
     )(ids, *[held_in_vmem(x) for x in near])
 
 
-def choose_kernel(count, ids, *refs):
-    arrived, weight, out = refs[:-2], refs[-2], refs[-1]
+def choose_kernel(count, ids, full, *refs):
+    arrived, (spare, weight, out) = refs[:-3], refs[-3:]
     group = lax.axis_index(AXES) // PLANE
     parts = []
     for j in range(ids.shape[0]):
@@ -145,17 +145,18 @@
         parts.append(part)
     rows = jnp.concatenate(parts).astype(jnp.bfloat16)
     result = jnp.dot(rows, weight[...], preferred_element_type=jnp.float32)
-    out[...] = result.reshape(out.shape).astype(out.dtype)
-
-
-def choose(ids, arrived, weight, count):
+    result = result.reshape(out.shape)
+    out[...] = jnp.where(full[0] > 0, spare[...].astype(jnp.float32), result).astype(out.dtype)
+
+
+def choose(ids, full, arrived, spare, weight, count):
     return pl.pallas_call(
         functools.partial(choose_kernel, count),
         out_shape=jax.ShapeDtypeStruct((ids.shape[0], *arrived[0].shape[1:]), arrived[0].dtype),
-        in_specs=[SMEM] + [VMEM] * (len(arrived) + 1),
+        in_specs=[SMEM, SMEM] + [VMEM] * (len(arrived) + 2),
         out_specs=VMEM,
         compiler_params=params(16),
-    )(ids, *[held_in_vmem(x) for x in arrived], held_in_vmem(weight))
+    )(ids, full, *[held_in_vmem(x) for x in (*arrived, spare, weight)])
 
 
 def send_kernel(ids, blocks, out, sems):
@@ -356,6 +357,19 @@
     def scattered(slots):
         return pick(ids, exchange(send_layout(slots, ids, blocks, devices)), block_count)
 
+    def load(unit):
+        at = ids // unit
+        return jnp.max(jnp.sum((at[:, None] == at[None, :]).astype(jnp.int32), axis=1))
+
+    full = (load(2 * block_count) > SLOTS) | (load(PLANE * block_count) > PLANE_SLOTS)
+    most = min(stripe_count, block_count)
+    spare = lax.cond(
+        full,
+        lambda: pick(ids, exchange(send_layout(most, ids, blocks, devices)), weight, block_count),
+        lambda: jnp.zeros((stripe_count, tile // devices, width), features.dtype),
+    )
+    full = full.astype(jnp.int32)[None]
+
     keep, give = halves(ids, blocks, devices)
     sent = merge(ids, keep, swap(give, 1), block_count)
     near = [sent[0]] + [swap(x, 2 * m) for m, x in enumerate(sent) if m > 0]
@@ -365,29 +379,22 @@
     near[1], for_pair = lax.optimization_barrier((near[1], for_pair))
     from_pair = swap(for_pair, 1)
 
+    near[2], spare = lax.optimization_barrier((near[2], spare))
     over = sort(ids, near, block_count)
     arrived = [over[0]] + [swap(x, PLANE * g) for g, x in enumerate(over) if g > 0]
 
     from_pair, _ = lax.optimization_barrier((from_pair, over[0]))
-    listed = [jnp.stack([for_own[m], from_pair[m]]) for m in range(PLANE // 2)]
-    listed = [swap(x, 2 * m) if m else x for m, x in enumerate(listed)]
-
-    arrived[1], *listed = lax.optimization_barrier((arrived[1], *listed))
-
-    def load(unit):
-        at = ids // unit
-        return jnp.max(jnp.sum((at[:, None] == at[None, :]).astype(jnp.int32), axis=1))
-
-    full = (load(2 * block_count) > SLOTS) | (load(PLANE * block_count) > PLANE_SLOTS)
-    most = min(stripe_count, block_count)
-    held = lax.cond(
-        full,
-        lambda x: pick(ids, exchange(send_layout(most, ids, blocks, devices)), weight, block_count),
-        lambda x: x,
-        choose(ids, arrived, weight, block_count),
-    )
+    both = jnp.stack([for_own, from_pair]).reshape(2, 2, 2, *for_own.shape[1:])
+    across = swap(both[:, 1], 4)
+
+    arrived[1], across = lax.optimization_barrier((arrived[1], across))
+
+    held = choose(ids, full, arrived, spare, weight, block_count)
 
     parts = [held] + [swap(held, PLANE * g) for g in range(1, groups)]
+    across, _ = lax.optimization_barrier((across, held))
+    turned = swap(jnp.stack([both[:, 0, 1], across[:, 1]]), 2)
+    listed = [both[:, 0, 0], turned[0], across[:, 0], turned[1]]
     ordered = [lax.select_n(group, *[parts[q ^ g] for g in range(groups)]) for q in range(groups)]
     own = jnp.concatenate(ordered, axis=1)
 

time: 68.6 us -> 67.8 us (0.988)
  waiting for transfers between devices: 21.1 us -> 20.1 us
    ppermute x26 -> x25, waiting for transfers between devices: 21.1 us -> 20.1 us  [swap(): return lax.ppermute(x, AXES, [(d, d ^ mask) for d in range(devices)])]
    ppermute x26 -> x25, starting transfers between devices: 27.5 us -> 28 us  [swap(): return lax.ppermute(x, AXES, [(d, d ^ mask) for d in range(devices)])]
  transfers between devices with their start and end apart: 26 -> 25, of which waited for: 15 -> 13; matrix products, arithmetic and copies ran while one was open for 3% -> 3% of each run, Pallas kernels for 5% -> 5%
where the time goes in v4:
time: 67.8 us; the launch traced here: 67.6 us
  starting transfers between devices  28 us (41%)
  waiting for transfers between devices  20.1 us (30%)
  Pallas kernels  15.8 us (23%)
  other arithmetic  1.84 us (3%)
  between operations  1.56 us (2%)
    ppermute x25, starting transfers between devices, swap(): return lax.ppermute(x, AXES, [(d, d ^ mask) for d in range(devices)])  28 us
    ppermute x25, waiting for transfers between devices, swap(): return lax.ppermute(x, AXES, [(d, d ^ mask) for d in range(devices)])  20.1 us
    pallas_call x1, Pallas kernels, layer(): pl.pallas_call(functools.partial(layer_kernel, group), out_shape=jax.Shap...  8.28 us
    pallas_call x1, Pallas kernels, halves(): pl.pallas_call(halves_kernel, out_shape=[shape, shape], in_specs=[SMEM, H...  2.71 us
    pallas_call x1, Pallas kernels, listed_rows(): pl.pallas_call(rows_kernel, out_shape=[shape, shape], in_specs=[VMEM] * 4...  1.94 us
  transfers between devices with their start and end apart: 25, of which 13 were waited for; matrix products, arithmetic and copies ran while one was open for 3% of the time, Pallas kernels for 5%

profile of v4, /device:TPU:0, one launch (start us, length us, event | category | flops | bytes accessed | tf_op | source)
XLA Modules:
  0.0 67.6 jit_solution(13131788454013941811)
XLA Ops:
  0.0 2.7 %shard_map.91 = (bf16[4,3,4,8,768]{4,3,2,1,0:T(8,128)(2,1)S(1)}, bf16[4,3,4,8,768]{4,3,2,1,0:T(8,128)(2,1)S(1)}) custom-call(s32[8]{0:T(128)} %ids.7, bf16[8,4,2,4,8,768]{5,4,3,2,1,0:T(8,128)(2,1)} %bitcast.57), custom_call_target="tpu_custom_call" | custom-call | tf_op jit(solution)/shard_map/pallas_call | solution.py:67
  2.7 0.5 collective-permute-start
  3.3 1.6 %collective-permute-done.got = bf16[4,3,4,8,768]{4,3,2,1,0:T(8,128)(2,1)S(1)} collective-permute-done((bf16[4,3,4,8,768]{4,3,2,1,0:T(8,128)(2,1)S(1)}, bf16[4,3,4,8,768]{4,3,2,1,0:T(8,128)(2,1)S(1)}, u32[]{:S(2)}, u32[]{:S(2)}) %collective-permute-start) | collective-permute-done | bytes 589856 | tf_op jit(solution)/shard_map/ppermute | solution.py:355
  4.9 0.0 copy-done.4
  4.9 0.7 %shard_map.92 = (bf16[3,4,8,768]{3,2,1,0:T(8,128)(2,1)S(1)}, bf16[3,4,8,768]{3,2,1,0:T(8,128)(2,1)S(1)}, bf16[3,4,8,768]{3,2,1,0:T(8,128)(2,1)S(1)}, bf16[3,4,8,768]{3,2,1,0:T(8,128)(2,1)S(1)}) custom-call(s32[8]{0:T(128)S(1)} %copy-done.4, bf16[4,3,4,8,768]{4,3,2,1,0:T(8,128)(2,1)S(1)} %get-tuple-element.43.keep, ...), custom_call_target="tpu_custom_call" | custom-call | tf_op jit(solution)/shard_map/pallas_call | solution.py:98
  5.6 3.0 %collective-permute-start.1 = (bf16[3,4,8,768]{3,2,1,0:T(8,128)(2,1)S(1)}, bf16[3,4,8,768]{3,2,1,0:T(8,128)(2,1)S(1)}, u32[]{:S(2)}, u32[]{:S(2)}) collective-permute-start(bf16[3,4,8,768]{3,2,1,0:T(8,128)(2,1)S(1)} %get-tuple-element.46), channel_id=1, source_target_pairs={{0,2},{1,3},{2,0},{3,1},{4,6},{5,7},{6,4},{7,5},{8,10},{9,11},{10,... | collective-permute-start | bytes 442376 | tf_op jit(solution)/shard_map/ppermute | solution.py:355
  8.6 1.5 %collective-permute-start.2 = (bf16[3,4,8,768]{3,2,1,0:T(8,128)(2,1)S(1)}, bf16[3,4,8,768]{3,2,1,0:T(8,128)(2,1)S(1)}, u32[]{:S(2)}, u32[]{:S(2)}) collective-permute-start(bf16[3,4,8,768]{3,2,1,0:T(8,128)(2,1)S(1)} %get-tuple-element.50), channel_id=1, source_target_pairs={{0,4},{1,5},{2,6},{3,7},{4,0},{5,1},{6,2},{7,3},{8,12},{9,13},{10,... | collective-permute-start | bytes 442376 | tf_op jit(solution)/shard_map/ppermute | solution.py:355
  10.1 0.0 collective-permute-start.3
  10.1 0.0 copy-done
  10.1 1.9 %shard_map.93 = (bf16[4,4,8,768]{3,2,1,0:T(8,128)(2,1)S(1)}, bf16[4,4,8,768]{3,2,1,0:T(8,128)(2,1)S(1)}) custom-call(s32[8,32]{1,0:T(8,128)S(1)} %bitcast.56, s32[1,32]{1,0:T(1,128)S(1)} %copy-done.2, bf16[2048,768]{1,0:T(8,128)(2,1)S(1)} %copy-done.3, bf16[768,768]{1,0:T(8,128)(2,1)S(1)} %copy-done), custom_call_target="tpu_custom_call" | custom-call | tf_op jit(solution)/shard_map/pallas_call | solution.py:235
  12.1 0.7 collective-permute-done.1.refs_1_
  12.7 0.0 collective-permute-start.5
  12.7 0.2 convert_reduce_fusion
  13.0 0.6 reduce_max.18
  13.6 0.7 %reduce_max.19 = s32[]{:T(128)} reduce(s32[8]{0:T(128)S(1)} %get-tuple-element.97, s32[]{:T(128)} %constant.67.clone.1), dimensions={0}, to_apply=%region_3.4 | reduce | flops 7 | bytes 40 | tf_op jit(solution)/shard_map/reduce_max | solution.py:362
  15.7 0.0 collective-permute-done.2.refs_2_
  15.7 1.5 %collective-permute-done.3.refs_3_ = bf16[3,4,8,768]{3,2,1,0:T(8,128)(2,1)S(1)} collective-permute-done((bf16[3,4,8,768]{3,2,1,0:T(8,128)(2,1)S(1)}, bf16[3,4,8,768]{3,2,1,0:T(8,128)(2,1)S(1)}, u32[]{:S(2)}, u32[]{:S(2)}) %collective-permute-start.3) | collective-permute-done | bytes 147488 | tf_op jit(solution)/shard_map/ppermute | solution.py:355
  17.1 1.2 %shard_map.94 = (bf16[5,8,768]{2,1,0:T(8,128)(2,1)S(1)}, bf16[5,8,768]{2,1,0:T(8,128)(2,1)S(1)}, bf16[5,8,768]{2,1,0:T(8,128)(2,1)S(1)}, bf16[5,8,768]{2,1,0:T(8,128)(2,1)S(1)}) custom-call(s32[8]{0:T(128)S(1)} %copy-done.4, bf16[3,4,8,768]{3,2,1,0:T(8,128)(2,1)S(1)} %get-tuple-element.45.refs_0_, bf16[3,4,8,768]{3,2,1,0:T(8,128)(2,1)S(1)} %collective-permute-done.1.refs_1_, ...), custom_call_target="tpu_custom_call" | custom-call | tf_op jit(solution)/shard_map/pallas_call | solution.py:126
  18.4 0.0 collective-permute-done.5
  18.4 1.7 %collective-permute-start.6 = (bf16[2,2,4,8,768]{4,3,0,2,1:T(8,128)(2,1)S(1)}, bf16[2,2,4,8,768]{4,3,0,2,1:T(8,128)(2,1)S(1)}, u32[]{:S(2)}, u32[]{:S(2)}) collective-permute-start(bf16[2,2,4,8,768]{4,3,0,2,1:T(8,128)(2,1)S(1)} %fusion.1), channel_id=1, source_target_pairs={{0,4},{1,5},{2,6},{3,7},{4,0},{5,1},{6,2},{7,3},{8,12},{9,13},{10,... | collective-permute-start | bytes 589832 | tf_op jit(solution)/shard_map/ppermute | solution.py:355
  20.1 1.6 %collective-permute-start.4 = (bf16[5,8,768]{2,1,0:T(8,128)(2,1)S(1)}, bf16[5,8,768]{2,1,0:T(8,128)(2,1)S(1)}, u32[]{:S(2)}, u32[]{:S(2)}) collective-permute-start(bf16[5,8,768]{2,1,0:T(8,128)(2,1)S(1)} %get-tuple-element.54), channel_id=1, source_target_pairs={{0,8},{1,9},{2,10},{3,11},{4,12},{5,13},{6,14},{7,15},{8,0},{9,1},... | collective-permute-start | bytes 184328 | tf_op jit(solution)/shard_map/ppermute | solution.py:355
  21.7 2.6 %collective-permute-start.7 = (bf16[5,8,768]{2,1,0:T(8,128)(2,1)S(1)}, bf16[5,8,768]{2,1,0:T(8,128)(2,1)S(1)}, u32[]{:S(2)}, u32[]{:S(2)}) collective-permute-start(bf16[5,8,768]{2,1,0:T(8,128)(2,1)S(1)} %get-tuple-element.59), channel_id=1, source_target_pairs={{0,16},{1,17},{2,18},{3,19},{4,20},{5,21},{6,22},{7,23},{8,24},{9,... | collective-permute-start | bytes 184328 | tf_op jit(solution)/shard_map/ppermute | solution.py:355
  24.3 0.2 collective-permute-start.8
  24.5 0.4 collective-permute-done.4.refs_1_
  24.9 0.0 collective-permute-done.6
  24.9 3.2 %collective-permute-done.7.refs_2_ = bf16[5,8,768]{2,1,0:T(8,128)(2,1)S(1)} collective-permute-done((bf16[5,8,768]{2,1,0:T(8,128)(2,1)S(1)}, bf16[5,8,768]{2,1,0:T(8,128)(2,1)S(1)}, u32[]{:S(2)}, u32[]{:S(2)}) %collective-permute-start.7) | collective-permute-done | bytes 61472 | tf_op jit(solution)/shard_map/ppermute | solution.py:355
  28.1 2.3 %collective-permute-done.8.refs_3_ = bf16[5,8,768]{2,1,0:T(8,128)(2,1)S(1)} collective-permute-done((bf16[5,8,768]{2,1,0:T(8,128)(2,1)S(1)}, bf16[5,8,768]{2,1,0:T(8,128)(2,1)S(1)}, u32[]{:S(2)}, u32[]{:S(2)}) %collective-permute-start.8) | collective-permute-done | bytes 61472 | tf_op jit(solution)/shard_map/ppermute | solution.py:355
  30.4 0.9 %shard_map.95 = bf16[8,8,768]{2,1,0:T(8,128)(2,1)S(1)} custom-call(s32[8]{0:T(128)S(1)} %copy-done.4, s32[1]{0:T(128)} %bitcast.1.full, bf16[5,8,768]{2,1,0:T(8,128)(2,1)S(1)} %get-tuple-element.53.refs_0_, bf16[5,8,768]{2,1,0:T(8,128)(2,1)S(1)} %collective-permute-done.4.refs_1_, bf16[5,8,768]{2,1,0:T(8,128)(2,1)S(1)} %collective-permute-done.7.refs_2_, ...), custom_call_target="tpu_custom_call" | custom-call | tf_op jit(solution)/shard_map/pallas_call | solution.py:153
  31.3 0.7 %collective-permute-start.11 = (bf16[8,8,768]{2,1,0:T(8,128)(2,1)S(1)}, bf16[8,8,768]{2,1,0:T(8,128)(2,1)S(1)}, u32[]{:S(2)}, u32[]{:S(2)}) collective-permute-start(bf16[8,8,768]{2,1,0:T(8,128)(2,1)S(1)} %shard_map.95), channel_id=1, source_target_pairs={{0,24},{1,25},{2,26},{3,27},{4,28},{5,29},{6,30},{7,31},{8,16},{9,... | collective-permute-start | bytes 294920 | tf_op jit(solution)/shard_map/ppermute | solution.py:355
  32.0 0.0 collective-permute-start.10
  32.0 3.7 %collective-permute-start.9 = (bf16[8,8,768]{2,1,0:T(8,128)(2,1)S(1)}, bf16[8,8,768]{2,1,0:T(8,128)(2,1)S(1)}, u32[]{:S(2)}, u32[]{:S(2)}) collective-permute-start(bf16[8,8,768]{2,1,0:T(8,128)(2,1)S(1)} %shard_map.95), channel_id=1, source_target_pairs={{0,8},{1,9},{2,10},{3,11},{4,12},{5,13},{6,14},{7,15},{8,0},{9,1},... | collective-permute-start | bytes 294920 | tf_op jit(solution)/shard_map/ppermute | solution.py:355
  35.8 1.6 %collective-permute-start.12 = (bf16[2,2,4,8,768]{4,3,1,2,0:T(8,128)(2,1)S(1)}, bf16[2,2,4,8,768]{4,3,1,2,0:T(8,128)(2,1)S(1)}, u32[]{:S(2)}, u32[]{:S(2)}) collective-permute-start(bf16[2,2,4,8,768]{4,3,1,2,0:T(8,128)(2,1)S(1)} %pad_maximum_fusion.1), channel_id=1, source_target_pairs={{0,2},{1,3},{2,0},{3,1},{4,6},{5,7},{6,4},{7,5},{8,10},{9,11},{10,... | collective-permute-start | bytes 589832 | tf_op jit(solution)/shard_map/ppermute | solution.py:355
  37.4 0.6 collective-permute-done.11
  38.0 2.4 %collective-permute-done.10 = bf16[8,8,768]{2,1,0:T(8,128)(2,1)S(1)} collective-permute-done((bf16[8,8,768]{2,1,0:T(8,128)(2,1)S(1)}, bf16[8,8,768]{2,1,0:T(8,128)(2,1)S(1)}, u32[]{:S(2)}, u32[]{:S(2)}) %collective-permute-start.10) | collective-permute-done | bytes 98336 | tf_op jit(solution)/shard_map/ppermute | solution.py:355
  40.3 0.0 collective-permute-done.9
  40.4 1.1 %collective-permute-done.12 = bf16[2,2,4,8,768]{4,3,1,2,0:T(8,128)(2,1)S(1)} collective-permute-done((bf16[2,2,4,8,768]{4,3,1,2,0:T(8,128)(2,1)S(1)}, bf16[2,2,4,8,768]{4,3,1,2,0:T(8,128)(2,1)S(1)}, u32[]{:S(2)}, u32[]{:S(2)}) %collective-permute-start.12) | collective-permute-done | bytes 196640 | tf_op jit(solution)/shard_map/ppermute | solution.py:355
  41.6 0.6 collective-permute-start.16
  42.2 1.5 %collective-permute-start.14 = (bf16[8,32,768]{2,1,0:T(8,128)(2,1)S(1)}, bf16[8,32,768]{2,1,0:T(8,128)(2,1)S(1)}, u32[]{:S(2)}, u32[]{:S(2)}) collective-permute-start(bf16[8,32,768]{2,1,0:T(8,128)(2,1)S(1)} %pad_maximum_fusion.refs_0_), channel_id=1, source_target_pairs={{0,2},{1,3},{2,0},{3,1},{4,6},{5,7},{6,4},{7,5},{8,10},{9,11},{10,... | collective-permute-start | bytes 1179656 | tf_op jit(solution)/shard_map/ppermute | solution.py:355
  43.8 0.4 collective-permute-start.22
  44.2 0.9 %collective-permute-start.23 = (bf16[4,2,8,768]{3,2,1,0:T(8,128)(2,1)S(1)}, bf16[4,2,8,768]{3,2,1,0:T(8,128)(2,1)S(1)}, u32[]{:S(2)}, u32[]{:S(2)}) collective-permute-start(bf16[4,2,8,768]{3,2,1,0:T(8,128)(2,1)S(1)} %pad_maximum_fusion.5), channel_id=1, source_target_pairs={{0,16},{1,17},{2,18},{3,19},{4,20},{5,21},{6,22},{7,23},{8,24},{9,... | collective-permute-start | bytes 294920 | tf_op jit(solution)/shard_map/ppermute | solution.py:355
  45.2 3.2 %collective-permute-start.24 = (bf16[4,2,8,768]{3,2,1,0:T(8,128)(2,1)S(1)}, bf16[4,2,8,768]{3,2,1,0:T(8,128)(2,1)S(1)}, u32[]{:S(2)}, u32[]{:S(2)}) collective-permute-start(bf16[4,2,8,768]{3,2,1,0:T(8,128)(2,1)S(1)} %pad_maximum_fusion.6), channel_id=1, source_target_pairs={{0,24},{1,25},{2,26},{3,27},{4,28},{5,29},{6,30},{7,31},{8,16},{9,... | collective-permute-start | bytes 294920 | tf_op jit(solution)/shard_map/ppermute | solution.py:355
  48.4 1.9 %collective-permute-done.16.refs_4_ = bf16[8,32,768]{2,1,0:T(8,128)(2,1)S(1)} collective-permute-done((bf16[8,32,768]{2,1,0:T(8,128)(2,1)S(1)}, bf16[8,32,768]{2,1,0:T(8,128)(2,1)S(1)}, u32[]{:S(2)}, u32[]{:S(2)}) %collective-permute-start.16) | collective-permute-done | bytes 393248 | tf_op jit(solution)/shard_map/ppermute | solution.py:355
  50.3 1.8 %collective-permute-start.18 = (bf16[8,32,384]{2,1,0:T(8,128)(2,1)S(1)}, bf16[8,32,384]{2,1,0:T(8,128)(2,1)S(1)}, u32[]{:S(2)}, u32[]{:S(2)}) collective-permute-start(bf16[8,32,384]{2,1,0:T(8,128)(2,1)S(1)} %slice.106), channel_id=1, source_target_pairs={{0,2},{1,3},{2,0},{3,1},{4,6},{5,7},{6,4},{7,5},{8,10},{9,11},{10,... | collective-permute-start | bytes 589832 | tf_op jit(solution)/shard_map/ppermute | solution.py:355
  52.1 0.0 collective-permute-done.14.refs_2_
  52.1 1.7 %collective-permute-start.20 = (bf16[8,32,384]{2,1,0:T(8,128)(2,1)S(1)}, bf16[8,32,384]{2,1,0:T(8,128)(2,1)S(1)}, u32[]{:S(2)}, u32[]{:S(2)}) collective-permute-start(bf16[8,32,384]{2,1,0:T(8,128)(2,1)S(1)} %slice.107), channel_id=1, source_target_pairs={{0,4},{1,5},{2,6},{3,7},{4,0},{5,1},{6,2},{7,3},{8,12},{9,13},{10,... | collective-permute-start | bytes 589832 | tf_op jit(solution)/shard_map/ppermute | solution.py:355
  53.9 0.0 collective-permute-done.22.refs_11_
  53.9 0.0 collective-permute-start.13
  53.9 0.0 collective-permute-done.23.refs_12_
  53.9 0.5 collective-permute-start.17
  54.4 0.0 collective-permute-done.24.refs_13_
  54.4 0.1 collective-permute-start.15
  54.5 0.1 copy.12
  54.6 0.1 reshape.15
  54.6 1.4 %collective-permute-done.18.refs_6_ = bf16[8,32,384]{2,1,0:T(8,128)(2,1)S(1)} collective-permute-done((bf16[8,32,384]{2,1,0:T(8,128)(2,1)S(1)}, bf16[8,32,384]{2,1,0:T(8,128)(2,1)S(1)}, u32[]{:S(2)}, u32[]{:S(2)}) %collective-permute-start.18) | collective-permute-done | bytes 196640 | tf_op jit(solution)/shard_map/ppermute | solution.py:355
  56.0 0.0 collective-permute-start.19
  56.1 1.8 %collective-permute-done.20.refs_8_ = bf16[8,32,384]{2,1,0:T(8,128)(2,1)S(1)} collective-permute-done((bf16[8,32,384]{2,1,0:T(8,128)(2,1)S(1)}, bf16[8,32,384]{2,1,0:T(8,128)(2,1)S(1)}, u32[]{:S(2)}, u32[]{:S(2)}) %collective-permute-start.20) | collective-permute-done | bytes 196640 | tf_op jit(solution)/shard_map/ppermute | solution.py:355
  57.9 0.0 collective-permute-start.21
  57.9 0.1 pad_add_fusion.meta
  58.0 0.0 collective-permute-done.13.refs_1_
  58.0 0.0 collective-permute-done.17.refs_5_
  58.0 0.0 collective-permute-done.15.refs_3_
  58.0 0.0 collective-permute-done.19.refs_7_
  58.0 1.3 %collective-permute-done.21.refs_9_ = bf16[8,32,384]{2,1,0:T(8,128)(2,1)S(1)} collective-permute-done((bf16[8,32,384]{2,1,0:T(8,128)(2,1)S(1)}, bf16[8,32,384]{2,1,0:T(8,128)(2,1)S(1)}, u32[]{:S(2)}, u32[]{:S(2)}) %collective-permute-start.21) | collective-permute-done | bytes 196640 | tf_op jit(solution)/shard_map/ppermute | solution.py:355
  59.3 8.3 %shard_map.96 = bf16[2048,768]{1,0:T(8,128)(2,1)} custom-call(s32[40]{0:T(128)S(1)} %pad_add_fusion.meta, bf16[8,32,768]{2,1,0:T(8,128)(2,1)S(1)} %pad_maximum_fusion.refs_0_, bf16[8,32,768]{2,1,0:T(8,128)(2,1)S(1)} %collective-permute-done.13.refs_1_, bf16[8,32,768]{2,1,0:T(8,128)(2,1)S(1)} %collective-permute-done.14.refs_2_, ...), custom_call_target="tpu_custom_call" | custom-call | flops 4026531840 | bytes 8388608 | tf_op jit(solution)/shard_map/pallas_call | solution.py:307
  (34 shorter events, 0.4 us)
Async XLA Ops:
  0.0 4.9 %copy-start.4 = (s32[8]{0:T(128)S(1)}, s32[8]{0:T(128)}, u32[]{:S(2)}) copy-start(s32[8]{0:T(128)} %ids.7) | copy-start | bytes 100
  0.0 10.1 %copy-start.3 = (bf16[2048,768]{1,0:T(8,128)(2,1)S(1)}, bf16[2048,768]{1,0:T(8,128)(2,1)}, u32[]{:S(2)}) copy-start(bf16[2048,768]{1,0:T(8,128)(2,1)} %features) | copy-start | bytes 9437188
  0.0 10.1 %copy-start = (bf16[768,768]{1,0:T(8,128)(2,1)S(1)}, bf16[768,768]{1,0:T(8,128)(2,1)}, u32[]{:S(2)}) copy-start(bf16[768,768]{1,0:T(8,128)(2,1)} %refs_5_.1) | copy-start | bytes 3538948
  0.0 10.1 %copy-start.2 = (s32[1,32]{1,0:T(1,128)S(1)}, s32[1,32]{1,0:T(1,128)}, u32[]{:S(2)}) copy-start(s32[1,32]{1,0:T(1,128)} %counts.1) | copy-start | bytes 388
  0.0 10.1 %copy-start.1 = (s32[1,32,8]{1,2,0:T(8,128)S(1)}, s32[1,32,8]{1,2,0:T(8,128)}, u32[]{:S(2)}) copy-start(s32[1,32,8]{1,2,0:T(8,128)} %param.16) | copy-start | bytes 3076
  2.7 2.1 %collective-permute-start = (bf16[4,3,4,8,768]{4,3,2,1,0:T(8,128)(2,1)S(1)}, bf16[4,3,4,8,768]{4,3,2,1,0:T(8,128)(2,1)S(1)}, u32[]{:S(2)}, u32[]{:S(2)}) collective-permute-start(bf16[4,3,4,8,768]{4,3,2,1,0:T(8,128)(2,1)S(1)} %get-tuple-element.44), channel_id=1, source_target_pairs={{0,1},{1,0},{2,3},{3,2},{4,5},{5,4},{6,7},{7,6},{8,9},{9,8},{10,11... | collective-permute-start | bytes 1769480 | tf_op jit(solution)/shard_map/ppermute | solution.py:355
  5.6 7.1 %collective-permute-start.1 = (bf16[3,4,8,768]{3,2,1,0:T(8,128)(2,1)S(1)}, bf16[3,4,8,768]{3,2,1,0:T(8,128)(2,1)S(1)}, u32[]{:S(2)}, u32[]{:S(2)}) collective-permute-start(bf16[3,4,8,768]{3,2,1,0:T(8,128)(2,1)S(1)} %get-tuple-element.46), channel_id=1, source_target_pairs={{0,2},{1,3},{2,0},{3,1},{4,6},{5,7},{6,4},{7,5},{8,10},{9,11},{10,... | collective-permute-start | bytes 442376 | tf_op jit(solution)/shard_map/ppermute | solution.py:355
  8.6 7.1 %collective-permute-start.2 = (bf16[3,4,8,768]{3,2,1,0:T(8,128)(2,1)S(1)}, bf16[3,4,8,768]{3,2,1,0:T(8,128)(2,1)S(1)}, u32[]{:S(2)}, u32[]{:S(2)}) collective-permute-start(bf16[3,4,8,768]{3,2,1,0:T(8,128)(2,1)S(1)} %get-tuple-element.50), channel_id=1, source_target_pairs={{0,4},{1,5},{2,6},{3,7},{4,0},{5,1},{6,2},{7,3},{8,12},{9,13},{10,... | collective-permute-start | bytes 442376 | tf_op jit(solution)/shard_map/ppermute | solution.py:355
  10.1 7.1 %collective-permute-start.3 = (bf16[3,4,8,768]{3,2,1,0:T(8,128)(2,1)S(1)}, bf16[3,4,8,768]{3,2,1,0:T(8,128)(2,1)S(1)}, u32[]{:S(2)}, u32[]{:S(2)}) collective-permute-start(bf16[3,4,8,768]{3,2,1,0:T(8,128)(2,1)S(1)} %get-tuple-element.52), channel_id=1, source_target_pairs={{0,6},{1,7},{2,4},{3,5},{4,2},{5,3},{6,0},{7,1},{8,14},{9,15},{10,... | collective-permute-start | bytes 442376 | tf_op jit(solution)/shard_map/ppermute | solution.py:355
  12.7 5.6 %collective-permute-start.5 = (bf16[4,4,8,768]{3,2,1,0:T(8,128)(2,1)S(1)}, bf16[4,4,8,768]{3,2,1,0:T(8,128)(2,1)S(1)}, u32[]{:S(2)}, u32[]{:S(2)}) collective-permute-start(bf16[4,4,8,768]{3,2,1,0:T(8,128)(2,1)S(1)} %get-tuple-element.56), channel_id=1, source_target_pairs={{0,1},{1,0},{2,3},{3,2},{4,5},{5,4},{6,7},{7,6},{8,9},{9,8},{10,11... | collective-permute-start | bytes 589832 | tf_op jit(solution)/shard_map/ppermute | solution.py:355
  18.4 6.5 %collective-permute-start.6 = (bf16[2,2,4,8,768]{4,3,0,2,1:T(8,128)(2,1)S(1)}, bf16[2,2,4,8,768]{4,3,0,2,1:T(8,128)(2,1)S(1)}, u32[]{:S(2)}, u32[]{:S(2)}) collective-permute-start(bf16[2,2,4,8,768]{4,3,0,2,1:T(8,128)(2,1)S(1)} %fusion.1), channel_id=1, source_target_pairs={{0,4},{1,5},{2,6},{3,7},{4,0},{5,1},{6,2},{7,3},{8,12},{9,13},{10,... | collective-permute-start | bytes 589832 | tf_op jit(solution)/shard_map/ppermute | solution.py:355
  20.1 4.8 %collective-permute-start.4 = (bf16[5,8,768]{2,1,0:T(8,128)(2,1)S(1)}, bf16[5,8,768]{2,1,0:T(8,128)(2,1)S(1)}, u32[]{:S(2)}, u32[]{:S(2)}) collective-permute-start(bf16[5,8,768]{2,1,0:T(8,128)(2,1)S(1)} %get-tuple-element.54), channel_id=1, source_target_pairs={{0,8},{1,9},{2,10},{3,11},{4,12},{5,13},{6,14},{7,15},{8,0},{9,1},... | collective-permute-start | bytes 184328 | tf_op jit(solution)/shard_map/ppermute | solution.py:355
  21.7 6.4 %collective-permute-start.7 = (bf16[5,8,768]{2,1,0:T(8,128)(2,1)S(1)}, bf16[5,8,768]{2,1,0:T(8,128)(2,1)S(1)}, u32[]{:S(2)}, u32[]{:S(2)}) collective-permute-start(bf16[5,8,768]{2,1,0:T(8,128)(2,1)S(1)} %get-tuple-element.59), channel_id=1, source_target_pairs={{0,16},{1,17},{2,18},{3,19},{4,20},{5,21},{6,22},{7,23},{8,24},{9,... | collective-permute-start | bytes 184328 | tf_op jit(solution)/shard_map/ppermute | solution.py:355
  24.3 6.1 %collective-permute-start.8 = (bf16[5,8,768]{2,1,0:T(8,128)(2,1)S(1)}, bf16[5,8,768]{2,1,0:T(8,128)(2,1)S(1)}, u32[]{:S(2)}, u32[]{:S(2)}) collective-permute-start(bf16[5,8,768]{2,1,0:T(8,128)(2,1)S(1)} %get-tuple-element.60), channel_id=1, source_target_pairs={{0,24},{1,25},{2,26},{3,27},{4,28},{5,29},{6,30},{7,31},{8,16},{9,... | collective-permute-start | bytes 184328 | tf_op jit(solution)/shard_map/ppermute | solution.py:355
  30.4 24.1 %copy-start.5 = (f32[768]{0:T(1024)S(1)}, f32[768]{0:T(1024)}, u32[]{:S(2)}) copy-start(f32[768]{0:T(1024)} %param.19) | copy-start | bytes 9220
  30.4 24.1 %copy-start.6 = (s32[8,4]{0,1:T(4,128)S(1)}, s32[8,4]{0,1:T(4,128)}, u32[]{:S(2)}) copy-start(s32[8,4]{0,1:T(4,128)} %param.13) | copy-start | bytes 388
  31.3 6.6 %collective-permute-start.11 = (bf16[8,8,768]{2,1,0:T(8,128)(2,1)S(1)}, bf16[8,8,768]{2,1,0:T(8,128)(2,1)S(1)}, u32[]{:S(2)}, u32[]{:S(2)}) collective-permute-start(bf16[8,8,768]{2,1,0:T(8,128)(2,1)S(1)} %shard_map.95), channel_id=1, source_target_pairs={{0,24},{1,25},{2,26},{3,27},{4,28},{5,29},{6,30},{7,31},{8,16},{9,... | collective-permute-start | bytes 294920 | tf_op jit(solution)/shard_map/ppermute | solution.py:355
  32.0 8.3 %collective-permute-start.10 = (bf16[8,8,768]{2,1,0:T(8,128)(2,1)S(1)}, bf16[8,8,768]{2,1,0:T(8,128)(2,1)S(1)}, u32[]{:S(2)}, u32[]{:S(2)}) collective-permute-start(bf16[8,8,768]{2,1,0:T(8,128)(2,1)S(1)} %shard_map.95), channel_id=1, source_target_pairs={{0,16},{1,17},{2,18},{3,19},{4,20},{5,21},{6,22},{7,23},{8,24},{9,... | collective-permute-start | bytes 294920 | tf_op jit(solution)/shard_map/ppermute | solution.py:355
  32.0 8.3 %collective-permute-start.9 = (bf16[8,8,768]{2,1,0:T(8,128)(2,1)S(1)}, bf16[8,8,768]{2,1,0:T(8,128)(2,1)S(1)}, u32[]{:S(2)}, u32[]{:S(2)}) collective-permute-start(bf16[8,8,768]{2,1,0:T(8,128)(2,1)S(1)} %shard_map.95), channel_id=1, source_target_pairs={{0,8},{1,9},{2,10},{3,11},{4,12},{5,13},{6,14},{7,15},{8,0},{9,1},... | collective-permute-start | bytes 294920 | tf_op jit(solution)/shard_map/ppermute | solution.py:355
  35.8 5.7 %collective-permute-start.12 = (bf16[2,2,4,8,768]{4,3,1,2,0:T(8,128)(2,1)S(1)}, bf16[2,2,4,8,768]{4,3,1,2,0:T(8,128)(2,1)S(1)}, u32[]{:S(2)}, u32[]{:S(2)}) collective-permute-start(bf16[2,2,4,8,768]{4,3,1,2,0:T(8,128)(2,1)S(1)} %pad_maximum_fusion.1), channel_id=1, source_target_pairs={{0,2},{1,3},{2,0},{3,1},{4,6},{5,7},{6,4},{7,5},{8,10},{9,11},{10,... | collective-permute-start | bytes 589832 | tf_op jit(solution)/shard_map/ppermute | solution.py:355
  41.6 8.7 %collective-permute-start.16 = (bf16[8,32,768]{2,1,0:T(8,128)(2,1)S(1)}, bf16[8,32,768]{2,1,0:T(8,128)(2,1)S(1)}, u32[]{:S(2)}, u32[]{:S(2)}) collective-permute-start(bf16[8,32,768]{2,1,0:T(8,128)(2,1)S(1)} %pad_maximum_fusion.refs_0_), channel_id=1, source_target_pairs={{0,4},{1,5},{2,6},{3,7},{4,0},{5,1},{6,2},{7,3},{8,12},{9,13},{10,... | collective-permute-start | bytes 1179656 | tf_op jit(solution)/shard_map/ppermute | solution.py:355
  42.2 10.0 %collective-permute-start.14 = (bf16[8,32,768]{2,1,0:T(8,128)(2,1)S(1)}, bf16[8,32,768]{2,1,0:T(8,128)(2,1)S(1)}, u32[]{:S(2)}, u32[]{:S(2)}) collective-permute-start(bf16[8,32,768]{2,1,0:T(8,128)(2,1)S(1)} %pad_maximum_fusion.refs_0_), channel_id=1, source_target_pairs={{0,2},{1,3},{2,0},{3,1},{4,6},{5,7},{6,4},{7,5},{8,10},{9,11},{10,... | collective-permute-start | bytes 1179656 | tf_op jit(solution)/shard_map/ppermute | solution.py:355
  43.8 10.1 %collective-permute-start.22 = (bf16[4,2,8,768]{3,2,1,0:T(8,128)(2,1)S(1)}, bf16[4,2,8,768]{3,2,1,0:T(8,128)(2,1)S(1)}, u32[]{:S(2)}, u32[]{:S(2)}) collective-permute-start(bf16[4,2,8,768]{3,2,1,0:T(8,128)(2,1)S(1)} %pad_maximum_fusion.4), channel_id=1, source_target_pairs={{0,8},{1,9},{2,10},{3,11},{4,12},{5,13},{6,14},{7,15},{8,0},{9,1},... | collective-permute-start | bytes 294920 | tf_op jit(solution)/shard_map/ppermute | solution.py:355
  44.2 9.7 %collective-permute-start.23 = (bf16[4,2,8,768]{3,2,1,0:T(8,128)(2,1)S(1)}, bf16[4,2,8,768]{3,2,1,0:T(8,128)(2,1)S(1)}, u32[]{:S(2)}, u32[]{:S(2)}) collective-permute-start(bf16[4,2,8,768]{3,2,1,0:T(8,128)(2,1)S(1)} %pad_maximum_fusion.5), channel_id=1, source_target_pairs={{0,16},{1,17},{2,18},{3,19},{4,20},{5,21},{6,22},{7,23},{8,24},{9,... | collective-permute-start | bytes 294920 | tf_op jit(solution)/shard_map/ppermute | solution.py:355
  45.2 9.2 %collective-permute-start.24 = (bf16[4,2,8,768]{3,2,1,0:T(8,128)(2,1)S(1)}, bf16[4,2,8,768]{3,2,1,0:T(8,128)(2,1)S(1)}, u32[]{:S(2)}, u32[]{:S(2)}) collective-permute-start(bf16[4,2,8,768]{3,2,1,0:T(8,128)(2,1)S(1)} %pad_maximum_fusion.6), channel_id=1, source_target_pairs={{0,24},{1,25},{2,26},{3,27},{4,28},{5,29},{6,30},{7,31},{8,16},{9,... | collective-permute-start | bytes 294920 | tf_op jit(solution)/shard_map/ppermute | solution.py:355
  50.3 5.7 %collective-permute-start.18 = (bf16[8,32,384]{2,1,0:T(8,128)(2,1)S(1)}, bf16[8,32,384]{2,1,0:T(8,128)(2,1)S(1)}, u32[]{:S(2)}, u32[]{:S(2)}) collective-permute-start(bf16[8,32,384]{2,1,0:T(8,128)(2,1)S(1)} %slice.106), channel_id=1, source_target_pairs={{0,2},{1,3},{2,0},{3,1},{4,6},{5,7},{6,4},{7,5},{8,10},{9,11},{10,... | collective-permute-start | bytes 589832 | tf_op jit(solution)/shard_map/ppermute | solution.py:355
  52.1 5.7 %collective-permute-start.20 = (bf16[8,32,384]{2,1,0:T(8,128)(2,1)S(1)}, bf16[8,32,384]{2,1,0:T(8,128)(2,1)S(1)}, u32[]{:S(2)}, u32[]{:S(2)}) collective-permute-start(bf16[8,32,384]{2,1,0:T(8,128)(2,1)S(1)} %slice.107), channel_id=1, source_target_pairs={{0,4},{1,5},{2,6},{3,7},{4,0},{5,1},{6,2},{7,3},{8,12},{9,13},{10,... | collective-permute-start | bytes 589832 | tf_op jit(solution)/shard_map/ppermute | solution.py:355
  53.9 4.1 %collective-permute-start.13 = (bf16[8,32,768]{2,1,0:T(8,128)(2,1)S(1)}, bf16[8,32,768]{2,1,0:T(8,128)(2,1)S(1)}, u32[]{:S(2)}, u32[]{:S(2)}) collective-permute-start(bf16[8,32,768]{2,1,0:T(8,128)(2,1)S(1)} %pad_maximum_fusion.refs_0_), channel_id=1, source_target_pairs={{0,1},{1,0},{2,3},{3,2},{4,5},{5,4},{6,7},{7,6},{8,9},{9,8},{10,11... | collective-permute-start | bytes 1179656 | tf_op jit(solution)/shard_map/ppermute | solution.py:355
  53.9 4.1 %collective-permute-start.17 = (bf16[8,32,768]{2,1,0:T(8,128)(2,1)S(1)}, bf16[8,32,768]{2,1,0:T(8,128)(2,1)S(1)}, u32[]{:S(2)}, u32[]{:S(2)}) collective-permute-start(bf16[8,32,768]{2,1,0:T(8,128)(2,1)S(1)} %collective-permute-done.16.refs_4_), channel_id=1, source_target_pairs={{0,1},{1,0},{2,3},{3,2},{4,5},{5,4},{6,7},{7,6},{8,9},{9,8},{10,11... | collective-permute-start | bytes 1179656 | tf_op jit(solution)/shard_map/ppermute | solution.py:355
  54.4 3.6 %collective-permute-start.15 = (bf16[8,32,768]{2,1,0:T(8,128)(2,1)S(1)}, bf16[8,32,768]{2,1,0:T(8,128)(2,1)S(1)}, u32[]{:S(2)}, u32[]{:S(2)}) collective-permute-start(bf16[8,32,768]{2,1,0:T(8,128)(2,1)S(1)} %collective-permute-done.14.refs_2_), channel_id=1, source_target_pairs={{0,1},{1,0},{2,3},{3,2},{4,5},{5,4},{6,7},{7,6},{8,9},{9,8},{10,11... | collective-permute-start | bytes 1179656 | tf_op jit(solution)/shard_map/ppermute | solution.py:355
  56.0 2.0 %collective-permute-start.19 = (bf16[8,32,384]{2,1,0:T(8,128)(2,1)S(1)}, bf16[8,32,384]{2,1,0:T(8,128)(2,1)S(1)}, u32[]{:S(2)}, u32[]{:S(2)}) collective-permute-start(bf16[8,32,384]{2,1,0:T(8,128)(2,1)S(1)} %collective-permute-done.18.refs_6_), channel_id=1, source_target_pairs={{0,1},{1,0},{2,3},{3,2},{4,5},{5,4},{6,7},{7,6},{8,9},{9,8},{10,11... | collective-permute-start | bytes 589832 | tf_op jit(solution)/shard_map/ppermute | solution.py:355
  57.9 1.4 %collective-permute-start.21 = (bf16[8,32,384]{2,1,0:T(8,128)(2,1)S(1)}, bf16[8,32,384]{2,1,0:T(8,128)(2,1)S(1)}, u32[]{:S(2)}, u32[]{:S(2)}) collective-permute-start(bf16[8,32,384]{2,1,0:T(8,128)(2,1)S(1)} %collective-permute-done.20.refs_8_), channel_id=1, source_target_pairs={{0,1},{1,0},{2,3},{3,2},{4,5},{5,4},{6,7},{7,6},{8,9},{9,8},{10,11... | collective-permute-start | bytes 589832 | tf_op jit(solution)/shard_map/ppermute | solution.py:355

commit v5 on v4

--- a/solution.py
+++ b/solution.py
@@ -47,16 +47,28 @@
     me = lax.axis_index(AXES)
     count = blocks.shape[0]
     core = me % 2
-    (at,) = scan(ids, lambda i: i // (2 * count) == me // 2, [lambda i: i % count])
+    at, owner = scan(
+        ids, lambda i: i // (2 * count) == me // 2, [lambda i: i % count, lambda i: i // count + 1]
+    )
     copies = []
     for s in range(SLOTS):
         for out, half in ((give, 1 - core), (keep, core)):
             copies.append(
                 pltpu.make_async_copy(blocks.at[at[s], :, half], out.at[:, s], sems.at[len(copies)])
             )
-            copies[-1].start()
-    for copy in copies:
-        copy.wait()
+    for s in range(SLOTS):
+
+        @pl.when(owner[s] == me + 1)
+        def _():
+            copies[2 * s].start()
+            copies[2 * s + 1].start()
+
+    for s in range(SLOTS):
+
+        @pl.when(owner[s] == me + 1)
+        def _():
+            copies[2 * s].wait()
+            copies[2 * s + 1].wait()
 
 
 def halves(ids, blocks, devices):
@@ -300,7 +312,7 @@
         out[rows] = jnp.maximum(total + bias[...], 0.0).astype(out.dtype)
 
 
-def layer(meta, pieces, listed, edge, sparse, bias, group=2):
+def layer(meta, pieces, listed, edge, sparse, bias, group=4):
     blocks, tiles_per, tile, _ = edge.shape
     stripes, _, width = pieces[0].shape
     lines = sparse.shape[1]
@@ -387,7 +399,7 @@
     both = jnp.stack([for_own, from_pair]).reshape(2, 2, 2, *for_own.shape[1:])
     across = swap(both[:, 1], 4)
 
-    arrived[1], across = lax.optimization_barrier((arrived[1], across))
+    arrived[-1], across = lax.optimization_barrier((arrived[-1], across))
 
     held = choose(ids, full, arrived, spare, weight, block_count)
 

time: 67.8 us -> 66.9 us (0.987)
  starting transfers between devices: 28 us -> 26.8 us
  waiting for transfers between devices: 20.1 us -> 20.9 us
    ppermute x25, starting transfers between devices: 28 us -> 26.8 us  [swap(): return lax.ppermute(x, AXES, [(d, d ^ mask) for d in range(devices)])]
    ppermute x25, waiting for transfers between devices: 20.1 us -> 20.9 us  [swap(): return lax.ppermute(x, AXES, [(d, d ^ mask) for d in range(devices)])]
  transfers between devices with their start and end apart: 25 -> 25, of which waited for: 13 -> 10; matrix products, arithmetic and copies ran while one was open for 3% -> 3% of each run, Pallas kernels for 5% -> 5%
where the time goes in v5:
time: 66.9 us; the launch traced here: 66.7 us
  starting transfers between devices  26.8 us (40%)
  waiting for transfers between devices  20.9 us (31%)
  Pallas kernels  15.3 us (23%)
  other arithmetic  1.84 us (3%)
  between operations  1.59 us (2%)
    ppermute x25, starting transfers between devices, swap(): return lax.ppermute(x, AXES, [(d, d ^ mask) for d in range(devices)])  26.8 us
    ppermute x25, waiting for transfers between devices, swap(): return lax.ppermute(x, AXES, [(d, d ^ mask) for d in range(devices)])  20.9 us
    pallas_call x1, Pallas kernels, layer(): pl.pallas_call(functools.partial(layer_kernel, group), out_shape=jax.Shap...  8.13 us
    pallas_call x1, Pallas kernels, halves(): pl.pallas_call(halves_kernel, out_shape=[shape, shape], in_specs=[SMEM, H...  2.41 us
    pallas_call x1, Pallas kernels, listed_rows(): pl.pallas_call(rows_kernel, out_shape=[shape, shape], in_specs=[VMEM] * 4...  1.94 us
    reduce_max x2, other arithmetic, load(): jnp.max(jnp.sum((at[:, None] == at[None, :]).astype(jnp.int32), axis=1))  1.34 us
  transfers between devices with their start and end apart: 25, of which 10 were waited for; matrix products, arithmetic and copies ran while one was open for 3% of the time, Pallas kernels for 5%

profile of v5, /device:TPU:0, one launch (start us, length us, event | category | flops | bytes accessed | tf_op | source)
XLA Modules:
  0.0 66.7 jit_solution(15232366951981836929)
XLA Ops:
  0.0 2.4 %shard_map.91 = (bf16[4,3,4,8,768]{4,3,2,1,0:T(8,128)(2,1)S(1)}, bf16[4,3,4,8,768]{4,3,2,1,0:T(8,128)(2,1)S(1)}) custom-call(s32[8]{0:T(128)} %ids.7, bf16[8,4,2,4,8,768]{5,4,3,2,1,0:T(8,128)(2,1)} %bitcast.57), custom_call_target="tpu_custom_call" | custom-call | tf_op jit(solution)/shard_map/pallas_call | solution.py:79
  2.4 0.1 collective-permute-start
  2.5 2.0 %collective-permute-done.got = bf16[4,3,4,8,768]{4,3,2,1,0:T(8,128)(2,1)S(1)} collective-permute-done((bf16[4,3,4,8,768]{4,3,2,1,0:T(8,128)(2,1)S(1)}, bf16[4,3,4,8,768]{4,3,2,1,0:T(8,128)(2,1)S(1)}, u32[]{:S(2)}, u32[]{:S(2)}) %collective-permute-start) | collective-permute-done | bytes 589856 | tf_op jit(solution)/shard_map/ppermute | solution.py:367
  4.5 0.7 %shard_map.92 = (bf16[3,4,8,768]{3,2,1,0:T(8,128)(2,1)S(1)}, bf16[3,4,8,768]{3,2,1,0:T(8,128)(2,1)S(1)}, bf16[3,4,8,768]{3,2,1,0:T(8,128)(2,1)S(1)}, bf16[3,4,8,768]{3,2,1,0:T(8,128)(2,1)S(1)}) custom-call(s32[8]{0:T(128)S(1)} %copy-done.4, bf16[4,3,4,8,768]{4,3,2,1,0:T(8,128)(2,1)S(1)} %get-tuple-element.43.keep, ...), custom_call_target="tpu_custom_call" | custom-call | tf_op jit(solution)/shard_map/pallas_call | solution.py:110
  5.2 1.6 %collective-permute-start.1 = (bf16[3,4,8,768]{3,2,1,0:T(8,128)(2,1)S(1)}, bf16[3,4,8,768]{3,2,1,0:T(8,128)(2,1)S(1)}, u32[]{:S(2)}, u32[]{:S(2)}) collective-permute-start(bf16[3,4,8,768]{3,2,1,0:T(8,128)(2,1)S(1)} %get-tuple-element.46), channel_id=1, source_target_pairs={{0,2},{1,3},{2,0},{3,1},{4,6},{5,7},{6,4},{7,5},{8,10},{9,11},{10,... | collective-permute-start | bytes 442376 | tf_op jit(solution)/shard_map/ppermute | solution.py:367
  6.9 1.5 %collective-permute-start.2 = (bf16[3,4,8,768]{3,2,1,0:T(8,128)(2,1)S(1)}, bf16[3,4,8,768]{3,2,1,0:T(8,128)(2,1)S(1)}, u32[]{:S(2)}, u32[]{:S(2)}) collective-permute-start(bf16[3,4,8,768]{3,2,1,0:T(8,128)(2,1)S(1)} %get-tuple-element.50), channel_id=1, source_target_pairs={{0,4},{1,5},{2,6},{3,7},{4,0},{5,1},{6,2},{7,3},{8,12},{9,13},{10,... | collective-permute-start | bytes 442376 | tf_op jit(solution)/shard_map/ppermute | solution.py:367
  8.4 0.8 %collective-permute-start.3 = (bf16[3,4,8,768]{3,2,1,0:T(8,128)(2,1)S(1)}, bf16[3,4,8,768]{3,2,1,0:T(8,128)(2,1)S(1)}, u32[]{:S(2)}, u32[]{:S(2)}) collective-permute-start(bf16[3,4,8,768]{3,2,1,0:T(8,128)(2,1)S(1)} %get-tuple-element.52), channel_id=1, source_target_pairs={{0,6},{1,7},{2,4},{3,5},{4,2},{5,3},{6,0},{7,1},{8,14},{9,15},{10,... | collective-permute-start | bytes 442376 | tf_op jit(solution)/shard_map/ppermute | solution.py:367
  9.2 1.9 %shard_map.93 = (bf16[4,4,8,768]{3,2,1,0:T(8,128)(2,1)S(1)}, bf16[4,4,8,768]{3,2,1,0:T(8,128)(2,1)S(1)}) custom-call(s32[8,32]{1,0:T(8,128)S(1)} %bitcast.56, s32[1,32]{1,0:T(1,128)S(1)} %copy-done.2, bf16[2048,768]{1,0:T(8,128)(2,1)S(1)} %copy-done.3, bf16[768,768]{1,0:T(8,128)(2,1)S(1)} %copy-done), custom_call_target="tpu_custom_call" | custom-call | tf_op jit(solution)/shard_map/pallas_call | solution.py:247
  11.1 0.0 collective-permute-done.1.refs_1_
  11.2 0.0 collective-permute-start.7
  11.2 0.2 convert_reduce_fusion
  11.5 0.6 reduce_max.18
  12.1 0.7 %reduce_max.19 = s32[]{:T(128)} reduce(s32[8]{0:T(128)S(1)} %get-tuple-element.97, s32[]{:T(128)} %constant.67.clone.1), dimensions={0}, to_apply=%region_3.4 | reduce | flops 7 | bytes 40 | tf_op jit(solution)/shard_map/reduce_max | solution.py:374
  14.2 0.0 collective-permute-done.2.refs_2_
  14.2 2.3 %collective-permute-done.3.refs_3_ = bf16[3,4,8,768]{3,2,1,0:T(8,128)(2,1)S(1)} collective-permute-done((bf16[3,4,8,768]{3,2,1,0:T(8,128)(2,1)S(1)}, bf16[3,4,8,768]{3,2,1,0:T(8,128)(2,1)S(1)}, u32[]{:S(2)}, u32[]{:S(2)}) %collective-permute-start.3) | collective-permute-done | bytes 147488 | tf_op jit(solution)/shard_map/ppermute | solution.py:367
  16.4 1.2 %shard_map.94 = (bf16[5,8,768]{2,1,0:T(8,128)(2,1)S(1)}, bf16[5,8,768]{2,1,0:T(8,128)(2,1)S(1)}, bf16[5,8,768]{2,1,0:T(8,128)(2,1)S(1)}, bf16[5,8,768]{2,1,0:T(8,128)(2,1)S(1)}) custom-call(s32[8]{0:T(128)S(1)} %copy-done.4, bf16[3,4,8,768]{3,2,1,0:T(8,128)(2,1)S(1)} %get-tuple-element.45.refs_0_, bf16[3,4,8,768]{3,2,1,0:T(8,128)(2,1)S(1)} %collective-permute-done.1.refs_1_, ...), custom_call_target="tpu_custom_call" | custom-call | tf_op jit(solution)/shard_map/pallas_call | solution.py:138
  17.6 0.0 collective-permute-done.7
  17.7 1.8 %collective-permute-start.8 = (bf16[2,2,4,8,768]{4,3,0,2,1:T(8,128)(2,1)S(1)}, bf16[2,2,4,8,768]{4,3,0,2,1:T(8,128)(2,1)S(1)}, u32[]{:S(2)}, u32[]{:S(2)}) collective-permute-start(bf16[2,2,4,8,768]{4,3,0,2,1:T(8,128)(2,1)S(1)} %fusion.1), channel_id=1, source_target_pairs={{0,4},{1,5},{2,6},{3,7},{4,0},{5,1},{6,2},{7,3},{8,12},{9,13},{10,... | collective-permute-start | bytes 589832 | tf_op jit(solution)/shard_map/ppermute | solution.py:367
  19.5 1.9 %collective-permute-start.4 = (bf16[5,8,768]{2,1,0:T(8,128)(2,1)S(1)}, bf16[5,8,768]{2,1,0:T(8,128)(2,1)S(1)}, u32[]{:S(2)}, u32[]{:S(2)}) collective-permute-start(bf16[5,8,768]{2,1,0:T(8,128)(2,1)S(1)} %get-tuple-element.54), channel_id=1, source_target_pairs={{0,8},{1,9},{2,10},{3,11},{4,12},{5,13},{6,14},{7,15},{8,0},{9,1},... | collective-permute-start | bytes 184328 | tf_op jit(solution)/shard_map/ppermute | solution.py:367
  21.4 2.1 %collective-permute-start.5 = (bf16[5,8,768]{2,1,0:T(8,128)(2,1)S(1)}, bf16[5,8,768]{2,1,0:T(8,128)(2,1)S(1)}, u32[]{:S(2)}, u32[]{:S(2)}) collective-permute-start(bf16[5,8,768]{2,1,0:T(8,128)(2,1)S(1)} %get-tuple-element.55), channel_id=1, source_target_pairs={{0,16},{1,17},{2,18},{3,19},{4,20},{5,21},{6,22},{7,23},{8,24},{9,... | collective-permute-start | bytes 184328 | tf_op jit(solution)/shard_map/ppermute | solution.py:367
  23.5 0.4 collective-permute-start.6
  23.9 5.7 %collective-permute-done.6.refs_3_ = bf16[5,8,768]{2,1,0:T(8,128)(2,1)S(1)} collective-permute-done((bf16[5,8,768]{2,1,0:T(8,128)(2,1)S(1)}, bf16[5,8,768]{2,1,0:T(8,128)(2,1)S(1)}, u32[]{:S(2)}, u32[]{:S(2)}) %collective-permute-start.6) | collective-permute-done | bytes 61472 | tf_op jit(solution)/shard_map/ppermute | solution.py:367
  29.6 0.0 collective-permute-done.8
  29.6 0.0 collective-permute-done.4.refs_1_
  29.6 0.0 collective-permute-done.5.refs_2_
  29.6 0.0 copy-start.5
  29.6 0.0 copy-start.6
  29.6 0.9 %shard_map.95 = bf16[8,8,768]{2,1,0:T(8,128)(2,1)S(1)} custom-call(s32[8]{0:T(128)S(1)} %copy-done.4, s32[1]{0:T(128)} %bitcast.1.full, bf16[5,8,768]{2,1,0:T(8,128)(2,1)S(1)} %get-tuple-element.53.refs_0_, bf16[5,8,768]{2,1,0:T(8,128)(2,1)S(1)} %collective-permute-done.4.refs_1_, bf16[5,8,768]{2,1,0:T(8,128)(2,1)S(1)} %collective-permute-done.5.refs_2_, ...), custom_call_target="tpu_custom_call" | custom-call | tf_op jit(solution)/shard_map/pallas_call | solution.py:165
  30.5 0.9 %collective-permute-start.11 = (bf16[8,8,768]{2,1,0:T(8,128)(2,1)S(1)}, bf16[8,8,768]{2,1,0:T(8,128)(2,1)S(1)}, u32[]{:S(2)}, u32[]{:S(2)}) collective-permute-start(bf16[8,8,768]{2,1,0:T(8,128)(2,1)S(1)} %shard_map.95), channel_id=1, source_target_pairs={{0,24},{1,25},{2,26},{3,27},{4,28},{5,29},{6,30},{7,31},{8,16},{9,... | collective-permute-start | bytes 294920 | tf_op jit(solution)/shard_map/ppermute | solution.py:367
  31.4 0.0 collective-permute-start.10
  31.4 3.5 %collective-permute-start.9 = (bf16[8,8,768]{2,1,0:T(8,128)(2,1)S(1)}, bf16[8,8,768]{2,1,0:T(8,128)(2,1)S(1)}, u32[]{:S(2)}, u32[]{:S(2)}) collective-permute-start(bf16[8,8,768]{2,1,0:T(8,128)(2,1)S(1)} %shard_map.95), channel_id=1, source_target_pairs={{0,8},{1,9},{2,10},{3,11},{4,12},{5,13},{6,14},{7,15},{8,0},{9,1},... | collective-permute-start | bytes 294920 | tf_op jit(solution)/shard_map/ppermute | solution.py:367
  35.0 1.8 %collective-permute-start.12 = (bf16[2,2,4,8,768]{4,3,1,2,0:T(8,128)(2,1)S(1)}, bf16[2,2,4,8,768]{4,3,1,2,0:T(8,128)(2,1)S(1)}, u32[]{:S(2)}, u32[]{:S(2)}) collective-permute-start(bf16[2,2,4,8,768]{4,3,1,2,0:T(8,128)(2,1)S(1)} %pad_maximum_fusion.1), channel_id=1, source_target_pairs={{0,2},{1,3},{2,0},{3,1},{4,6},{5,7},{6,4},{7,5},{8,10},{9,11},{10,... | collective-permute-start | bytes 589832 | tf_op jit(solution)/shard_map/ppermute | solution.py:367
  36.8 0.3 collective-permute-done.11
  37.2 2.8 %collective-permute-done.10 = bf16[8,8,768]{2,1,0:T(8,128)(2,1)S(1)} collective-permute-done((bf16[8,8,768]{2,1,0:T(8,128)(2,1)S(1)}, bf16[8,8,768]{2,1,0:T(8,128)(2,1)S(1)}, u32[]{:S(2)}, u32[]{:S(2)}) %collective-permute-start.10) | collective-permute-done | bytes 98336 | tf_op jit(solution)/shard_map/ppermute | solution.py:367
  40.0 0.0 collective-permute-done.9
  40.1 0.7 %collective-permute-done.12 = bf16[2,2,4,8,768]{4,3,1,2,0:T(8,128)(2,1)S(1)} collective-permute-done((bf16[2,2,4,8,768]{4,3,1,2,0:T(8,128)(2,1)S(1)}, bf16[2,2,4,8,768]{4,3,1,2,0:T(8,128)(2,1)S(1)}, u32[]{:S(2)}, u32[]{:S(2)}) %collective-permute-start.12) | collective-permute-done | bytes 196640 | tf_op jit(solution)/shard_map/ppermute | solution.py:367
  40.8 0.3 collective-permute-start.16
  41.1 1.7 %collective-permute-start.14 = (bf16[8,32,768]{2,1,0:T(8,128)(2,1)S(1)}, bf16[8,32,768]{2,1,0:T(8,128)(2,1)S(1)}, u32[]{:S(2)}, u32[]{:S(2)}) collective-permute-start(bf16[8,32,768]{2,1,0:T(8,128)(2,1)S(1)} %pad_maximum_fusion.refs_0_), channel_id=1, source_target_pairs={{0,2},{1,3},{2,0},{3,1},{4,6},{5,7},{6,4},{7,5},{8,10},{9,11},{10,... | collective-permute-start | bytes 1179656 | tf_op jit(solution)/shard_map/ppermute | solution.py:367
  42.8 0.9 %collective-permute-start.22 = (bf16[4,2,8,768]{3,2,1,0:T(8,128)(2,1)S(1)}, bf16[4,2,8,768]{3,2,1,0:T(8,128)(2,1)S(1)}, u32[]{:S(2)}, u32[]{:S(2)}) collective-permute-start(bf16[4,2,8,768]{3,2,1,0:T(8,128)(2,1)S(1)} %pad_maximum_fusion.4), channel_id=1, source_target_pairs={{0,8},{1,9},{2,10},{3,11},{4,12},{5,13},{6,14},{7,15},{8,0},{9,1},... | collective-permute-start | bytes 294920 | tf_op jit(solution)/shard_map/ppermute | solution.py:367
  43.7 0.9 %collective-permute-start.23 = (bf16[4,2,8,768]{3,2,1,0:T(8,128)(2,1)S(1)}, bf16[4,2,8,768]{3,2,1,0:T(8,128)(2,1)S(1)}, u32[]{:S(2)}, u32[]{:S(2)}) collective-permute-start(bf16[4,2,8,768]{3,2,1,0:T(8,128)(2,1)S(1)} %pad_maximum_fusion.5), channel_id=1, source_target_pairs={{0,16},{1,17},{2,18},{3,19},{4,20},{5,21},{6,22},{7,23},{8,24},{9,... | collective-permute-start | bytes 294920 | tf_op jit(solution)/shard_map/ppermute | solution.py:367
  44.6 2.8 %collective-permute-start.24 = (bf16[4,2,8,768]{3,2,1,0:T(8,128)(2,1)S(1)}, bf16[4,2,8,768]{3,2,1,0:T(8,128)(2,1)S(1)}, u32[]{:S(2)}, u32[]{:S(2)}) collective-permute-start(bf16[4,2,8,768]{3,2,1,0:T(8,128)(2,1)S(1)} %pad_maximum_fusion.6), channel_id=1, source_target_pairs={{0,24},{1,25},{2,26},{3,27},{4,28},{5,29},{6,30},{7,31},{8,16},{9,... | collective-permute-start | bytes 294920 | tf_op jit(solution)/shard_map/ppermute | solution.py:367
  47.5 2.5 %collective-permute-done.16.refs_4_ = bf16[8,32,768]{2,1,0:T(8,128)(2,1)S(1)} collective-permute-done((bf16[8,32,768]{2,1,0:T(8,128)(2,1)S(1)}, bf16[8,32,768]{2,1,0:T(8,128)(2,1)S(1)}, u32[]{:S(2)}, u32[]{:S(2)}) %collective-permute-start.16) | collective-permute-done | bytes 393248 | tf_op jit(solution)/shard_map/ppermute | solution.py:367
  50.0 1.4 %collective-permute-start.18 = (bf16[8,32,384]{2,1,0:T(8,128)(2,1)S(1)}, bf16[8,32,384]{2,1,0:T(8,128)(2,1)S(1)}, u32[]{:S(2)}, u32[]{:S(2)}) collective-permute-start(bf16[8,32,384]{2,1,0:T(8,128)(2,1)S(1)} %slice.106), channel_id=1, source_target_pairs={{0,2},{1,3},{2,0},{3,1},{4,6},{5,7},{6,4},{7,5},{8,10},{9,11},{10,... | collective-permute-start | bytes 589832 | tf_op jit(solution)/shard_map/ppermute | solution.py:367
  51.4 0.0 collective-permute-done.14.refs_2_
  51.4 1.7 %collective-permute-start.20 = (bf16[8,32,384]{2,1,0:T(8,128)(2,1)S(1)}, bf16[8,32,384]{2,1,0:T(8,128)(2,1)S(1)}, u32[]{:S(2)}, u32[]{:S(2)}) collective-permute-start(bf16[8,32,384]{2,1,0:T(8,128)(2,1)S(1)} %slice.107), channel_id=1, source_target_pairs={{0,4},{1,5},{2,6},{3,7},{4,0},{5,1},{6,2},{7,3},{8,12},{9,13},{10,... | collective-permute-start | bytes 589832 | tf_op jit(solution)/shard_map/ppermute | solution.py:367
  53.1 0.0 collective-permute-done.22.refs_11_
  53.1 0.0 collective-permute-start.13
  53.1 0.0 collective-permute-done.23.refs_12_
  53.2 0.5 collective-permute-start.17
  53.7 0.0 collective-permute-done.24.refs_13_
  53.7 0.1 collective-permute-start.15
  53.7 0.1 copy.12
  53.8 0.1 reshape.15
  53.9 1.8 %collective-permute-done.18.refs_6_ = bf16[8,32,384]{2,1,0:T(8,128)(2,1)S(1)} collective-permute-done((bf16[8,32,384]{2,1,0:T(8,128)(2,1)S(1)}, bf16[8,32,384]{2,1,0:T(8,128)(2,1)S(1)}, u32[]{:S(2)}, u32[]{:S(2)}) %collective-permute-start.18) | collective-permute-done | bytes 196640 | tf_op jit(solution)/shard_map/ppermute | solution.py:367
  55.7 0.0 collective-permute-start.19
  55.7 1.4 %collective-permute-done.20.refs_8_ = bf16[8,32,384]{2,1,0:T(8,128)(2,1)S(1)} collective-permute-done((bf16[8,32,384]{2,1,0:T(8,128)(2,1)S(1)}, bf16[8,32,384]{2,1,0:T(8,128)(2,1)S(1)}, u32[]{:S(2)}, u32[]{:S(2)}) %collective-permute-start.20) | collective-permute-done | bytes 196640 | tf_op jit(solution)/shard_map/ppermute | solution.py:367
  57.2 0.0 collective-permute-start.21
  57.2 0.1 pad_add_fusion.meta
  57.3 0.0 collective-permute-done.13.refs_1_
  57.3 0.0 collective-permute-done.17.refs_5_
  57.3 0.0 collective-permute-done.15.refs_3_
  57.3 0.0 collective-permute-done.19.refs_7_
  57.3 1.3 %collective-permute-done.21.refs_9_ = bf16[8,32,384]{2,1,0:T(8,128)(2,1)S(1)} collective-permute-done((bf16[8,32,384]{2,1,0:T(8,128)(2,1)S(1)}, bf16[8,32,384]{2,1,0:T(8,128)(2,1)S(1)}, u32[]{:S(2)}, u32[]{:S(2)}) %collective-permute-start.21) | collective-permute-done | bytes 196640 | tf_op jit(solution)/shard_map/ppermute | solution.py:367
  58.6 8.1 %shard_map.96 = bf16[2048,768]{1,0:T(8,128)(2,1)} custom-call(s32[40]{0:T(128)S(1)} %pad_add_fusion.meta, bf16[8,32,768]{2,1,0:T(8,128)(2,1)S(1)} %pad_maximum_fusion.refs_0_, bf16[8,32,768]{2,1,0:T(8,128)(2,1)S(1)} %collective-permute-done.13.refs_1_, bf16[8,32,768]{2,1,0:T(8,128)(2,1)S(1)} %collective-permute-done.14.refs_2_, ...), custom_call_target="tpu_custom_call" | custom-call | flops 4026531840 | bytes 8388608 | tf_op jit(solution)/shard_map/pallas_call | solution.py:319
  (34 shorter events, 0.4 us)
Async XLA Ops:
  0.0 4.5 %copy-start.4 = (s32[8]{0:T(128)S(1)}, s32[8]{0:T(128)}, u32[]{:S(2)}) copy-start(s32[8]{0:T(128)} %ids.7) | copy-start | bytes 100
  0.0 9.2 %copy-start.3 = (bf16[2048,768]{1,0:T(8,128)(2,1)S(1)}, bf16[2048,768]{1,0:T(8,128)(2,1)}, u32[]{:S(2)}) copy-start(bf16[2048,768]{1,0:T(8,128)(2,1)} %features) | copy-start | bytes 9437188
  0.0 9.2 %copy-start = (bf16[768,768]{1,0:T(8,128)(2,1)S(1)}, bf16[768,768]{1,0:T(8,128)(2,1)}, u32[]{:S(2)}) copy-start(bf16[768,768]{1,0:T(8,128)(2,1)} %refs_5_.1) | copy-start | bytes 3538948
  0.0 9.2 %copy-start.2 = (s32[1,32]{1,0:T(1,128)S(1)}, s32[1,32]{1,0:T(1,128)}, u32[]{:S(2)}) copy-start(s32[1,32]{1,0:T(1,128)} %counts.1) | copy-start | bytes 388
  0.0 9.2 %copy-start.1 = (s32[1,32,8]{1,2,0:T(8,128)S(1)}, s32[1,32,8]{1,2,0:T(8,128)}, u32[]{:S(2)}) copy-start(s32[1,32,8]{1,2,0:T(8,128)} %param.16) | copy-start | bytes 3076
  2.4 2.1 %collective-permute-start = (bf16[4,3,4,8,768]{4,3,2,1,0:T(8,128)(2,1)S(1)}, bf16[4,3,4,8,768]{4,3,2,1,0:T(8,128)(2,1)S(1)}, u32[]{:S(2)}, u32[]{:S(2)}) collective-permute-start(bf16[4,3,4,8,768]{4,3,2,1,0:T(8,128)(2,1)S(1)} %get-tuple-element.44), channel_id=1, source_target_pairs={{0,1},{1,0},{2,3},{3,2},{4,5},{5,4},{6,7},{7,6},{8,9},{9,8},{10,11... | collective-permute-start | bytes 1769480 | tf_op jit(solution)/shard_map/ppermute | solution.py:367
  5.2 6.0 %collective-permute-start.1 = (bf16[3,4,8,768]{3,2,1,0:T(8,128)(2,1)S(1)}, bf16[3,4,8,768]{3,2,1,0:T(8,128)(2,1)S(1)}, u32[]{:S(2)}, u32[]{:S(2)}) collective-permute-start(bf16[3,4,8,768]{3,2,1,0:T(8,128)(2,1)S(1)} %get-tuple-element.46), channel_id=1, source_target_pairs={{0,2},{1,3},{2,0},{3,1},{4,6},{5,7},{6,4},{7,5},{8,10},{9,11},{10,... | collective-permute-start | bytes 442376 | tf_op jit(solution)/shard_map/ppermute | solution.py:367
  6.9 7.3 %collective-permute-start.2 = (bf16[3,4,8,768]{3,2,1,0:T(8,128)(2,1)S(1)}, bf16[3,4,8,768]{3,2,1,0:T(8,128)(2,1)S(1)}, u32[]{:S(2)}, u32[]{:S(2)}) collective-permute-start(bf16[3,4,8,768]{3,2,1,0:T(8,128)(2,1)S(1)} %get-tuple-element.50), channel_id=1, source_target_pairs={{0,4},{1,5},{2,6},{3,7},{4,0},{5,1},{6,2},{7,3},{8,12},{9,13},{10,... | collective-permute-start | bytes 442376 | tf_op jit(solution)/shard_map/ppermute | solution.py:367
  8.4 8.1 %collective-permute-start.3 = (bf16[3,4,8,768]{3,2,1,0:T(8,128)(2,1)S(1)}, bf16[3,4,8,768]{3,2,1,0:T(8,128)(2,1)S(1)}, u32[]{:S(2)}, u32[]{:S(2)}) collective-permute-start(bf16[3,4,8,768]{3,2,1,0:T(8,128)(2,1)S(1)} %get-tuple-element.52), channel_id=1, source_target_pairs={{0,6},{1,7},{2,4},{3,5},{4,2},{5,3},{6,0},{7,1},{8,14},{9,15},{10,... | collective-permute-start | bytes 442376 | tf_op jit(solution)/shard_map/ppermute | solution.py:367
  11.2 6.5 %collective-permute-start.7 = (bf16[4,4,8,768]{3,2,1,0:T(8,128)(2,1)S(1)}, bf16[4,4,8,768]{3,2,1,0:T(8,128)(2,1)S(1)}, u32[]{:S(2)}, u32[]{:S(2)}) collective-permute-start(bf16[4,4,8,768]{3,2,1,0:T(8,128)(2,1)S(1)} %get-tuple-element.58), channel_id=1, source_target_pairs={{0,1},{1,0},{2,3},{3,2},{4,5},{5,4},{6,7},{7,6},{8,9},{9,8},{10,11... | collective-permute-start | bytes 589832 | tf_op jit(solution)/shard_map/ppermute | solution.py:367
  17.7 11.9 %collective-permute-start.8 = (bf16[2,2,4,8,768]{4,3,0,2,1:T(8,128)(2,1)S(1)}, bf16[2,2,4,8,768]{4,3,0,2,1:T(8,128)(2,1)S(1)}, u32[]{:S(2)}, u32[]{:S(2)}) collective-permute-start(bf16[2,2,4,8,768]{4,3,0,2,1:T(8,128)(2,1)S(1)} %fusion.1), channel_id=1, source_target_pairs={{0,4},{1,5},{2,6},{3,7},{4,0},{5,1},{6,2},{7,3},{8,12},{9,13},{10,... | collective-permute-start | bytes 589832 | tf_op jit(solution)/shard_map/ppermute | solution.py:367
  19.5 10.1 %collective-permute-start.4 = (bf16[5,8,768]{2,1,0:T(8,128)(2,1)S(1)}, bf16[5,8,768]{2,1,0:T(8,128)(2,1)S(1)}, u32[]{:S(2)}, u32[]{:S(2)}) collective-permute-start(bf16[5,8,768]{2,1,0:T(8,128)(2,1)S(1)} %get-tuple-element.54), channel_id=1, source_target_pairs={{0,8},{1,9},{2,10},{3,11},{4,12},{5,13},{6,14},{7,15},{8,0},{9,1},... | collective-permute-start | bytes 184328 | tf_op jit(solution)/shard_map/ppermute | solution.py:367
  21.4 8.2 %collective-permute-start.5 = (bf16[5,8,768]{2,1,0:T(8,128)(2,1)S(1)}, bf16[5,8,768]{2,1,0:T(8,128)(2,1)S(1)}, u32[]{:S(2)}, u32[]{:S(2)}) collective-permute-start(bf16[5,8,768]{2,1,0:T(8,128)(2,1)S(1)} %get-tuple-element.55), channel_id=1, source_target_pairs={{0,16},{1,17},{2,18},{3,19},{4,20},{5,21},{6,22},{7,23},{8,24},{9,... | collective-permute-start | bytes 184328 | tf_op jit(solution)/shard_map/ppermute | solution.py:367
  23.5 6.1 %collective-permute-start.6 = (bf16[5,8,768]{2,1,0:T(8,128)(2,1)S(1)}, bf16[5,8,768]{2,1,0:T(8,128)(2,1)S(1)}, u32[]{:S(2)}, u32[]{:S(2)}) collective-permute-start(bf16[5,8,768]{2,1,0:T(8,128)(2,1)S(1)} %get-tuple-element.56), channel_id=1, source_target_pairs={{0,24},{1,25},{2,26},{3,27},{4,28},{5,29},{6,30},{7,31},{8,16},{9,... | collective-permute-start | bytes 184328 | tf_op jit(solution)/shard_map/ppermute | solution.py:367
  29.6 24.2 %copy-start.5 = (f32[768]{0:T(1024)S(1)}, f32[768]{0:T(1024)}, u32[]{:S(2)}) copy-start(f32[768]{0:T(1024)} %param.19) | copy-start | bytes 9220
  29.6 24.2 %copy-start.6 = (s32[8,4]{0,1:T(4,128)S(1)}, s32[8,4]{0,1:T(4,128)}, u32[]{:S(2)}) copy-start(s32[8,4]{0,1:T(4,128)} %param.13) | copy-start | bytes 388
  30.5 6.6 %collective-permute-start.11 = (bf16[8,8,768]{2,1,0:T(8,128)(2,1)S(1)}, bf16[8,8,768]{2,1,0:T(8,128)(2,1)S(1)}, u32[]{:S(2)}, u32[]{:S(2)}) collective-permute-start(bf16[8,8,768]{2,1,0:T(8,128)(2,1)S(1)} %shard_map.95), channel_id=1, source_target_pairs={{0,24},{1,25},{2,26},{3,27},{4,28},{5,29},{6,30},{7,31},{8,16},{9,... | collective-permute-start | bytes 294920 | tf_op jit(solution)/shard_map/ppermute | solution.py:367
  31.4 8.6 %collective-permute-start.10 = (bf16[8,8,768]{2,1,0:T(8,128)(2,1)S(1)}, bf16[8,8,768]{2,1,0:T(8,128)(2,1)S(1)}, u32[]{:S(2)}, u32[]{:S(2)}) collective-permute-start(bf16[8,8,768]{2,1,0:T(8,128)(2,1)S(1)} %shard_map.95), channel_id=1, source_target_pairs={{0,16},{1,17},{2,18},{3,19},{4,20},{5,21},{6,22},{7,23},{8,24},{9,... | collective-permute-start | bytes 294920 | tf_op jit(solution)/shard_map/ppermute | solution.py:367
  31.4 8.6 %collective-permute-start.9 = (bf16[8,8,768]{2,1,0:T(8,128)(2,1)S(1)}, bf16[8,8,768]{2,1,0:T(8,128)(2,1)S(1)}, u32[]{:S(2)}, u32[]{:S(2)}) collective-permute-start(bf16[8,8,768]{2,1,0:T(8,128)(2,1)S(1)} %shard_map.95), channel_id=1, source_target_pairs={{0,8},{1,9},{2,10},{3,11},{4,12},{5,13},{6,14},{7,15},{8,0},{9,1},... | collective-permute-start | bytes 294920 | tf_op jit(solution)/shard_map/ppermute | solution.py:367
  35.0 5.7 %collective-permute-start.12 = (bf16[2,2,4,8,768]{4,3,1,2,0:T(8,128)(2,1)S(1)}, bf16[2,2,4,8,768]{4,3,1,2,0:T(8,128)(2,1)S(1)}, u32[]{:S(2)}, u32[]{:S(2)}) collective-permute-start(bf16[2,2,4,8,768]{4,3,1,2,0:T(8,128)(2,1)S(1)} %pad_maximum_fusion.1), channel_id=1, source_target_pairs={{0,2},{1,3},{2,0},{3,1},{4,6},{5,7},{6,4},{7,5},{8,10},{9,11},{10,... | collective-permute-start | bytes 589832 | tf_op jit(solution)/shard_map/ppermute | solution.py:367
  40.8 9.2 %collective-permute-start.16 = (bf16[8,32,768]{2,1,0:T(8,128)(2,1)S(1)}, bf16[8,32,768]{2,1,0:T(8,128)(2,1)S(1)}, u32[]{:S(2)}, u32[]{:S(2)}) collective-permute-start(bf16[8,32,768]{2,1,0:T(8,128)(2,1)S(1)} %pad_maximum_fusion.refs_0_), channel_id=1, source_target_pairs={{0,4},{1,5},{2,6},{3,7},{4,0},{5,1},{6,2},{7,3},{8,12},{9,13},{10,... | collective-permute-start | bytes 1179656 | tf_op jit(solution)/shard_map/ppermute | solution.py:367
  41.1 10.3 %collective-permute-start.14 = (bf16[8,32,768]{2,1,0:T(8,128)(2,1)S(1)}, bf16[8,32,768]{2,1,0:T(8,128)(2,1)S(1)}, u32[]{:S(2)}, u32[]{:S(2)}) collective-permute-start(bf16[8,32,768]{2,1,0:T(8,128)(2,1)S(1)} %pad_maximum_fusion.refs_0_), channel_id=1, source_target_pairs={{0,2},{1,3},{2,0},{3,1},{4,6},{5,7},{6,4},{7,5},{8,10},{9,11},{10,... | collective-permute-start | bytes 1179656 | tf_op jit(solution)/shard_map/ppermute | solution.py:367
  42.8 10.3 %collective-permute-start.22 = (bf16[4,2,8,768]{3,2,1,0:T(8,128)(2,1)S(1)}, bf16[4,2,8,768]{3,2,1,0:T(8,128)(2,1)S(1)}, u32[]{:S(2)}, u32[]{:S(2)}) collective-permute-start(bf16[4,2,8,768]{3,2,1,0:T(8,128)(2,1)S(1)} %pad_maximum_fusion.4), channel_id=1, source_target_pairs={{0,8},{1,9},{2,10},{3,11},{4,12},{5,13},{6,14},{7,15},{8,0},{9,1},... | collective-permute-start | bytes 294920 | tf_op jit(solution)/shard_map/ppermute | solution.py:367
  43.7 9.4 %collective-permute-start.23 = (bf16[4,2,8,768]{3,2,1,0:T(8,128)(2,1)S(1)}, bf16[4,2,8,768]{3,2,1,0:T(8,128)(2,1)S(1)}, u32[]{:S(2)}, u32[]{:S(2)}) collective-permute-start(bf16[4,2,8,768]{3,2,1,0:T(8,128)(2,1)S(1)} %pad_maximum_fusion.5), channel_id=1, source_target_pairs={{0,16},{1,17},{2,18},{3,19},{4,20},{5,21},{6,22},{7,23},{8,24},{9,... | collective-permute-start | bytes 294920 | tf_op jit(solution)/shard_map/ppermute | solution.py:367
  44.6 9.0 %collective-permute-start.24 = (bf16[4,2,8,768]{3,2,1,0:T(8,128)(2,1)S(1)}, bf16[4,2,8,768]{3,2,1,0:T(8,128)(2,1)S(1)}, u32[]{:S(2)}, u32[]{:S(2)}) collective-permute-start(bf16[4,2,8,768]{3,2,1,0:T(8,128)(2,1)S(1)} %pad_maximum_fusion.6), channel_id=1, source_target_pairs={{0,24},{1,25},{2,26},{3,27},{4,28},{5,29},{6,30},{7,31},{8,16},{9,... | collective-permute-start | bytes 294920 | tf_op jit(solution)/shard_map/ppermute | solution.py:367
  50.0 5.7 %collective-permute-start.18 = (bf16[8,32,384]{2,1,0:T(8,128)(2,1)S(1)}, bf16[8,32,384]{2,1,0:T(8,128)(2,1)S(1)}, u32[]{:S(2)}, u32[]{:S(2)}) collective-permute-start(bf16[8,32,384]{2,1,0:T(8,128)(2,1)S(1)} %slice.106), channel_id=1, source_target_pairs={{0,2},{1,3},{2,0},{3,1},{4,6},{5,7},{6,4},{7,5},{8,10},{9,11},{10,... | collective-permute-start | bytes 589832 | tf_op jit(solution)/shard_map/ppermute | solution.py:367
  51.4 5.7 %collective-permute-start.20 = (bf16[8,32,384]{2,1,0:T(8,128)(2,1)S(1)}, bf16[8,32,384]{2,1,0:T(8,128)(2,1)S(1)}, u32[]{:S(2)}, u32[]{:S(2)}) collective-permute-start(bf16[8,32,384]{2,1,0:T(8,128)(2,1)S(1)} %slice.107), channel_id=1, source_target_pairs={{0,4},{1,5},{2,6},{3,7},{4,0},{5,1},{6,2},{7,3},{8,12},{9,13},{10,... | collective-permute-start | bytes 589832 | tf_op jit(solution)/shard_map/ppermute | solution.py:367
  53.1 4.1 %collective-permute-start.13 = (bf16[8,32,768]{2,1,0:T(8,128)(2,1)S(1)}, bf16[8,32,768]{2,1,0:T(8,128)(2,1)S(1)}, u32[]{:S(2)}, u32[]{:S(2)}) collective-permute-start(bf16[8,32,768]{2,1,0:T(8,128)(2,1)S(1)} %pad_maximum_fusion.refs_0_), channel_id=1, source_target_pairs={{0,1},{1,0},{2,3},{3,2},{4,5},{5,4},{6,7},{7,6},{8,9},{9,8},{10,11... | collective-permute-start | bytes 1179656 | tf_op jit(solution)/shard_map/ppermute | solution.py:367
  53.2 4.1 %collective-permute-start.17 = (bf16[8,32,768]{2,1,0:T(8,128)(2,1)S(1)}, bf16[8,32,768]{2,1,0:T(8,128)(2,1)S(1)}, u32[]{:S(2)}, u32[]{:S(2)}) collective-permute-start(bf16[8,32,768]{2,1,0:T(8,128)(2,1)S(1)} %collective-permute-done.16.refs_4_), channel_id=1, source_target_pairs={{0,1},{1,0},{2,3},{3,2},{4,5},{5,4},{6,7},{7,6},{8,9},{9,8},{10,11... | collective-permute-start | bytes 1179656 | tf_op jit(solution)/shard_map/ppermute | solution.py:367
  53.7 3.6 %collective-permute-start.15 = (bf16[8,32,768]{2,1,0:T(8,128)(2,1)S(1)}, bf16[8,32,768]{2,1,0:T(8,128)(2,1)S(1)}, u32[]{:S(2)}, u32[]{:S(2)}) collective-permute-start(bf16[8,32,768]{2,1,0:T(8,128)(2,1)S(1)} %collective-permute-done.14.refs_2_), channel_id=1, source_target_pairs={{0,1},{1,0},{2,3},{3,2},{4,5},{5,4},{6,7},{7,6},{8,9},{9,8},{10,11... | collective-permute-start | bytes 1179656 | tf_op jit(solution)/shard_map/ppermute | solution.py:367
  55.7 1.6 %collective-permute-start.19 = (bf16[8,32,384]{2,1,0:T(8,128)(2,1)S(1)}, bf16[8,32,384]{2,1,0:T(8,128)(2,1)S(1)}, u32[]{:S(2)}, u32[]{:S(2)}) collective-permute-start(bf16[8,32,384]{2,1,0:T(8,128)(2,1)S(1)} %collective-permute-done.18.refs_6_), channel_id=1, source_target_pairs={{0,1},{1,0},{2,3},{3,2},{4,5},{5,4},{6,7},{7,6},{8,9},{9,8},{10,11... | collective-permute-start | bytes 589832 | tf_op jit(solution)/shard_map/ppermute | solution.py:367
  57.2 1.4 %collective-permute-start.21 = (bf16[8,32,384]{2,1,0:T(8,128)(2,1)S(1)}, bf16[8,32,384]{2,1,0:T(8,128)(2,1)S(1)}, u32[]{:S(2)}, u32[]{:S(2)}) collective-permute-start(bf16[8,32,384]{2,1,0:T(8,128)(2,1)S(1)} %collective-permute-done.20.refs_8_), channel_id=1, source_target_pairs={{0,1},{1,0},{2,3},{3,2},{4,5},{5,4},{6,7},{7,6},{8,9},{9,8},{10,11... | collective-permute-start | bytes 589832 | tf_op jit(solution)/shard_map/ppermute | solution.py:367

commit v6 on v5

--- a/solution.py
+++ b/solution.py
@@ -124,12 +124,15 @@
         owner = ids[j] // count
         slot = jnp.minimum(slot_of(ids, j, 2 * count), SLOTS - 1)
         to = jnp.minimum(slot_of(ids, j, PLANE * count), PLANE_SLOTS - 1)
-        for m, ref in enumerate(near):
-
-            @pl.when((owner // PLANE == group) & (owner % PLANE // 2 ^ place == m))
-            def _():
-                for g, out in enumerate(outs):
-                    out[to] = ref[slot, group ^ g]
+
+        @pl.when(owner // PLANE == group)
+        def _():
+            for m, ref in enumerate(near):
+
+                @pl.when(owner % PLANE // 2 ^ place == m)
+                def _():
+                    for g, out in enumerate(outs):
+                        out[to] = ref[slot, group ^ g]
 
 
 def sort(ids, near, count):

time: 66.9 us -> 66.9 us (level)
  waiting for transfers between devices: 20.9 us -> 20.2 us
  transfers between devices with their start and end apart: 25 -> 25, of which waited for: 10 -> 11; matrix products, arithmetic and copies ran while one was open for 3% -> 3% of each run, Pallas kernels for 5% -> 5%
where the time goes in v6:
time: 66.9 us; the launch traced here: 66.5 us
  starting transfers between devices  27.3 us (41%)
  waiting for transfers between devices  20.2 us (30%)
  Pallas kernels  15.2 us (23%)
  other arithmetic  1.84 us (3%)
  between operations  1.61 us (2%)
    ppermute x25, starting transfers between devices, swap(): return lax.ppermute(x, AXES, [(d, d ^ mask) for d in range(devices)])  27.3 us
    ppermute x25, waiting for transfers between devices, swap(): return lax.ppermute(x, AXES, [(d, d ^ mask) for d in range(devices)])  20.2 us
    pallas_call x1, Pallas kernels, layer(): pl.pallas_call(functools.partial(layer_kernel, group), out_shape=jax.Shap...  8.13 us
    pallas_call x1, Pallas kernels, halves(): pl.pallas_call(halves_kernel, out_shape=[shape, shape], in_specs=[SMEM, H...  2.41 us
    pallas_call x1, Pallas kernels, listed_rows(): pl.pallas_call(rows_kernel, out_shape=[shape, shape], in_specs=[VMEM] * 4...  1.94 us
    reduce_max x2, other arithmetic, load(): jnp.max(jnp.sum((at[:, None] == at[None, :]).astype(jnp.int32), axis=1))  1.34 us
  transfers between devices with their start and end apart: 25, of which 11 were waited for; matrix products, arithmetic and copies ran while one was open for 3% of the time, Pallas kernels for 5%

profile of v6, /device:TPU:0, one launch (start us, length us, event | category | flops | bytes accessed | tf_op | source)
XLA Modules:
  0.0 66.5 jit_solution(4979177778991496157)
XLA Ops:
  0.0 2.4 %shard_map.91 = (bf16[4,3,4,8,768]{4,3,2,1,0:T(8,128)(2,1)S(1)}, bf16[4,3,4,8,768]{4,3,2,1,0:T(8,128)(2,1)S(1)}) custom-call(s32[8]{0:T(128)} %ids.7, bf16[8,4,2,4,8,768]{5,4,3,2,1,0:T(8,128)(2,1)} %bitcast.57), custom_call_target="tpu_custom_call" | custom-call | tf_op jit(solution)/shard_map/pallas_call | solution.py:79
  2.4 0.1 collective-permute-start
  2.5 2.0 %collective-permute-done.got = bf16[4,3,4,8,768]{4,3,2,1,0:T(8,128)(2,1)S(1)} collective-permute-done((bf16[4,3,4,8,768]{4,3,2,1,0:T(8,128)(2,1)S(1)}, bf16[4,3,4,8,768]{4,3,2,1,0:T(8,128)(2,1)S(1)}, u32[]{:S(2)}, u32[]{:S(2)}) %collective-permute-start) | collective-permute-done | bytes 589856 | tf_op jit(solution)/shard_map/ppermute | solution.py:370
  4.5 0.7 %shard_map.92 = (bf16[3,4,8,768]{3,2,1,0:T(8,128)(2,1)S(1)}, bf16[3,4,8,768]{3,2,1,0:T(8,128)(2,1)S(1)}, bf16[3,4,8,768]{3,2,1,0:T(8,128)(2,1)S(1)}, bf16[3,4,8,768]{3,2,1,0:T(8,128)(2,1)S(1)}) custom-call(s32[8]{0:T(128)S(1)} %copy-done.4, bf16[4,3,4,8,768]{4,3,2,1,0:T(8,128)(2,1)S(1)} %get-tuple-element.43.keep, ...), custom_call_target="tpu_custom_call" | custom-call | tf_op jit(solution)/shard_map/pallas_call | solution.py:110
  5.2 1.6 %collective-permute-start.1 = (bf16[3,4,8,768]{3,2,1,0:T(8,128)(2,1)S(1)}, bf16[3,4,8,768]{3,2,1,0:T(8,128)(2,1)S(1)}, u32[]{:S(2)}, u32[]{:S(2)}) collective-permute-start(bf16[3,4,8,768]{3,2,1,0:T(8,128)(2,1)S(1)} %get-tuple-element.46), channel_id=1, source_target_pairs={{0,2},{1,3},{2,0},{3,1},{4,6},{5,7},{6,4},{7,5},{8,10},{9,11},{10,... | collective-permute-start | bytes 442376 | tf_op jit(solution)/shard_map/ppermute | solution.py:370
  6.9 3.1 %collective-permute-start.2 = (bf16[3,4,8,768]{3,2,1,0:T(8,128)(2,1)S(1)}, bf16[3,4,8,768]{3,2,1,0:T(8,128)(2,1)S(1)}, u32[]{:S(2)}, u32[]{:S(2)}) collective-permute-start(bf16[3,4,8,768]{3,2,1,0:T(8,128)(2,1)S(1)} %get-tuple-element.50), channel_id=1, source_target_pairs={{0,4},{1,5},{2,6},{3,7},{4,0},{5,1},{6,2},{7,3},{8,12},{9,13},{10,... | collective-permute-start | bytes 442376 | tf_op jit(solution)/shard_map/ppermute | solution.py:370
  9.9 0.0 collective-permute-start.3
  10.0 1.9 %shard_map.93 = (bf16[4,4,8,768]{3,2,1,0:T(8,128)(2,1)S(1)}, bf16[4,4,8,768]{3,2,1,0:T(8,128)(2,1)S(1)}) custom-call(s32[8,32]{1,0:T(8,128)S(1)} %bitcast.56, s32[1,32]{1,0:T(1,128)S(1)} %copy-done.2, bf16[2048,768]{1,0:T(8,128)(2,1)S(1)} %copy-done.3, bf16[768,768]{1,0:T(8,128)(2,1)S(1)} %copy-done), custom_call_target="tpu_custom_call" | custom-call | tf_op jit(solution)/shard_map/pallas_call | solution.py:250
  11.9 0.0 collective-permute-done.1.refs_1_
  11.9 0.1 collective-permute-start.7
  12.0 0.2 convert_reduce_fusion
  12.2 0.6 reduce_max.18
  12.9 0.7 %reduce_max.19 = s32[]{:T(128)} reduce(s32[8]{0:T(128)S(1)} %get-tuple-element.97, s32[]{:T(128)} %constant.67.clone.1), dimensions={0}, to_apply=%region_3.4 | reduce | flops 7 | bytes 40 | tf_op jit(solution)/shard_map/reduce_max | solution.py:377
  14.9 0.0 collective-permute-done.2.refs_2_
  15.0 1.8 %collective-permute-done.3.refs_3_ = bf16[3,4,8,768]{3,2,1,0:T(8,128)(2,1)S(1)} collective-permute-done((bf16[3,4,8,768]{3,2,1,0:T(8,128)(2,1)S(1)}, bf16[3,4,8,768]{3,2,1,0:T(8,128)(2,1)S(1)}, u32[]{:S(2)}, u32[]{:S(2)}) %collective-permute-start.3) | collective-permute-done | bytes 147488 | tf_op jit(solution)/shard_map/ppermute | solution.py:370
  16.8 1.1 %shard_map.94 = (bf16[5,8,768]{2,1,0:T(8,128)(2,1)S(1)}, bf16[5,8,768]{2,1,0:T(8,128)(2,1)S(1)}, bf16[5,8,768]{2,1,0:T(8,128)(2,1)S(1)}, bf16[5,8,768]{2,1,0:T(8,128)(2,1)S(1)}) custom-call(s32[8]{0:T(128)S(1)} %copy-done.4, bf16[3,4,8,768]{3,2,1,0:T(8,128)(2,1)S(1)} %get-tuple-element.45.refs_0_, bf16[3,4,8,768]{3,2,1,0:T(8,128)(2,1)S(1)} %collective-permute-done.1.refs_1_, ...), custom_call_target="tpu_custom_call" | custom-call | tf_op jit(solution)/shard_map/pallas_call | solution.py:141
  17.9 0.0 collective-permute-done.7
  17.9 1.8 %collective-permute-start.8 = (bf16[2,2,4,8,768]{4,3,0,2,1:T(8,128)(2,1)S(1)}, bf16[2,2,4,8,768]{4,3,0,2,1:T(8,128)(2,1)S(1)}, u32[]{:S(2)}, u32[]{:S(2)}) collective-permute-start(bf16[2,2,4,8,768]{4,3,0,2,1:T(8,128)(2,1)S(1)} %fusion.1), channel_id=1, source_target_pairs={{0,4},{1,5},{2,6},{3,7},{4,0},{5,1},{6,2},{7,3},{8,12},{9,13},{10,... | collective-permute-start | bytes 589832 | tf_op jit(solution)/shard_map/ppermute | solution.py:370
  19.7 1.2 %collective-permute-start.4 = (bf16[5,8,768]{2,1,0:T(8,128)(2,1)S(1)}, bf16[5,8,768]{2,1,0:T(8,128)(2,1)S(1)}, u32[]{:S(2)}, u32[]{:S(2)}) collective-permute-start(bf16[5,8,768]{2,1,0:T(8,128)(2,1)S(1)} %get-tuple-element.54), channel_id=1, source_target_pairs={{0,8},{1,9},{2,10},{3,11},{4,12},{5,13},{6,14},{7,15},{8,0},{9,1},... | collective-permute-start | bytes 184328 | tf_op jit(solution)/shard_map/ppermute | solution.py:370
  20.9 2.6 %collective-permute-start.5 = (bf16[5,8,768]{2,1,0:T(8,128)(2,1)S(1)}, bf16[5,8,768]{2,1,0:T(8,128)(2,1)S(1)}, u32[]{:S(2)}, u32[]{:S(2)}) collective-permute-start(bf16[5,8,768]{2,1,0:T(8,128)(2,1)S(1)} %get-tuple-element.55), channel_id=1, source_target_pairs={{0,16},{1,17},{2,18},{3,19},{4,20},{5,21},{6,22},{7,23},{8,24},{9,... | collective-permute-start | bytes 184328 | tf_op jit(solution)/shard_map/ppermute | solution.py:370
  23.5 0.6 collective-permute-start.6
  24.1 5.5 %collective-permute-done.6.refs_3_ = bf16[5,8,768]{2,1,0:T(8,128)(2,1)S(1)} collective-permute-done((bf16[5,8,768]{2,1,0:T(8,128)(2,1)S(1)}, bf16[5,8,768]{2,1,0:T(8,128)(2,1)S(1)}, u32[]{:S(2)}, u32[]{:S(2)}) %collective-permute-start.6) | collective-permute-done | bytes 61472 | tf_op jit(solution)/shard_map/ppermute | solution.py:370
  29.6 0.0 collective-permute-done.8
  29.6 0.0 collective-permute-done.4.refs_1_
  29.6 0.0 collective-permute-done.5.refs_2_
  29.7 0.0 copy-start.5
  29.7 0.0 copy-start.6
  29.7 0.9 %shard_map.95 = bf16[8,8,768]{2,1,0:T(8,128)(2,1)S(1)} custom-call(s32[8]{0:T(128)S(1)} %copy-done.4, s32[1]{0:T(128)} %bitcast.1.full, bf16[5,8,768]{2,1,0:T(8,128)(2,1)S(1)} %get-tuple-element.53.refs_0_, bf16[5,8,768]{2,1,0:T(8,128)(2,1)S(1)} %collective-permute-done.4.refs_1_, bf16[5,8,768]{2,1,0:T(8,128)(2,1)S(1)} %collective-permute-done.5.refs_2_, ...), custom_call_target="tpu_custom_call" | custom-call | tf_op jit(solution)/shard_map/pallas_call | solution.py:168
  30.6 0.7 %collective-permute-start.11 = (bf16[8,8,768]{2,1,0:T(8,128)(2,1)S(1)}, bf16[8,8,768]{2,1,0:T(8,128)(2,1)S(1)}, u32[]{:S(2)}, u32[]{:S(2)}) collective-permute-start(bf16[8,8,768]{2,1,0:T(8,128)(2,1)S(1)} %shard_map.95), channel_id=1, source_target_pairs={{0,24},{1,25},{2,26},{3,27},{4,28},{5,29},{6,30},{7,31},{8,16},{9,... | collective-permute-start | bytes 294920 | tf_op jit(solution)/shard_map/ppermute | solution.py:370
  31.3 0.0 collective-permute-start.10
  31.3 3.7 %collective-permute-start.9 = (bf16[8,8,768]{2,1,0:T(8,128)(2,1)S(1)}, bf16[8,8,768]{2,1,0:T(8,128)(2,1)S(1)}, u32[]{:S(2)}, u32[]{:S(2)}) collective-permute-start(bf16[8,8,768]{2,1,0:T(8,128)(2,1)S(1)} %shard_map.95), channel_id=1, source_target_pairs={{0,8},{1,9},{2,10},{3,11},{4,12},{5,13},{6,14},{7,15},{8,0},{9,1},... | collective-permute-start | bytes 294920 | tf_op jit(solution)/shard_map/ppermute | solution.py:370
  35.1 1.6 %collective-permute-start.12 = (bf16[2,2,4,8,768]{4,3,1,2,0:T(8,128)(2,1)S(1)}, bf16[2,2,4,8,768]{4,3,1,2,0:T(8,128)(2,1)S(1)}, u32[]{:S(2)}, u32[]{:S(2)}) collective-permute-start(bf16[2,2,4,8,768]{4,3,1,2,0:T(8,128)(2,1)S(1)} %pad_maximum_fusion.1), channel_id=1, source_target_pairs={{0,2},{1,3},{2,0},{3,1},{4,6},{5,7},{6,4},{7,5},{8,10},{9,11},{10,... | collective-permute-start | bytes 589832 | tf_op jit(solution)/shard_map/ppermute | solution.py:370
  36.7 0.6 collective-permute-done.11
  37.3 2.4 %collective-permute-done.10 = bf16[8,8,768]{2,1,0:T(8,128)(2,1)S(1)} collective-permute-done((bf16[8,8,768]{2,1,0:T(8,128)(2,1)S(1)}, bf16[8,8,768]{2,1,0:T(8,128)(2,1)S(1)}, u32[]{:S(2)}, u32[]{:S(2)}) %collective-permute-start.10) | collective-permute-done | bytes 98336 | tf_op jit(solution)/shard_map/ppermute | solution.py:370
  39.7 0.0 collective-permute-done.9
  39.8 1.1 %collective-permute-done.12 = bf16[2,2,4,8,768]{4,3,1,2,0:T(8,128)(2,1)S(1)} collective-permute-done((bf16[2,2,4,8,768]{4,3,1,2,0:T(8,128)(2,1)S(1)}, bf16[2,2,4,8,768]{4,3,1,2,0:T(8,128)(2,1)S(1)}, u32[]{:S(2)}, u32[]{:S(2)}) %collective-permute-start.12) | collective-permute-done | bytes 196640 | tf_op jit(solution)/shard_map/ppermute | solution.py:370
  40.9 0.2 collective-permute-start.16
  41.1 1.6 %collective-permute-start.14 = (bf16[8,32,768]{2,1,0:T(8,128)(2,1)S(1)}, bf16[8,32,768]{2,1,0:T(8,128)(2,1)S(1)}, u32[]{:S(2)}, u32[]{:S(2)}) collective-permute-start(bf16[8,32,768]{2,1,0:T(8,128)(2,1)S(1)} %pad_maximum_fusion.refs_0_), channel_id=1, source_target_pairs={{0,2},{1,3},{2,0},{3,1},{4,6},{5,7},{6,4},{7,5},{8,10},{9,11},{10,... | collective-permute-start | bytes 1179656 | tf_op jit(solution)/shard_map/ppermute | solution.py:370
  42.7 1.2 %collective-permute-start.22 = (bf16[4,2,8,768]{3,2,1,0:T(8,128)(2,1)S(1)}, bf16[4,2,8,768]{3,2,1,0:T(8,128)(2,1)S(1)}, u32[]{:S(2)}, u32[]{:S(2)}) collective-permute-start(bf16[4,2,8,768]{3,2,1,0:T(8,128)(2,1)S(1)} %pad_maximum_fusion.4), channel_id=1, source_target_pairs={{0,8},{1,9},{2,10},{3,11},{4,12},{5,13},{6,14},{7,15},{8,0},{9,1},... | collective-permute-start | bytes 294920 | tf_op jit(solution)/shard_map/ppermute | solution.py:370
  44.0 0.2 collective-permute-start.23
  44.2 3.2 %collective-permute-start.24 = (bf16[4,2,8,768]{3,2,1,0:T(8,128)(2,1)S(1)}, bf16[4,2,8,768]{3,2,1,0:T(8,128)(2,1)S(1)}, u32[]{:S(2)}, u32[]{:S(2)}) collective-permute-start(bf16[4,2,8,768]{3,2,1,0:T(8,128)(2,1)S(1)} %pad_maximum_fusion.6), channel_id=1, source_target_pairs={{0,24},{1,25},{2,26},{3,27},{4,28},{5,29},{6,30},{7,31},{8,16},{9,... | collective-permute-start | bytes 294920 | tf_op jit(solution)/shard_map/ppermute | solution.py:370
  47.4 2.6 %collective-permute-done.16.refs_4_ = bf16[8,32,768]{2,1,0:T(8,128)(2,1)S(1)} collective-permute-done((bf16[8,32,768]{2,1,0:T(8,128)(2,1)S(1)}, bf16[8,32,768]{2,1,0:T(8,128)(2,1)S(1)}, u32[]{:S(2)}, u32[]{:S(2)}) %collective-permute-start.16) | collective-permute-done | bytes 393248 | tf_op jit(solution)/shard_map/ppermute | solution.py:370
  50.0 0.3 collective-permute-start.18
  50.3 0.0 collective-permute-done.14.refs_2_
  50.3 3.0 %collective-permute-start.20 = (bf16[8,32,384]{2,1,0:T(8,128)(2,1)S(1)}, bf16[8,32,384]{2,1,0:T(8,128)(2,1)S(1)}, u32[]{:S(2)}, u32[]{:S(2)}) collective-permute-start(bf16[8,32,384]{2,1,0:T(8,128)(2,1)S(1)} %slice.107), channel_id=1, source_target_pairs={{0,4},{1,5},{2,6},{3,7},{4,0},{5,1},{6,2},{7,3},{8,12},{9,13},{10,... | collective-permute-start | bytes 589832 | tf_op jit(solution)/shard_map/ppermute | solution.py:370
  53.3 0.0 collective-permute-done.22.refs_11_
  53.3 0.0 collective-permute-start.13
  53.3 0.0 collective-permute-done.23.refs_12_
  53.3 0.5 collective-permute-start.17
  53.8 0.0 collective-permute-done.24.refs_13_
  53.8 0.1 collective-permute-start.15
  53.9 0.1 copy.12
  54.0 0.1 reshape.15
  54.1 1.7 %collective-permute-done.18.refs_6_ = bf16[8,32,384]{2,1,0:T(8,128)(2,1)S(1)} collective-permute-done((bf16[8,32,384]{2,1,0:T(8,128)(2,1)S(1)}, bf16[8,32,384]{2,1,0:T(8,128)(2,1)S(1)}, u32[]{:S(2)}, u32[]{:S(2)}) %collective-permute-start.18) | collective-permute-done | bytes 196640 | tf_op jit(solution)/shard_map/ppermute | solution.py:370
  55.8 0.0 collective-permute-start.19
  55.8 1.2 %collective-permute-done.20.refs_8_ = bf16[8,32,384]{2,1,0:T(8,128)(2,1)S(1)} collective-permute-done((bf16[8,32,384]{2,1,0:T(8,128)(2,1)S(1)}, bf16[8,32,384]{2,1,0:T(8,128)(2,1)S(1)}, u32[]{:S(2)}, u32[]{:S(2)}) %collective-permute-start.20) | collective-permute-done | bytes 196640 | tf_op jit(solution)/shard_map/ppermute | solution.py:370
  57.0 0.0 collective-permute-start.21
  57.0 0.1 pad_add_fusion.meta
  57.1 0.0 collective-permute-done.13.refs_1_
  57.1 0.0 collective-permute-done.17.refs_5_
  57.1 0.0 collective-permute-done.15.refs_3_
  57.1 0.1 collective-permute-done.19.refs_7_
  57.2 1.2 %collective-permute-done.21.refs_9_ = bf16[8,32,384]{2,1,0:T(8,128)(2,1)S(1)} collective-permute-done((bf16[8,32,384]{2,1,0:T(8,128)(2,1)S(1)}, bf16[8,32,384]{2,1,0:T(8,128)(2,1)S(1)}, u32[]{:S(2)}, u32[]{:S(2)}) %collective-permute-start.21) | collective-permute-done | bytes 196640 | tf_op jit(solution)/shard_map/ppermute | solution.py:370
  58.4 8.1 %shard_map.96 = bf16[2048,768]{1,0:T(8,128)(2,1)} custom-call(s32[40]{0:T(128)S(1)} %pad_add_fusion.meta, bf16[8,32,768]{2,1,0:T(8,128)(2,1)S(1)} %pad_maximum_fusion.refs_0_, bf16[8,32,768]{2,1,0:T(8,128)(2,1)S(1)} %collective-permute-done.13.refs_1_, bf16[8,32,768]{2,1,0:T(8,128)(2,1)S(1)} %collective-permute-done.14.refs_2_, ...), custom_call_target="tpu_custom_call" | custom-call | flops 4026531840 | bytes 8388608 | tf_op jit(solution)/shard_map/pallas_call | solution.py:322
  (34 shorter events, 0.4 us)
Async XLA Ops:
  0.0 4.5 %copy-start.4 = (s32[8]{0:T(128)S(1)}, s32[8]{0:T(128)}, u32[]{:S(2)}) copy-start(s32[8]{0:T(128)} %ids.7) | copy-start | bytes 100
  0.0 9.9 %copy-start.3 = (bf16[2048,768]{1,0:T(8,128)(2,1)S(1)}, bf16[2048,768]{1,0:T(8,128)(2,1)}, u32[]{:S(2)}) copy-start(bf16[2048,768]{1,0:T(8,128)(2,1)} %features) | copy-start | bytes 9437188
  0.0 10.0 %copy-start = (bf16[768,768]{1,0:T(8,128)(2,1)S(1)}, bf16[768,768]{1,0:T(8,128)(2,1)}, u32[]{:S(2)}) copy-start(bf16[768,768]{1,0:T(8,128)(2,1)} %refs_5_.1) | copy-start | bytes 3538948
  0.0 10.0 %copy-start.2 = (s32[1,32]{1,0:T(1,128)S(1)}, s32[1,32]{1,0:T(1,128)}, u32[]{:S(2)}) copy-start(s32[1,32]{1,0:T(1,128)} %counts.1) | copy-start | bytes 388
  0.0 10.0 %copy-start.1 = (s32[1,32,8]{1,2,0:T(8,128)S(1)}, s32[1,32,8]{1,2,0:T(8,128)}, u32[]{:S(2)}) copy-start(s32[1,32,8]{1,2,0:T(8,128)} %param.16) | copy-start | bytes 3076
  2.4 2.1 %collective-permute-start = (bf16[4,3,4,8,768]{4,3,2,1,0:T(8,128)(2,1)S(1)}, bf16[4,3,4,8,768]{4,3,2,1,0:T(8,128)(2,1)S(1)}, u32[]{:S(2)}, u32[]{:S(2)}) collective-permute-start(bf16[4,3,4,8,768]{4,3,2,1,0:T(8,128)(2,1)S(1)} %get-tuple-element.44), channel_id=1, source_target_pairs={{0,1},{1,0},{2,3},{3,2},{4,5},{5,4},{6,7},{7,6},{8,9},{9,8},{10,11... | collective-permute-start | bytes 1769480 | tf_op jit(solution)/shard_map/ppermute | solution.py:370
  5.2 6.7 %collective-permute-start.1 = (bf16[3,4,8,768]{3,2,1,0:T(8,128)(2,1)S(1)}, bf16[3,4,8,768]{3,2,1,0:T(8,128)(2,1)S(1)}, u32[]{:S(2)}, u32[]{:S(2)}) collective-permute-start(bf16[3,4,8,768]{3,2,1,0:T(8,128)(2,1)S(1)} %get-tuple-element.46), channel_id=1, source_target_pairs={{0,2},{1,3},{2,0},{3,1},{4,6},{5,7},{6,4},{7,5},{8,10},{9,11},{10,... | collective-permute-start | bytes 442376 | tf_op jit(solution)/shard_map/ppermute | solution.py:370
  6.9 8.1 %collective-permute-start.2 = (bf16[3,4,8,768]{3,2,1,0:T(8,128)(2,1)S(1)}, bf16[3,4,8,768]{3,2,1,0:T(8,128)(2,1)S(1)}, u32[]{:S(2)}, u32[]{:S(2)}) collective-permute-start(bf16[3,4,8,768]{3,2,1,0:T(8,128)(2,1)S(1)} %get-tuple-element.50), channel_id=1, source_target_pairs={{0,4},{1,5},{2,6},{3,7},{4,0},{5,1},{6,2},{7,3},{8,12},{9,13},{10,... | collective-permute-start | bytes 442376 | tf_op jit(solution)/shard_map/ppermute | solution.py:370
  9.9 6.8 %collective-permute-start.3 = (bf16[3,4,8,768]{3,2,1,0:T(8,128)(2,1)S(1)}, bf16[3,4,8,768]{3,2,1,0:T(8,128)(2,1)S(1)}, u32[]{:S(2)}, u32[]{:S(2)}) collective-permute-start(bf16[3,4,8,768]{3,2,1,0:T(8,128)(2,1)S(1)} %get-tuple-element.52), channel_id=1, source_target_pairs={{0,6},{1,7},{2,4},{3,5},{4,2},{5,3},{6,0},{7,1},{8,14},{9,15},{10,... | collective-permute-start | bytes 442376 | tf_op jit(solution)/shard_map/ppermute | solution.py:370
  11.9 5.9 %collective-permute-start.7 = (bf16[4,4,8,768]{3,2,1,0:T(8,128)(2,1)S(1)}, bf16[4,4,8,768]{3,2,1,0:T(8,128)(2,1)S(1)}, u32[]{:S(2)}, u32[]{:S(2)}) collective-permute-start(bf16[4,4,8,768]{3,2,1,0:T(8,128)(2,1)S(1)} %get-tuple-element.58), channel_id=1, source_target_pairs={{0,1},{1,0},{2,3},{3,2},{4,5},{5,4},{6,7},{7,6},{8,9},{9,8},{10,11... | collective-permute-start | bytes 589832 | tf_op jit(solution)/shard_map/ppermute | solution.py:370
  17.9 11.7 %collective-permute-start.8 = (bf16[2,2,4,8,768]{4,3,0,2,1:T(8,128)(2,1)S(1)}, bf16[2,2,4,8,768]{4,3,0,2,1:T(8,128)(2,1)S(1)}, u32[]{:S(2)}, u32[]{:S(2)}) collective-permute-start(bf16[2,2,4,8,768]{4,3,0,2,1:T(8,128)(2,1)S(1)} %fusion.1), channel_id=1, source_target_pairs={{0,4},{1,5},{2,6},{3,7},{4,0},{5,1},{6,2},{7,3},{8,12},{9,13},{10,... | collective-permute-start | bytes 589832 | tf_op jit(solution)/shard_map/ppermute | solution.py:370
  19.7 9.9 %collective-permute-start.4 = (bf16[5,8,768]{2,1,0:T(8,128)(2,1)S(1)}, bf16[5,8,768]{2,1,0:T(8,128)(2,1)S(1)}, u32[]{:S(2)}, u32[]{:S(2)}) collective-permute-start(bf16[5,8,768]{2,1,0:T(8,128)(2,1)S(1)} %get-tuple-element.54), channel_id=1, source_target_pairs={{0,8},{1,9},{2,10},{3,11},{4,12},{5,13},{6,14},{7,15},{8,0},{9,1},... | collective-permute-start | bytes 184328 | tf_op jit(solution)/shard_map/ppermute | solution.py:370
  20.9 8.8 %collective-permute-start.5 = (bf16[5,8,768]{2,1,0:T(8,128)(2,1)S(1)}, bf16[5,8,768]{2,1,0:T(8,128)(2,1)S(1)}, u32[]{:S(2)}, u32[]{:S(2)}) collective-permute-start(bf16[5,8,768]{2,1,0:T(8,128)(2,1)S(1)} %get-tuple-element.55), channel_id=1, source_target_pairs={{0,16},{1,17},{2,18},{3,19},{4,20},{5,21},{6,22},{7,23},{8,24},{9,... | collective-permute-start | bytes 184328 | tf_op jit(solution)/shard_map/ppermute | solution.py:370
  23.5 6.1 %collective-permute-start.6 = (bf16[5,8,768]{2,1,0:T(8,128)(2,1)S(1)}, bf16[5,8,768]{2,1,0:T(8,128)(2,1)S(1)}, u32[]{:S(2)}, u32[]{:S(2)}) collective-permute-start(bf16[5,8,768]{2,1,0:T(8,128)(2,1)S(1)} %get-tuple-element.56), channel_id=1, source_target_pairs={{0,24},{1,25},{2,26},{3,27},{4,28},{5,29},{6,30},{7,31},{8,16},{9,... | collective-permute-start | bytes 184328 | tf_op jit(solution)/shard_map/ppermute | solution.py:370
  29.7 24.2 %copy-start.5 = (f32[768]{0:T(1024)S(1)}, f32[768]{0:T(1024)}, u32[]{:S(2)}) copy-start(f32[768]{0:T(1024)} %param.19) | copy-start | bytes 9220
  29.7 24.2 %copy-start.6 = (s32[8,4]{0,1:T(4,128)S(1)}, s32[8,4]{0,1:T(4,128)}, u32[]{:S(2)}) copy-start(s32[8,4]{0,1:T(4,128)} %param.13) | copy-start | bytes 388
  30.6 6.6 %collective-permute-start.11 = (bf16[8,8,768]{2,1,0:T(8,128)(2,1)S(1)}, bf16[8,8,768]{2,1,0:T(8,128)(2,1)S(1)}, u32[]{:S(2)}, u32[]{:S(2)}) collective-permute-start(bf16[8,8,768]{2,1,0:T(8,128)(2,1)S(1)} %shard_map.95), channel_id=1, source_target_pairs={{0,24},{1,25},{2,26},{3,27},{4,28},{5,29},{6,30},{7,31},{8,16},{9,... | collective-permute-start | bytes 294920 | tf_op jit(solution)/shard_map/ppermute | solution.py:370
  31.3 8.3 %collective-permute-start.10 = (bf16[8,8,768]{2,1,0:T(8,128)(2,1)S(1)}, bf16[8,8,768]{2,1,0:T(8,128)(2,1)S(1)}, u32[]{:S(2)}, u32[]{:S(2)}) collective-permute-start(bf16[8,8,768]{2,1,0:T(8,128)(2,1)S(1)} %shard_map.95), channel_id=1, source_target_pairs={{0,16},{1,17},{2,18},{3,19},{4,20},{5,21},{6,22},{7,23},{8,24},{9,... | collective-permute-start | bytes 294920 | tf_op jit(solution)/shard_map/ppermute | solution.py:370
  31.3 8.3 %collective-permute-start.9 = (bf16[8,8,768]{2,1,0:T(8,128)(2,1)S(1)}, bf16[8,8,768]{2,1,0:T(8,128)(2,1)S(1)}, u32[]{:S(2)}, u32[]{:S(2)}) collective-permute-start(bf16[8,8,768]{2,1,0:T(8,128)(2,1)S(1)} %shard_map.95), channel_id=1, source_target_pairs={{0,8},{1,9},{2,10},{3,11},{4,12},{5,13},{6,14},{7,15},{8,0},{9,1},... | collective-permute-start | bytes 294920 | tf_op jit(solution)/shard_map/ppermute | solution.py:370
  35.1 5.7 %collective-permute-start.12 = (bf16[2,2,4,8,768]{4,3,1,2,0:T(8,128)(2,1)S(1)}, bf16[2,2,4,8,768]{4,3,1,2,0:T(8,128)(2,1)S(1)}, u32[]{:S(2)}, u32[]{:S(2)}) collective-permute-start(bf16[2,2,4,8,768]{4,3,1,2,0:T(8,128)(2,1)S(1)} %pad_maximum_fusion.1), channel_id=1, source_target_pairs={{0,2},{1,3},{2,0},{3,1},{4,6},{5,7},{6,4},{7,5},{8,10},{9,11},{10,... | collective-permute-start | bytes 589832 | tf_op jit(solution)/shard_map/ppermute | solution.py:370
  40.9 9.1 %collective-permute-start.16 = (bf16[8,32,768]{2,1,0:T(8,128)(2,1)S(1)}, bf16[8,32,768]{2,1,0:T(8,128)(2,1)S(1)}, u32[]{:S(2)}, u32[]{:S(2)}) collective-permute-start(bf16[8,32,768]{2,1,0:T(8,128)(2,1)S(1)} %pad_maximum_fusion.refs_0_), channel_id=1, source_target_pairs={{0,4},{1,5},{2,6},{3,7},{4,0},{5,1},{6,2},{7,3},{8,12},{9,13},{10,... | collective-permute-start | bytes 1179656 | tf_op jit(solution)/shard_map/ppermute | solution.py:370
  41.1 9.2 %collective-permute-start.14 = (bf16[8,32,768]{2,1,0:T(8,128)(2,1)S(1)}, bf16[8,32,768]{2,1,0:T(8,128)(2,1)S(1)}, u32[]{:S(2)}, u32[]{:S(2)}) collective-permute-start(bf16[8,32,768]{2,1,0:T(8,128)(2,1)S(1)} %pad_maximum_fusion.refs_0_), channel_id=1, source_target_pairs={{0,2},{1,3},{2,0},{3,1},{4,6},{5,7},{6,4},{7,5},{8,10},{9,11},{10,... | collective-permute-start | bytes 1179656 | tf_op jit(solution)/shard_map/ppermute | solution.py:370
  42.7 10.6 %collective-permute-start.22 = (bf16[4,2,8,768]{3,2,1,0:T(8,128)(2,1)S(1)}, bf16[4,2,8,768]{3,2,1,0:T(8,128)(2,1)S(1)}, u32[]{:S(2)}, u32[]{:S(2)}) collective-permute-start(bf16[4,2,8,768]{3,2,1,0:T(8,128)(2,1)S(1)} %pad_maximum_fusion.4), channel_id=1, source_target_pairs={{0,8},{1,9},{2,10},{3,11},{4,12},{5,13},{6,14},{7,15},{8,0},{9,1},... | collective-permute-start | bytes 294920 | tf_op jit(solution)/shard_map/ppermute | solution.py:370
  44.0 9.3 %collective-permute-start.23 = (bf16[4,2,8,768]{3,2,1,0:T(8,128)(2,1)S(1)}, bf16[4,2,8,768]{3,2,1,0:T(8,128)(2,1)S(1)}, u32[]{:S(2)}, u32[]{:S(2)}) collective-permute-start(bf16[4,2,8,768]{3,2,1,0:T(8,128)(2,1)S(1)} %pad_maximum_fusion.5), channel_id=1, source_target_pairs={{0,16},{1,17},{2,18},{3,19},{4,20},{5,21},{6,22},{7,23},{8,24},{9,... | collective-permute-start | bytes 294920 | tf_op jit(solution)/shard_map/ppermute | solution.py:370
  44.2 9.6 %collective-permute-start.24 = (bf16[4,2,8,768]{3,2,1,0:T(8,128)(2,1)S(1)}, bf16[4,2,8,768]{3,2,1,0:T(8,128)(2,1)S(1)}, u32[]{:S(2)}, u32[]{:S(2)}) collective-permute-start(bf16[4,2,8,768]{3,2,1,0:T(8,128)(2,1)S(1)} %pad_maximum_fusion.6), channel_id=1, source_target_pairs={{0,24},{1,25},{2,26},{3,27},{4,28},{5,29},{6,30},{7,31},{8,16},{9,... | collective-permute-start | bytes 294920 | tf_op jit(solution)/shard_map/ppermute | solution.py:370
  50.0 5.7 %collective-permute-start.18 = (bf16[8,32,384]{2,1,0:T(8,128)(2,1)S(1)}, bf16[8,32,384]{2,1,0:T(8,128)(2,1)S(1)}, u32[]{:S(2)}, u32[]{:S(2)}) collective-permute-start(bf16[8,32,384]{2,1,0:T(8,128)(2,1)S(1)} %slice.106), channel_id=1, source_target_pairs={{0,2},{1,3},{2,0},{3,1},{4,6},{5,7},{6,4},{7,5},{8,10},{9,11},{10,... | collective-permute-start | bytes 589832 | tf_op jit(solution)/shard_map/ppermute | solution.py:370
  50.3 6.6 %collective-permute-start.20 = (bf16[8,32,384]{2,1,0:T(8,128)(2,1)S(1)}, bf16[8,32,384]{2,1,0:T(8,128)(2,1)S(1)}, u32[]{:S(2)}, u32[]{:S(2)}) collective-permute-start(bf16[8,32,384]{2,1,0:T(8,128)(2,1)S(1)} %slice.107), channel_id=1, source_target_pairs={{0,4},{1,5},{2,6},{3,7},{4,0},{5,1},{6,2},{7,3},{8,12},{9,13},{10,... | collective-permute-start | bytes 589832 | tf_op jit(solution)/shard_map/ppermute | solution.py:370
  53.3 3.7 %collective-permute-start.13 = (bf16[8,32,768]{2,1,0:T(8,128)(2,1)S(1)}, bf16[8,32,768]{2,1,0:T(8,128)(2,1)S(1)}, u32[]{:S(2)}, u32[]{:S(2)}) collective-permute-start(bf16[8,32,768]{2,1,0:T(8,128)(2,1)S(1)} %pad_maximum_fusion.refs_0_), channel_id=1, source_target_pairs={{0,1},{1,0},{2,3},{3,2},{4,5},{5,4},{6,7},{7,6},{8,9},{9,8},{10,11... | collective-permute-start | bytes 1179656 | tf_op jit(solution)/shard_map/ppermute | solution.py:370
  53.3 3.7 %collective-permute-start.17 = (bf16[8,32,768]{2,1,0:T(8,128)(2,1)S(1)}, bf16[8,32,768]{2,1,0:T(8,128)(2,1)S(1)}, u32[]{:S(2)}, u32[]{:S(2)}) collective-permute-start(bf16[8,32,768]{2,1,0:T(8,128)(2,1)S(1)} %collective-permute-done.16.refs_4_), channel_id=1, source_target_pairs={{0,1},{1,0},{2,3},{3,2},{4,5},{5,4},{6,7},{7,6},{8,9},{9,8},{10,11... | collective-permute-start | bytes 1179656 | tf_op jit(solution)/shard_map/ppermute | solution.py:370
  53.8 3.2 %collective-permute-start.15 = (bf16[8,32,768]{2,1,0:T(8,128)(2,1)S(1)}, bf16[8,32,768]{2,1,0:T(8,128)(2,1)S(1)}, u32[]{:S(2)}, u32[]{:S(2)}) collective-permute-start(bf16[8,32,768]{2,1,0:T(8,128)(2,1)S(1)} %collective-permute-done.14.refs_2_), channel_id=1, source_target_pairs={{0,1},{1,0},{2,3},{3,2},{4,5},{5,4},{6,7},{7,6},{8,9},{9,8},{10,11... | collective-permute-start | bytes 1179656 | tf_op jit(solution)/shard_map/ppermute | solution.py:370
  55.8 1.4 %collective-permute-start.19 = (bf16[8,32,384]{2,1,0:T(8,128)(2,1)S(1)}, bf16[8,32,384]{2,1,0:T(8,128)(2,1)S(1)}, u32[]{:S(2)}, u32[]{:S(2)}) collective-permute-start(bf16[8,32,384]{2,1,0:T(8,128)(2,1)S(1)} %collective-permute-done.18.refs_6_), channel_id=1, source_target_pairs={{0,1},{1,0},{2,3},{3,2},{4,5},{5,4},{6,7},{7,6},{8,9},{9,8},{10,11... | collective-permute-start | bytes 589832 | tf_op jit(solution)/shard_map/ppermute | solution.py:370
  57.0 1.4 %collective-permute-start.21 = (bf16[8,32,384]{2,1,0:T(8,128)(2,1)S(1)}, bf16[8,32,384]{2,1,0:T(8,128)(2,1)S(1)}, u32[]{:S(2)}, u32[]{:S(2)}) collective-permute-start(bf16[8,32,384]{2,1,0:T(8,128)(2,1)S(1)} %collective-permute-done.20.refs_8_), channel_id=1, source_target_pairs={{0,1},{1,0},{2,3},{3,2},{4,5},{5,4},{6,7},{7,6},{8,9},{9,8},{10,11... | collective-permute-start | bytes 589832 | tf_op jit(solution)/shard_map/ppermute | solution.py:370

commit v7 on v5

--- a/solution.py
+++ b/solution.py
@@ -88,18 +88,16 @@
 
 def merge_kernel(count, ids, keep, got, *outs):
     me = lax.axis_index(AXES)
-    core, place = me % 2, me % PLANE // 2
-    (cores,) = scan(
-        ids, lambda i: i // (2 * count) == me // 2, [lambda i: i // count % 2]
-    )
+    place = me % PLANE // 2
+    (owner,) = scan(ids, lambda i: i // (2 * count) == me // 2, [lambda i: i // count + 1])
     for s in range(SLOTS):
 
-        @pl.when(cores[s] == core)
+        @pl.when(owner[s] == me + 1)
         def _():
             for m, out in enumerate(outs):
                 out[s] = keep[place ^ m, s]
 
-        @pl.when(cores[s] != core)
+        @pl.when((owner[s] > 0) & (owner[s] != me + 1))
         def _():
             for m, out in enumerate(outs):
                 out[s] = got[place ^ m, s]

time: 66.9 us -> 66.7 us (level)
  transfers between devices with their start and end apart: 25 -> 25, of which waited for: 10 -> 11; matrix products, arithmetic and copies ran while one was open for 3% -> 3% of each run, Pallas kernels for 5% -> 5%
where the time goes in v7:
time: 66.7 us; the launch traced here: 66.5 us
  starting transfers between devices  26.8 us (40%)
  waiting for transfers between devices  20.4 us (31%)
  Pallas kernels  15.5 us (23%)
  other arithmetic  1.84 us (3%)
  between operations  1.59 us (2%)
    ppermute x25, starting transfers between devices, swap(): return lax.ppermute(x, AXES, [(d, d ^ mask) for d in range(devices)])  26.8 us
    ppermute x25, waiting for transfers between devices, swap(): return lax.ppermute(x, AXES, [(d, d ^ mask) for d in range(devices)])  20.4 us
    pallas_call x1, Pallas kernels, layer(): pl.pallas_call(functools.partial(layer_kernel, group), out_shape=jax.Shap...  8.14 us
    pallas_call x1, Pallas kernels, halves(): pl.pallas_call(halves_kernel, out_shape=[shape, shape], in_specs=[SMEM, H...  2.6 us
    pallas_call x1, Pallas kernels, listed_rows(): pl.pallas_call(rows_kernel, out_shape=[shape, shape], in_specs=[VMEM] * 4...  1.94 us
    reduce_max x2, other arithmetic, load(): jnp.max(jnp.sum((at[:, None] == at[None, :]).astype(jnp.int32), axis=1))  1.34 us
  transfers between devices with their start and end apart: 25, of which 11 were waited for; matrix products, arithmetic and copies ran while one was open for 3% of the time, Pallas kernels for 5%

profile of v7, /device:TPU:0, one launch (start us, length us, event | category | flops | bytes accessed | tf_op | source)
XLA Modules:
  0.0 66.5 jit_solution(9517835553578177142)
XLA Ops:
  0.0 2.6 %shard_map.91 = (bf16[4,3,4,8,768]{4,3,2,1,0:T(8,128)(2,1)S(1)}, bf16[4,3,4,8,768]{4,3,2,1,0:T(8,128)(2,1)S(1)}) custom-call(s32[8]{0:T(128)} %ids.7, bf16[8,4,2,4,8,768]{5,4,3,2,1,0:T(8,128)(2,1)} %bitcast.57), custom_call_target="tpu_custom_call" | custom-call | tf_op jit(solution)/shard_map/pallas_call | solution.py:79
  2.6 0.1 collective-permute-start
  2.7 2.0 %collective-permute-done.got = bf16[4,3,4,8,768]{4,3,2,1,0:T(8,128)(2,1)S(1)} collective-permute-done((bf16[4,3,4,8,768]{4,3,2,1,0:T(8,128)(2,1)S(1)}, bf16[4,3,4,8,768]{4,3,2,1,0:T(8,128)(2,1)S(1)}, u32[]{:S(2)}, u32[]{:S(2)}) %collective-permute-start) | collective-permute-done | bytes 589856 | tf_op jit(solution)/shard_map/ppermute | solution.py:365
  4.7 0.7 %shard_map.92 = (bf16[3,4,8,768]{3,2,1,0:T(8,128)(2,1)S(1)}, bf16[3,4,8,768]{3,2,1,0:T(8,128)(2,1)S(1)}, bf16[3,4,8,768]{3,2,1,0:T(8,128)(2,1)S(1)}, bf16[3,4,8,768]{3,2,1,0:T(8,128)(2,1)S(1)}) custom-call(s32[8]{0:T(128)S(1)} %copy-done.4, bf16[4,3,4,8,768]{4,3,2,1,0:T(8,128)(2,1)S(1)} %get-tuple-element.43.keep, ...), custom_call_target="tpu_custom_call" | custom-call | tf_op jit(solution)/shard_map/pallas_call | solution.py:108
  5.4 2.8 %collective-permute-start.1 = (bf16[3,4,8,768]{3,2,1,0:T(8,128)(2,1)S(1)}, bf16[3,4,8,768]{3,2,1,0:T(8,128)(2,1)S(1)}, u32[]{:S(2)}, u32[]{:S(2)}) collective-permute-start(bf16[3,4,8,768]{3,2,1,0:T(8,128)(2,1)S(1)} %get-tuple-element.46), channel_id=1, source_target_pairs={{0,2},{1,3},{2,0},{3,1},{4,6},{5,7},{6,4},{7,5},{8,10},{9,11},{10,... | collective-permute-start | bytes 442376 | tf_op jit(solution)/shard_map/ppermute | solution.py:365
  8.2 0.1 collective-permute-start.2
  8.3 1.5 %collective-permute-start.3 = (bf16[3,4,8,768]{3,2,1,0:T(8,128)(2,1)S(1)}, bf16[3,4,8,768]{3,2,1,0:T(8,128)(2,1)S(1)}, u32[]{:S(2)}, u32[]{:S(2)}) collective-permute-start(bf16[3,4,8,768]{3,2,1,0:T(8,128)(2,1)S(1)} %get-tuple-element.52), channel_id=1, source_target_pairs={{0,6},{1,7},{2,4},{3,5},{4,2},{5,3},{6,0},{7,1},{8,14},{9,15},{10,... | collective-permute-start | bytes 442376 | tf_op jit(solution)/shard_map/ppermute | solution.py:365
  9.8 1.9 %shard_map.93 = (bf16[4,4,8,768]{3,2,1,0:T(8,128)(2,1)S(1)}, bf16[4,4,8,768]{3,2,1,0:T(8,128)(2,1)S(1)}) custom-call(s32[8,32]{1,0:T(8,128)S(1)} %bitcast.56, s32[1,32]{1,0:T(1,128)S(1)} %copy-done.2, bf16[2048,768]{1,0:T(8,128)(2,1)S(1)} %copy-done.3, bf16[768,768]{1,0:T(8,128)(2,1)S(1)} %copy-done), custom_call_target="tpu_custom_call" | custom-call | tf_op jit(solution)/shard_map/pallas_call | solution.py:245
  11.7 0.6 collective-permute-done.1.refs_1_
  12.4 0.0 collective-permute-start.7
  12.4 0.2 convert_reduce_fusion
  12.6 0.6 reduce_max.18
  13.3 0.7 %reduce_max.19 = s32[]{:T(128)} reduce(s32[8]{0:T(128)S(1)} %get-tuple-element.97, s32[]{:T(128)} %constant.67.clone.1), dimensions={0}, to_apply=%region_3.4 | reduce | flops 7 | bytes 40 | tf_op jit(solution)/shard_map/reduce_max | solution.py:372
  15.3 0.0 collective-permute-done.2.refs_2_
  15.3 1.5 %collective-permute-done.3.refs_3_ = bf16[3,4,8,768]{3,2,1,0:T(8,128)(2,1)S(1)} collective-permute-done((bf16[3,4,8,768]{3,2,1,0:T(8,128)(2,1)S(1)}, bf16[3,4,8,768]{3,2,1,0:T(8,128)(2,1)S(1)}, u32[]{:S(2)}, u32[]{:S(2)}) %collective-permute-start.3) | collective-permute-done | bytes 147488 | tf_op jit(solution)/shard_map/ppermute | solution.py:365
  16.8 1.2 %shard_map.94 = (bf16[5,8,768]{2,1,0:T(8,128)(2,1)S(1)}, bf16[5,8,768]{2,1,0:T(8,128)(2,1)S(1)}, bf16[5,8,768]{2,1,0:T(8,128)(2,1)S(1)}, bf16[5,8,768]{2,1,0:T(8,128)(2,1)S(1)}) custom-call(s32[8]{0:T(128)S(1)} %copy-done.4, bf16[3,4,8,768]{3,2,1,0:T(8,128)(2,1)S(1)} %get-tuple-element.45.refs_0_, bf16[3,4,8,768]{3,2,1,0:T(8,128)(2,1)S(1)} %collective-permute-done.1.refs_1_, ...), custom_call_target="tpu_custom_call" | custom-call | tf_op jit(solution)/shard_map/pallas_call | solution.py:136
  18.0 0.0 collective-permute-done.7
  18.1 0.4 collective-permute-start.8
  18.4 2.6 %collective-permute-start.4 = (bf16[5,8,768]{2,1,0:T(8,128)(2,1)S(1)}, bf16[5,8,768]{2,1,0:T(8,128)(2,1)S(1)}, u32[]{:S(2)}, u32[]{:S(2)}) collective-permute-start(bf16[5,8,768]{2,1,0:T(8,128)(2,1)S(1)} %get-tuple-element.54), channel_id=1, source_target_pairs={{0,8},{1,9},{2,10},{3,11},{4,12},{5,13},{6,14},{7,15},{8,0},{9,1},... | collective-permute-start | bytes 184328 | tf_op jit(solution)/shard_map/ppermute | solution.py:365
  21.0 2.4 %collective-permute-start.5 = (bf16[5,8,768]{2,1,0:T(8,128)(2,1)S(1)}, bf16[5,8,768]{2,1,0:T(8,128)(2,1)S(1)}, u32[]{:S(2)}, u32[]{:S(2)}) collective-permute-start(bf16[5,8,768]{2,1,0:T(8,128)(2,1)S(1)} %get-tuple-element.55), channel_id=1, source_target_pairs={{0,16},{1,17},{2,18},{3,19},{4,20},{5,21},{6,22},{7,23},{8,24},{9,... | collective-permute-start | bytes 184328 | tf_op jit(solution)/shard_map/ppermute | solution.py:365
  23.5 0.2 collective-permute-start.6
  23.7 5.8 %collective-permute-done.6.refs_3_ = bf16[5,8,768]{2,1,0:T(8,128)(2,1)S(1)} collective-permute-done((bf16[5,8,768]{2,1,0:T(8,128)(2,1)S(1)}, bf16[5,8,768]{2,1,0:T(8,128)(2,1)S(1)}, u32[]{:S(2)}, u32[]{:S(2)}) %collective-permute-start.6) | collective-permute-done | bytes 61472 | tf_op jit(solution)/shard_map/ppermute | solution.py:365
  29.5 0.0 collective-permute-done.8
  29.5 0.0 collective-permute-done.4.refs_1_
  29.5 0.0 collective-permute-done.5.refs_2_
  29.5 0.0 copy-start.5
  29.5 0.0 copy-start.6
  29.5 0.9 %shard_map.95 = bf16[8,8,768]{2,1,0:T(8,128)(2,1)S(1)} custom-call(s32[8]{0:T(128)S(1)} %copy-done.4, s32[1]{0:T(128)} %bitcast.1.full, bf16[5,8,768]{2,1,0:T(8,128)(2,1)S(1)} %get-tuple-element.53.refs_0_, bf16[5,8,768]{2,1,0:T(8,128)(2,1)S(1)} %collective-permute-done.4.refs_1_, bf16[5,8,768]{2,1,0:T(8,128)(2,1)S(1)} %collective-permute-done.5.refs_2_, ...), custom_call_target="tpu_custom_call" | custom-call | tf_op jit(solution)/shard_map/pallas_call | solution.py:163
  30.5 1.0 %collective-permute-start.11 = (bf16[8,8,768]{2,1,0:T(8,128)(2,1)S(1)}, bf16[8,8,768]{2,1,0:T(8,128)(2,1)S(1)}, u32[]{:S(2)}, u32[]{:S(2)}) collective-permute-start(bf16[8,8,768]{2,1,0:T(8,128)(2,1)S(1)} %shard_map.95), channel_id=1, source_target_pairs={{0,24},{1,25},{2,26},{3,27},{4,28},{5,29},{6,30},{7,31},{8,16},{9,... | collective-permute-start | bytes 294920 | tf_op jit(solution)/shard_map/ppermute | solution.py:365
  31.5 0.0 collective-permute-start.10
  31.5 3.4 %collective-permute-start.9 = (bf16[8,8,768]{2,1,0:T(8,128)(2,1)S(1)}, bf16[8,8,768]{2,1,0:T(8,128)(2,1)S(1)}, u32[]{:S(2)}, u32[]{:S(2)}) collective-permute-start(bf16[8,8,768]{2,1,0:T(8,128)(2,1)S(1)} %shard_map.95), channel_id=1, source_target_pairs={{0,8},{1,9},{2,10},{3,11},{4,12},{5,13},{6,14},{7,15},{8,0},{9,1},... | collective-permute-start | bytes 294920 | tf_op jit(solution)/shard_map/ppermute | solution.py:365
  35.0 1.7 %collective-permute-start.12 = (bf16[2,2,4,8,768]{4,3,1,2,0:T(8,128)(2,1)S(1)}, bf16[2,2,4,8,768]{4,3,1,2,0:T(8,128)(2,1)S(1)}, u32[]{:S(2)}, u32[]{:S(2)}) collective-permute-start(bf16[2,2,4,8,768]{4,3,1,2,0:T(8,128)(2,1)S(1)} %pad_maximum_fusion.1), channel_id=1, source_target_pairs={{0,2},{1,3},{2,0},{3,1},{4,6},{5,7},{6,4},{7,5},{8,10},{9,11},{10,... | collective-permute-start | bytes 589832 | tf_op jit(solution)/shard_map/ppermute | solution.py:365
  36.7 0.4 collective-permute-done.11
  37.1 2.7 %collective-permute-done.10 = bf16[8,8,768]{2,1,0:T(8,128)(2,1)S(1)} collective-permute-done((bf16[8,8,768]{2,1,0:T(8,128)(2,1)S(1)}, bf16[8,8,768]{2,1,0:T(8,128)(2,1)S(1)}, u32[]{:S(2)}, u32[]{:S(2)}) %collective-permute-start.10) | collective-permute-done | bytes 98336 | tf_op jit(solution)/shard_map/ppermute | solution.py:365
  39.9 0.0 collective-permute-done.9
  39.9 0.8 %collective-permute-done.12 = bf16[2,2,4,8,768]{4,3,1,2,0:T(8,128)(2,1)S(1)} collective-permute-done((bf16[2,2,4,8,768]{4,3,1,2,0:T(8,128)(2,1)S(1)}, bf16[2,2,4,8,768]{4,3,1,2,0:T(8,128)(2,1)S(1)}, u32[]{:S(2)}, u32[]{:S(2)}) %collective-permute-start.12) | collective-permute-done | bytes 196640 | tf_op jit(solution)/shard_map/ppermute | solution.py:365
  40.7 0.3 collective-permute-start.16
  41.1 1.7 %collective-permute-start.14 = (bf16[8,32,768]{2,1,0:T(8,128)(2,1)S(1)}, bf16[8,32,768]{2,1,0:T(8,128)(2,1)S(1)}, u32[]{:S(2)}, u32[]{:S(2)}) collective-permute-start(bf16[8,32,768]{2,1,0:T(8,128)(2,1)S(1)} %pad_maximum_fusion.refs_0_), channel_id=1, source_target_pairs={{0,2},{1,3},{2,0},{3,1},{4,6},{5,7},{6,4},{7,5},{8,10},{9,11},{10,... | collective-permute-start | bytes 1179656 | tf_op jit(solution)/shard_map/ppermute | solution.py:365
  42.8 0.1 collective-permute-start.22
  42.9 1.7 %collective-permute-start.23 = (bf16[4,2,8,768]{3,2,1,0:T(8,128)(2,1)S(1)}, bf16[4,2,8,768]{3,2,1,0:T(8,128)(2,1)S(1)}, u32[]{:S(2)}, u32[]{:S(2)}) collective-permute-start(bf16[4,2,8,768]{3,2,1,0:T(8,128)(2,1)S(1)} %pad_maximum_fusion.5), channel_id=1, source_target_pairs={{0,16},{1,17},{2,18},{3,19},{4,20},{5,21},{6,22},{7,23},{8,24},{9,... | collective-permute-start | bytes 294920 | tf_op jit(solution)/shard_map/ppermute | solution.py:365
  44.6 2.8 %collective-permute-start.24 = (bf16[4,2,8,768]{3,2,1,0:T(8,128)(2,1)S(1)}, bf16[4,2,8,768]{3,2,1,0:T(8,128)(2,1)S(1)}, u32[]{:S(2)}, u32[]{:S(2)}) collective-permute-start(bf16[4,2,8,768]{3,2,1,0:T(8,128)(2,1)S(1)} %pad_maximum_fusion.6), channel_id=1, source_target_pairs={{0,24},{1,25},{2,26},{3,27},{4,28},{5,29},{6,30},{7,31},{8,16},{9,... | collective-permute-start | bytes 294920 | tf_op jit(solution)/shard_map/ppermute | solution.py:365
  47.4 2.4 %collective-permute-done.16.refs_4_ = bf16[8,32,768]{2,1,0:T(8,128)(2,1)S(1)} collective-permute-done((bf16[8,32,768]{2,1,0:T(8,128)(2,1)S(1)}, bf16[8,32,768]{2,1,0:T(8,128)(2,1)S(1)}, u32[]{:S(2)}, u32[]{:S(2)}) %collective-permute-start.16) | collective-permute-done | bytes 393248 | tf_op jit(solution)/shard_map/ppermute | solution.py:365
  49.9 0.5 collective-permute-start.18
  50.3 0.0 collective-permute-done.14.refs_2_
  50.4 2.9 %collective-permute-start.20 = (bf16[8,32,384]{2,1,0:T(8,128)(2,1)S(1)}, bf16[8,32,384]{2,1,0:T(8,128)(2,1)S(1)}, u32[]{:S(2)}, u32[]{:S(2)}) collective-permute-start(bf16[8,32,384]{2,1,0:T(8,128)(2,1)S(1)} %slice.107), channel_id=1, source_target_pairs={{0,4},{1,5},{2,6},{3,7},{4,0},{5,1},{6,2},{7,3},{8,12},{9,13},{10,... | collective-permute-start | bytes 589832 | tf_op jit(solution)/shard_map/ppermute | solution.py:365
  53.3 0.0 collective-permute-done.22.refs_11_
  53.3 0.0 collective-permute-start.13
  53.3 0.0 collective-permute-done.23.refs_12_
  53.3 0.5 collective-permute-start.17
  53.8 0.0 collective-permute-done.24.refs_13_
  53.8 0.1 collective-permute-start.15
  53.9 0.1 copy.12
  54.0 0.1 reshape.15
  54.0 1.6 %collective-permute-done.18.refs_6_ = bf16[8,32,384]{2,1,0:T(8,128)(2,1)S(1)} collective-permute-done((bf16[8,32,384]{2,1,0:T(8,128)(2,1)S(1)}, bf16[8,32,384]{2,1,0:T(8,128)(2,1)S(1)}, u32[]{:S(2)}, u32[]{:S(2)}) %collective-permute-start.18) | collective-permute-done | bytes 196640 | tf_op jit(solution)/shard_map/ppermute | solution.py:365
  55.6 0.0 collective-permute-start.19
  55.6 1.3 %collective-permute-done.20.refs_8_ = bf16[8,32,384]{2,1,0:T(8,128)(2,1)S(1)} collective-permute-done((bf16[8,32,384]{2,1,0:T(8,128)(2,1)S(1)}, bf16[8,32,384]{2,1,0:T(8,128)(2,1)S(1)}, u32[]{:S(2)}, u32[]{:S(2)}) %collective-permute-start.20) | collective-permute-done | bytes 196640 | tf_op jit(solution)/shard_map/ppermute | solution.py:365
  56.9 0.0 collective-permute-start.21
  56.9 0.1 pad_add_fusion.meta
  57.0 0.0 collective-permute-done.13.refs_1_
  57.0 0.0 collective-permute-done.17.refs_5_
  57.0 0.0 collective-permute-done.15.refs_3_
  57.0 0.0 collective-permute-done.19.refs_7_
  57.1 1.3 %collective-permute-done.21.refs_9_ = bf16[8,32,384]{2,1,0:T(8,128)(2,1)S(1)} collective-permute-done((bf16[8,32,384]{2,1,0:T(8,128)(2,1)S(1)}, bf16[8,32,384]{2,1,0:T(8,128)(2,1)S(1)}, u32[]{:S(2)}, u32[]{:S(2)}) %collective-permute-start.21) | collective-permute-done | bytes 196640 | tf_op jit(solution)/shard_map/ppermute | solution.py:365
  58.4 8.1 %shard_map.96 = bf16[2048,768]{1,0:T(8,128)(2,1)} custom-call(s32[40]{0:T(128)S(1)} %pad_add_fusion.meta, bf16[8,32,768]{2,1,0:T(8,128)(2,1)S(1)} %pad_maximum_fusion.refs_0_, bf16[8,32,768]{2,1,0:T(8,128)(2,1)S(1)} %collective-permute-done.13.refs_1_, bf16[8,32,768]{2,1,0:T(8,128)(2,1)S(1)} %collective-permute-done.14.refs_2_, ...), custom_call_target="tpu_custom_call" | custom-call | flops 4026531840 | bytes 8388608 | tf_op jit(solution)/shard_map/pallas_call | solution.py:317
  (34 shorter events, 0.4 us)
Async XLA Ops:
  0.0 4.7 %copy-start.4 = (s32[8]{0:T(128)S(1)}, s32[8]{0:T(128)}, u32[]{:S(2)}) copy-start(s32[8]{0:T(128)} %ids.7) | copy-start | bytes 100
  0.0 9.8 %copy-start.3 = (bf16[2048,768]{1,0:T(8,128)(2,1)S(1)}, bf16[2048,768]{1,0:T(8,128)(2,1)}, u32[]{:S(2)}) copy-start(bf16[2048,768]{1,0:T(8,128)(2,1)} %features) | copy-start | bytes 9437188
  0.0 9.8 %copy-start = (bf16[768,768]{1,0:T(8,128)(2,1)S(1)}, bf16[768,768]{1,0:T(8,128)(2,1)}, u32[]{:S(2)}) copy-start(bf16[768,768]{1,0:T(8,128)(2,1)} %refs_5_.1) | copy-start | bytes 3538948
  0.0 9.8 %copy-start.2 = (s32[1,32]{1,0:T(1,128)S(1)}, s32[1,32]{1,0:T(1,128)}, u32[]{:S(2)}) copy-start(s32[1,32]{1,0:T(1,128)} %counts.1) | copy-start | bytes 388
  0.0 9.8 %copy-start.1 = (s32[1,32,8]{1,2,0:T(8,128)S(1)}, s32[1,32,8]{1,2,0:T(8,128)}, u32[]{:S(2)}) copy-start(s32[1,32,8]{1,2,0:T(8,128)} %param.16) | copy-start | bytes 3076
  2.6 2.1 %collective-permute-start = (bf16[4,3,4,8,768]{4,3,2,1,0:T(8,128)(2,1)S(1)}, bf16[4,3,4,8,768]{4,3,2,1,0:T(8,128)(2,1)S(1)}, u32[]{:S(2)}, u32[]{:S(2)}) collective-permute-start(bf16[4,3,4,8,768]{4,3,2,1,0:T(8,128)(2,1)S(1)} %get-tuple-element.44), channel_id=1, source_target_pairs={{0,1},{1,0},{2,3},{3,2},{4,5},{5,4},{6,7},{7,6},{8,9},{9,8},{10,11... | collective-permute-start | bytes 1769480 | tf_op jit(solution)/shard_map/ppermute | solution.py:365
  5.4 7.0 %collective-permute-start.1 = (bf16[3,4,8,768]{3,2,1,0:T(8,128)(2,1)S(1)}, bf16[3,4,8,768]{3,2,1,0:T(8,128)(2,1)S(1)}, u32[]{:S(2)}, u32[]{:S(2)}) collective-permute-start(bf16[3,4,8,768]{3,2,1,0:T(8,128)(2,1)S(1)} %get-tuple-element.46), channel_id=1, source_target_pairs={{0,2},{1,3},{2,0},{3,1},{4,6},{5,7},{6,4},{7,5},{8,10},{9,11},{10,... | collective-permute-start | bytes 442376 | tf_op jit(solution)/shard_map/ppermute | solution.py:365
  8.2 7.1 %collective-permute-start.2 = (bf16[3,4,8,768]{3,2,1,0:T(8,128)(2,1)S(1)}, bf16[3,4,8,768]{3,2,1,0:T(8,128)(2,1)S(1)}, u32[]{:S(2)}, u32[]{:S(2)}) collective-permute-start(bf16[3,4,8,768]{3,2,1,0:T(8,128)(2,1)S(1)} %get-tuple-element.50), channel_id=1, source_target_pairs={{0,4},{1,5},{2,6},{3,7},{4,0},{5,1},{6,2},{7,3},{8,12},{9,13},{10,... | collective-permute-start | bytes 442376 | tf_op jit(solution)/shard_map/ppermute | solution.py:365
  8.3 8.5 %collective-permute-start.3 = (bf16[3,4,8,768]{3,2,1,0:T(8,128)(2,1)S(1)}, bf16[3,4,8,768]{3,2,1,0:T(8,128)(2,1)S(1)}, u32[]{:S(2)}, u32[]{:S(2)}) collective-permute-start(bf16[3,4,8,768]{3,2,1,0:T(8,128)(2,1)S(1)} %get-tuple-element.52), channel_id=1, source_target_pairs={{0,6},{1,7},{2,4},{3,5},{4,2},{5,3},{6,0},{7,1},{8,14},{9,15},{10,... | collective-permute-start | bytes 442376 | tf_op jit(solution)/shard_map/ppermute | solution.py:365
  12.4 5.6 %collective-permute-start.7 = (bf16[4,4,8,768]{3,2,1,0:T(8,128)(2,1)S(1)}, bf16[4,4,8,768]{3,2,1,0:T(8,128)(2,1)S(1)}, u32[]{:S(2)}, u32[]{:S(2)}) collective-permute-start(bf16[4,4,8,768]{3,2,1,0:T(8,128)(2,1)S(1)} %get-tuple-element.58), channel_id=1, source_target_pairs={{0,1},{1,0},{2,3},{3,2},{4,5},{5,4},{6,7},{7,6},{8,9},{9,8},{10,11... | collective-permute-start | bytes 589832 | tf_op jit(solution)/shard_map/ppermute | solution.py:365
  18.1 11.4 %collective-permute-start.8 = (bf16[2,2,4,8,768]{4,3,0,2,1:T(8,128)(2,1)S(1)}, bf16[2,2,4,8,768]{4,3,0,2,1:T(8,128)(2,1)S(1)}, u32[]{:S(2)}, u32[]{:S(2)}) collective-permute-start(bf16[2,2,4,8,768]{4,3,0,2,1:T(8,128)(2,1)S(1)} %fusion.1), channel_id=1, source_target_pairs={{0,4},{1,5},{2,6},{3,7},{4,0},{5,1},{6,2},{7,3},{8,12},{9,13},{10,... | collective-permute-start | bytes 589832 | tf_op jit(solution)/shard_map/ppermute | solution.py:365
  18.4 11.1 %collective-permute-start.4 = (bf16[5,8,768]{2,1,0:T(8,128)(2,1)S(1)}, bf16[5,8,768]{2,1,0:T(8,128)(2,1)S(1)}, u32[]{:S(2)}, u32[]{:S(2)}) collective-permute-start(bf16[5,8,768]{2,1,0:T(8,128)(2,1)S(1)} %get-tuple-element.54), channel_id=1, source_target_pairs={{0,8},{1,9},{2,10},{3,11},{4,12},{5,13},{6,14},{7,15},{8,0},{9,1},... | collective-permute-start | bytes 184328 | tf_op jit(solution)/shard_map/ppermute | solution.py:365
  21.0 8.5 %collective-permute-start.5 = (bf16[5,8,768]{2,1,0:T(8,128)(2,1)S(1)}, bf16[5,8,768]{2,1,0:T(8,128)(2,1)S(1)}, u32[]{:S(2)}, u32[]{:S(2)}) collective-permute-start(bf16[5,8,768]{2,1,0:T(8,128)(2,1)S(1)} %get-tuple-element.55), channel_id=1, source_target_pairs={{0,16},{1,17},{2,18},{3,19},{4,20},{5,21},{6,22},{7,23},{8,24},{9,... | collective-permute-start | bytes 184328 | tf_op jit(solution)/shard_map/ppermute | solution.py:365
  23.5 6.0 %collective-permute-start.6 = (bf16[5,8,768]{2,1,0:T(8,128)(2,1)S(1)}, bf16[5,8,768]{2,1,0:T(8,128)(2,1)S(1)}, u32[]{:S(2)}, u32[]{:S(2)}) collective-permute-start(bf16[5,8,768]{2,1,0:T(8,128)(2,1)S(1)} %get-tuple-element.56), channel_id=1, source_target_pairs={{0,24},{1,25},{2,26},{3,27},{4,28},{5,29},{6,30},{7,31},{8,16},{9,... | collective-permute-start | bytes 184328 | tf_op jit(solution)/shard_map/ppermute | solution.py:365
  29.5 24.4 %copy-start.5 = (f32[768]{0:T(1024)S(1)}, f32[768]{0:T(1024)}, u32[]{:S(2)}) copy-start(f32[768]{0:T(1024)} %param.19) | copy-start | bytes 9220
  29.5 24.3 %copy-start.6 = (s32[8,4]{0,1:T(4,128)S(1)}, s32[8,4]{0,1:T(4,128)}, u32[]{:S(2)}) copy-start(s32[8,4]{0,1:T(4,128)} %param.13) | copy-start | bytes 388
  30.5 6.6 %collective-permute-start.11 = (bf16[8,8,768]{2,1,0:T(8,128)(2,1)S(1)}, bf16[8,8,768]{2,1,0:T(8,128)(2,1)S(1)}, u32[]{:S(2)}, u32[]{:S(2)}) collective-permute-start(bf16[8,8,768]{2,1,0:T(8,128)(2,1)S(1)} %shard_map.95), channel_id=1, source_target_pairs={{0,24},{1,25},{2,26},{3,27},{4,28},{5,29},{6,30},{7,31},{8,16},{9,... | collective-permute-start | bytes 294920 | tf_op jit(solution)/shard_map/ppermute | solution.py:365
  31.5 8.3 %collective-permute-start.10 = (bf16[8,8,768]{2,1,0:T(8,128)(2,1)S(1)}, bf16[8,8,768]{2,1,0:T(8,128)(2,1)S(1)}, u32[]{:S(2)}, u32[]{:S(2)}) collective-permute-start(bf16[8,8,768]{2,1,0:T(8,128)(2,1)S(1)} %shard_map.95), channel_id=1, source_target_pairs={{0,16},{1,17},{2,18},{3,19},{4,20},{5,21},{6,22},{7,23},{8,24},{9,... | collective-permute-start | bytes 294920 | tf_op jit(solution)/shard_map/ppermute | solution.py:365
  31.5 8.3 %collective-permute-start.9 = (bf16[8,8,768]{2,1,0:T(8,128)(2,1)S(1)}, bf16[8,8,768]{2,1,0:T(8,128)(2,1)S(1)}, u32[]{:S(2)}, u32[]{:S(2)}) collective-permute-start(bf16[8,8,768]{2,1,0:T(8,128)(2,1)S(1)} %shard_map.95), channel_id=1, source_target_pairs={{0,8},{1,9},{2,10},{3,11},{4,12},{5,13},{6,14},{7,15},{8,0},{9,1},... | collective-permute-start | bytes 294920 | tf_op jit(solution)/shard_map/ppermute | solution.py:365
  35.0 5.7 %collective-permute-start.12 = (bf16[2,2,4,8,768]{4,3,1,2,0:T(8,128)(2,1)S(1)}, bf16[2,2,4,8,768]{4,3,1,2,0:T(8,128)(2,1)S(1)}, u32[]{:S(2)}, u32[]{:S(2)}) collective-permute-start(bf16[2,2,4,8,768]{4,3,1,2,0:T(8,128)(2,1)S(1)} %pad_maximum_fusion.1), channel_id=1, source_target_pairs={{0,2},{1,3},{2,0},{3,1},{4,6},{5,7},{6,4},{7,5},{8,10},{9,11},{10,... | collective-permute-start | bytes 589832 | tf_op jit(solution)/shard_map/ppermute | solution.py:365
  40.7 9.1 %collective-permute-start.16 = (bf16[8,32,768]{2,1,0:T(8,128)(2,1)S(1)}, bf16[8,32,768]{2,1,0:T(8,128)(2,1)S(1)}, u32[]{:S(2)}, u32[]{:S(2)}) collective-permute-start(bf16[8,32,768]{2,1,0:T(8,128)(2,1)S(1)} %pad_maximum_fusion.refs_0_), channel_id=1, source_target_pairs={{0,4},{1,5},{2,6},{3,7},{4,0},{5,1},{6,2},{7,3},{8,12},{9,13},{10,... | collective-permute-start | bytes 1179656 | tf_op jit(solution)/shard_map/ppermute | solution.py:365
  41.1 9.3 %collective-permute-start.14 = (bf16[8,32,768]{2,1,0:T(8,128)(2,1)S(1)}, bf16[8,32,768]{2,1,0:T(8,128)(2,1)S(1)}, u32[]{:S(2)}, u32[]{:S(2)}) collective-permute-start(bf16[8,32,768]{2,1,0:T(8,128)(2,1)S(1)} %pad_maximum_fusion.refs_0_), channel_id=1, source_target_pairs={{0,2},{1,3},{2,0},{3,1},{4,6},{5,7},{6,4},{7,5},{8,10},{9,11},{10,... | collective-permute-start | bytes 1179656 | tf_op jit(solution)/shard_map/ppermute | solution.py:365
  42.8 10.5 %collective-permute-start.22 = (bf16[4,2,8,768]{3,2,1,0:T(8,128)(2,1)S(1)}, bf16[4,2,8,768]{3,2,1,0:T(8,128)(2,1)S(1)}, u32[]{:S(2)}, u32[]{:S(2)}) collective-permute-start(bf16[4,2,8,768]{3,2,1,0:T(8,128)(2,1)S(1)} %pad_maximum_fusion.4), channel_id=1, source_target_pairs={{0,8},{1,9},{2,10},{3,11},{4,12},{5,13},{6,14},{7,15},{8,0},{9,1},... | collective-permute-start | bytes 294920 | tf_op jit(solution)/shard_map/ppermute | solution.py:365
  42.9 10.4 %collective-permute-start.23 = (bf16[4,2,8,768]{3,2,1,0:T(8,128)(2,1)S(1)}, bf16[4,2,8,768]{3,2,1,0:T(8,128)(2,1)S(1)}, u32[]{:S(2)}, u32[]{:S(2)}) collective-permute-start(bf16[4,2,8,768]{3,2,1,0:T(8,128)(2,1)S(1)} %pad_maximum_fusion.5), channel_id=1, source_target_pairs={{0,16},{1,17},{2,18},{3,19},{4,20},{5,21},{6,22},{7,23},{8,24},{9,... | collective-permute-start | bytes 294920 | tf_op jit(solution)/shard_map/ppermute | solution.py:365
  44.6 9.2 %collective-permute-start.24 = (bf16[4,2,8,768]{3,2,1,0:T(8,128)(2,1)S(1)}, bf16[4,2,8,768]{3,2,1,0:T(8,128)(2,1)S(1)}, u32[]{:S(2)}, u32[]{:S(2)}) collective-permute-start(bf16[4,2,8,768]{3,2,1,0:T(8,128)(2,1)S(1)} %pad_maximum_fusion.6), channel_id=1, source_target_pairs={{0,24},{1,25},{2,26},{3,27},{4,28},{5,29},{6,30},{7,31},{8,16},{9,... | collective-permute-start | bytes 294920 | tf_op jit(solution)/shard_map/ppermute | solution.py:365
  49.9 5.7 %collective-permute-start.18 = (bf16[8,32,384]{2,1,0:T(8,128)(2,1)S(1)}, bf16[8,32,384]{2,1,0:T(8,128)(2,1)S(1)}, u32[]{:S(2)}, u32[]{:S(2)}) collective-permute-start(bf16[8,32,384]{2,1,0:T(8,128)(2,1)S(1)} %slice.106), channel_id=1, source_target_pairs={{0,2},{1,3},{2,0},{3,1},{4,6},{5,7},{6,4},{7,5},{8,10},{9,11},{10,... | collective-permute-start | bytes 589832 | tf_op jit(solution)/shard_map/ppermute | solution.py:365
  50.4 6.6 %collective-permute-start.20 = (bf16[8,32,384]{2,1,0:T(8,128)(2,1)S(1)}, bf16[8,32,384]{2,1,0:T(8,128)(2,1)S(1)}, u32[]{:S(2)}, u32[]{:S(2)}) collective-permute-start(bf16[8,32,384]{2,1,0:T(8,128)(2,1)S(1)} %slice.107), channel_id=1, source_target_pairs={{0,4},{1,5},{2,6},{3,7},{4,0},{5,1},{6,2},{7,3},{8,12},{9,13},{10,... | collective-permute-start | bytes 589832 | tf_op jit(solution)/shard_map/ppermute | solution.py:365
  53.3 3.7 %collective-permute-start.13 = (bf16[8,32,768]{2,1,0:T(8,128)(2,1)S(1)}, bf16[8,32,768]{2,1,0:T(8,128)(2,1)S(1)}, u32[]{:S(2)}, u32[]{:S(2)}) collective-permute-start(bf16[8,32,768]{2,1,0:T(8,128)(2,1)S(1)} %pad_maximum_fusion.refs_0_), channel_id=1, source_target_pairs={{0,1},{1,0},{2,3},{3,2},{4,5},{5,4},{6,7},{7,6},{8,9},{9,8},{10,11... | collective-permute-start | bytes 1179656 | tf_op jit(solution)/shard_map/ppermute | solution.py:365
  53.3 3.7 %collective-permute-start.17 = (bf16[8,32,768]{2,1,0:T(8,128)(2,1)S(1)}, bf16[8,32,768]{2,1,0:T(8,128)(2,1)S(1)}, u32[]{:S(2)}, u32[]{:S(2)}) collective-permute-start(bf16[8,32,768]{2,1,0:T(8,128)(2,1)S(1)} %collective-permute-done.16.refs_4_), channel_id=1, source_target_pairs={{0,1},{1,0},{2,3},{3,2},{4,5},{5,4},{6,7},{7,6},{8,9},{9,8},{10,11... | collective-permute-start | bytes 1179656 | tf_op jit(solution)/shard_map/ppermute | solution.py:365
  53.8 3.2 %collective-permute-start.15 = (bf16[8,32,768]{2,1,0:T(8,128)(2,1)S(1)}, bf16[8,32,768]{2,1,0:T(8,128)(2,1)S(1)}, u32[]{:S(2)}, u32[]{:S(2)}) collective-permute-start(bf16[8,32,768]{2,1,0:T(8,128)(2,1)S(1)} %collective-permute-done.14.refs_2_), channel_id=1, source_target_pairs={{0,1},{1,0},{2,3},{3,2},{4,5},{5,4},{6,7},{7,6},{8,9},{9,8},{10,11... | collective-permute-start | bytes 1179656 | tf_op jit(solution)/shard_map/ppermute | solution.py:365
  55.6 1.4 %collective-permute-start.19 = (bf16[8,32,384]{2,1,0:T(8,128)(2,1)S(1)}, bf16[8,32,384]{2,1,0:T(8,128)(2,1)S(1)}, u32[]{:S(2)}, u32[]{:S(2)}) collective-permute-start(bf16[8,32,384]{2,1,0:T(8,128)(2,1)S(1)} %collective-permute-done.18.refs_6_), channel_id=1, source_target_pairs={{0,1},{1,0},{2,3},{3,2},{4,5},{5,4},{6,7},{7,6},{8,9},{9,8},{10,11... | collective-permute-start | bytes 589832 | tf_op jit(solution)/shard_map/ppermute | solution.py:365
  56.9 1.4 %collective-permute-start.21 = (bf16[8,32,384]{2,1,0:T(8,128)(2,1)S(1)}, bf16[8,32,384]{2,1,0:T(8,128)(2,1)S(1)}, u32[]{:S(2)}, u32[]{:S(2)}) collective-permute-start(bf16[8,32,384]{2,1,0:T(8,128)(2,1)S(1)} %collective-permute-done.20.refs_8_), channel_id=1, source_target_pairs={{0,1},{1,0},{2,3},{3,2},{4,5},{5,4},{6,7},{7,6},{8,9},{9,8},{10,11... | collective-permute-start | bytes 589832 | tf_op jit(solution)/shard_map/ppermute | solution.py:365
